TPU v7x, 32 devices: a whole 2x2x4 slice. The times are simulated.
32 devices in a mesh: dp: 16 (over z, y, x), section: 2 (over core).
Axes of the slice: x: 2, y: 2, z: 4, core: 2. Of those that a mesh axis runs over, the one named last changes fastest.
Arguments:
- activations: bfloat16 [2, 16, 4, 48, 4224], P('section', 'dp'), may hold values from -6 to 6
- key_grads: bfloat16 [2, 16, 4, 48, 640], P('section', 'dp'), may hold values from -6 to 6
- top_grad: bfloat16 [16, 4, 48, 4224], P('dp'), may hold values from -6 to 6
- norm_gains: float32 [2, 4224], P('section'), may hold values from 0.1 to 1.9
- w_key: bfloat16 [2, 4224, 640], P('section', 'dp'), may hold values from -0.09375 to 0.09375
- lengths: int32 [16, 4], P('dp'), may hold values from 1 to 48
Outputs:
- section_grads: bfloat16 [2, 16, 4, 48, 4224], P('section', 'dp')
- gain_grad: float32 [2, 4224], P('section', 'dp')
All inputs are finite; a program needn't handle non-finite values.
Results may differ from a plain program's by a relative error of at most 0.0035.
Values may be sent and summed in bfloat16 or wider, within the bound.
No kernel may reach another device: no remote copies, remote signals or barrier semaphores. Data moves between devices by JAX's collectives and lax.ppermute only.
A program may use at most 64 MiB of HBM per device.

v0:
```python
import functools
import math

import jax
import jax.numpy as jnp
from jax import lax
from jax.experimental import pallas as pl
from jax.experimental.pallas import tpu as pltpu
from jax.sharding import PartitionSpec as P

norm_epsilon = 1e-05
mebibyte = 1024 * 1024
product_cost = 10


def grant(*arrays):
    total = 4 * mebibyte
    for array in arrays:
        lanes = -(-array.shape[-1] // 128) * 128
        total += math.prod(array.shape[:-1]) * lanes * jnp.dtype(array.dtype).itemsize
    return -(-total // mebibyte) * mebibyte


def plane_size(replicas):
    size = 1
    while (2 * size) ** 2 <= replicas and replicas % (2 * size) == 0:
        size *= 2
    return size


def ahead(place, step, count):
    if count & (count - 1) == 0:
        return place ^ step
    return (place + step) % count


def behind(place, step, count):
    if count & (count - 1) == 0:
        return place ^ step
    return (place + count - step) % count


def along_line(value, step, line, plane):
    pairs = [
        (z * plane + q, ahead(z, step, line) * plane + q)
        for z in range(line)
        for q in range(plane)
    ]
    return lax.ppermute(value, "dp", pairs)


def along_plane(value, step, line, plane, back=False):
    partner = behind if back else ahead
    pairs = [
        (z * plane + q, z * plane + partner(q, step, plane))
        for z in range(line)
        for q in range(plane)
    ]
    return lax.ppermute(value, "dp", pairs)


def product_kernel(token_count, weight_count, fold, *refs):
    tokens = refs[:token_count]
    weights = refs[token_count : token_count + weight_count]
    outs = refs[token_count + weight_count :]
    for token_ref, out_ref in zip(tokens, outs):
        for index, weight_ref in enumerate(weights):
            product = lax.dot_general(
                token_ref[...],
                weight_ref[...],
                (((1,), (1,)), ((), ())),
                preferred_element_type=jnp.float32,
            ).astype(out_ref.dtype)
            width = product.shape[1]
            for part in range(product.shape[0] // fold):
                out_ref[index, :, part * width : (part + 1) * width] = product[part * fold : (part + 1) * fold, :]


def products(fold, tokens, weights, cost):
    rows, depth = tokens[0].shape
    width = weights[0].shape[0]
    count = len(weights)
    folded = (count, fold, rows // fold * width)
    outs = [jax.ShapeDtypeStruct(folded, jnp.bfloat16) for _ in tokens]
    return pl.pallas_call(
        functools.partial(product_kernel, len(tokens), count, fold),
        out_shape=outs,
        in_specs=[pl.BlockSpec(memory_space=pltpu.VMEM)] * (len(tokens) + count),
        out_specs=[pl.BlockSpec(memory_space=pltpu.VMEM)] * len(tokens),
        compiler_params=pltpu.CompilerParams(vmem_limit_bytes=grant(*tokens, *weights, *outs)),
        cost_estimate=pl.CostEstimate(
            flops=cost * 2 * rows * depth * width * count * len(tokens),
            bytes_accessed=2 * (rows * depth * len(tokens) + depth * width * count + rows * width * count * len(tokens)),
            transcendentals=0,
        ),
        name="token_products",
    )(*tokens, *weights)


def column_tile(features, most=512):
    tile = 128
    for width in range(128, most + 1, 128):
        if features % width == 0:
            tile = width
    return tile


def inverse_kernel(seq_rows, chunk, tile, lengths_ref, act_ref, inverse_ref):
    rows, features = act_ref.shape

    def one_chunk(index, _):
        start = pl.multiple_of(index * chunk, chunk)
        part = pl.ds(start, chunk)
        squares = jnp.zeros((chunk, 128), jnp.float32)
        for left in range(0, features, tile):
            wide = act_ref[part, left : left + tile].astype(jnp.float32)
            wide = wide * wide
            for lane in range(0, tile, 128):
                squares = squares + wide[:, lane : lane + 128]
        mean = jnp.sum(squares, axis=1, keepdims=True) / features
        position = lax.broadcasted_iota(jnp.int32, (chunk, 1), 0) + lax.rem(start, seq_rows)
        keep = position < lengths_ref[lax.div(start, seq_rows)]
        inverse = jnp.where(keep, lax.rsqrt(mean + norm_epsilon), 0.0)
        inverse_ref[part, :] = jnp.broadcast_to(inverse, (chunk, 128))
        return 0

    lax.fori_loop(0, rows // chunk, one_chunk, 0)


def live_inverse(seq_rows, lengths, act):
    rows, features = act.shape
    return pl.pallas_call(
        functools.partial(inverse_kernel, seq_rows, math.gcd(seq_rows, 16), column_tile(features)),
        out_shape=jax.ShapeDtypeStruct((rows, 128), jnp.float32),
        in_specs=[pl.BlockSpec(memory_space=pltpu.SMEM), pl.BlockSpec(memory_space=pltpu.VMEM)],
        out_specs=pl.BlockSpec(memory_space=pltpu.VMEM),
        compiler_params=pltpu.CompilerParams(vmem_limit_bytes=grant(act)),
        cost_estimate=pl.CostEstimate(
            flops=2 * rows * features, bytes_accessed=2 * rows * features, transcendentals=rows
        ),
        name="live_inverse",
    )(lengths, act)


def relative(owner, place, count):
    if count & (count - 1) == 0:
        return owner ^ place
    return (place + count - owner) % count


def place_pieces(line, plane, groups, fold, pieces, held, back):
    width = back.shape[1] // (line * plane)
    me = lax.axis_index("dp")
    z, q = lax.div(me, plane), lax.rem(me, plane)
    for step in range(plane):
        owner_q = ahead(q, step, plane)
        for group_index, group in enumerate(groups):
            piece = pieces[step * len(groups) + group_index]
            for index, line_step in enumerate(group):
                held[behind(z, line_step, line) * plane + owner_q] = piece[index]
    steps = [line_step for group in groups for line_step in group]
    for owner_z in range(line):
        line_step = relative(owner_z, z, line)
        here = functools.reduce(jnp.logical_or, [line_step == step for step in steps])

        @pl.when(here)
        def _():
            for part in range(back.shape[0] // fold):
                rows = slice(part * fold, (part + 1) * fold)
                for block in range(owner_z * plane, (owner_z + 1) * plane):
                    back[rows, block * width : (block + 1) * width] = held[
                        block, :, part * width : (part + 1) * width
                    ]


def add_sums(lefts, part, project, inverse_ref, act_ref, gain_ref, gain_sum, pulls):
    inverse = inverse_ref[part, :]
    pull = pulls[part, :]
    for left in lefts:
        cols = slice(left, left + 128)
        both = act_ref[part, cols].astype(jnp.float32) * project(part, cols)
        pull = pull + both * gain_ref[:, cols]
        both = both * inverse
        folded = both[:8, :]
        for row in range(8, both.shape[0], 8):
            folded = folded + both[row : row + 8, :]
        gain_sum[:, cols] += folded
    pulls[part, :] = pull


def early_kernel(line, plane, groups, fold, chunk, inverse_ref, act_ref, gain_ref, *refs):
    pieces = refs[:-4]
    back, pulls, gain_sum, held = refs[-4:]
    back[...] = jnp.zeros_like(back)
    place_pieces(line, plane, groups, fold, pieces, held, back)
    gain_sum[...] = jnp.zeros_like(gain_sum)
    pulls[...] = jnp.zeros_like(pulls)

    def project(part, cols):
        return back[part, cols].astype(jnp.float32)

    def one_chunk(index, _):
        part = pl.ds(pl.multiple_of(index * chunk, chunk), chunk)
        add_sums(range(0, back.shape[1], 128), part, project, inverse_ref, act_ref, gain_ref, gain_sum, pulls)
        return 0

    lax.fori_loop(0, back.shape[0] // chunk, one_chunk, 0)


def placed_early(line, plane, groups, fold, inverse, act, gain, pieces):
    rows, features = act.shape
    vmem = pl.BlockSpec(memory_space=pltpu.VMEM)
    outs = [
        jax.ShapeDtypeStruct((rows, features), jnp.bfloat16),
        jax.ShapeDtypeStruct((rows, 128), jnp.float32),
        jax.ShapeDtypeStruct((8, features), jnp.float32),
    ]
    scratch = [pltpu.VMEM((line * plane,) + pieces[0].shape[1:], jnp.bfloat16)]
    return pl.pallas_call(
        functools.partial(early_kernel, line, plane, groups, fold, math.gcd(rows, 32)),
        out_shape=outs,
        in_specs=[vmem] * (3 + len(pieces)),
        out_specs=[vmem] * len(outs),
        scratch_shapes=scratch,
        compiler_params=pltpu.CompilerParams(
            vmem_limit_bytes=grant(inverse, act, gain, *pieces, *outs, *scratch)
        ),
        cost_estimate=pl.CostEstimate(
            flops=8 * rows * features, bytes_accessed=8 * rows * features, transcendentals=0
        ),
        name="placed_early",
    )(inverse, act, gain, *pieces)


def finish_kernel(
    line, plane, groups, fold, chunk, early_ref, early_pulls, early_gains, inverse_ref, act_ref, top_ref, gain_ref, *refs
):
    pieces = refs[:-10]
    passed_ref, local_ref, gain_out, held, back, gain_sum, pulls, passing, gain_blocks, copied = refs[-10:]
    rows, features = back.shape
    width = features // (line * plane)
    late_steps = [step for group in groups for step in group]
    late_z = behind(lax.div(lax.axis_index("dp"), plane), late_steps[0], line)
    back[...] = early_ref[...]
    place_pieces(line, plane, groups, fold, pieces, held, back)
    gain_sum[...] = early_gains[...]
    pulls[...] = early_pulls[...]

    def project(part, cols):
        return back[part, cols].astype(jnp.float32) - early_ref[part, cols].astype(jnp.float32)

    def add_late(part, lefts):
        add_sums(lefts, part, project, inverse_ref, act_ref, gain_ref, gain_sum, pulls)

    def out_copy(index):
        part = pl.ds(pl.multiple_of(index * chunk, chunk), chunk)
        return pltpu.make_async_copy(passing.at[part], passed_ref.at[part], copied.at[index])

    def one_chunk(index, _):
        part = pl.ds(pl.multiple_of(index * chunk, chunk), chunk)
        if len(late_steps) > 1:
            add_late(part, range(0, features, 128))
        else:
            for owner_z in range(line):
                first = owner_z * plane * width // 128 * 128
                after = (owner_z + 1) * plane * width

                @pl.when(late_z == owner_z)
                def _():
                    add_late(part, range(first, after, 128))

        inverse = inverse_ref[part, :]
        pull = jnp.sum(pulls[part, :], axis=1, keepdims=True) / features
        pull = jnp.broadcast_to(pull, inverse.shape) * inverse * inverse * inverse
        for left in range(0, features, 128):
            cols = slice(left, left + 128)
            scaled = back[part, cols].astype(jnp.float32) * gain_ref[:, cols]
            local = inverse * scaled - act_ref[part, cols].astype(jnp.float32) * pull
            local_ref[part, cols] = local
            passing[part, cols] = (top_ref[part, cols].astype(jnp.float32) + local).astype(jnp.bfloat16)
        out_copy(index).start()
        return 0

    lax.fori_loop(0, rows // chunk, one_chunk, 0)
    total = jnp.sum(gain_sum[...], axis=0, keepdims=True)
    for block in range(line * plane):
        gain_blocks[block] = total[:, block * width : (block + 1) * width]
    gain_copy = pltpu.make_async_copy(gain_blocks, gain_out, copied.at[rows // chunk])
    gain_copy.start()
    for index in range(rows // chunk):
        out_copy(index).wait()
    gain_copy.wait()


def finish(line, plane, groups, fold, early, inverse, act, top, gain, pieces):
    rows, features = act.shape
    blocks = line * plane
    vmem = pl.BlockSpec(memory_space=pltpu.VMEM)
    outs = [
        jax.ShapeDtypeStruct((rows, features), jnp.bfloat16),
        jax.ShapeDtypeStruct((rows, features), jnp.float32),
        jax.ShapeDtypeStruct((blocks, 1, features // blocks), jnp.float32),
    ]
    scratch = [
        pltpu.VMEM((blocks,) + pieces[0].shape[1:], jnp.bfloat16),
        pltpu.VMEM((rows, features), jnp.bfloat16),
        pltpu.VMEM((8, features), jnp.float32),
        pltpu.VMEM((rows, 128), jnp.float32),
        pltpu.VMEM((rows, features), jnp.bfloat16),
        pltpu.VMEM(outs[2].shape, jnp.float32),
    ]
    chunk = math.gcd(rows, 32)
    return pl.pallas_call(
        functools.partial(finish_kernel, line, plane, groups, fold, chunk),
        out_shape=outs,
        in_specs=[vmem] * (4 + len(early) + len(pieces)),
        out_specs=[pl.BlockSpec(memory_space=pl.ANY), vmem, pl.BlockSpec(memory_space=pl.ANY)],
        scratch_shapes=scratch + [pltpu.SemaphoreType.DMA((rows // chunk + 1,))],
        compiler_params=pltpu.CompilerParams(
            vmem_limit_bytes=grant(*early, act, top, *pieces, *outs, *scratch)
        ),
        cost_estimate=pl.CostEstimate(
            flops=16 * rows * features, bytes_accessed=12 * rows * features, transcendentals=0
        ),
        name="norm_backward",
    )(*early, inverse, act, top, gain, *pieces)


def hand_kernel(turn, chunk, incoming_ref, local_ref, result_ref, out_ref, loaded, staged, arrived, copied):
    rows, features = local_ref.shape
    parts = [pl.ds(start, chunk) for start in range(0, rows, chunk)]
    is_turn = lax.axis_index("section") == turn

    def through(source, staging, work):
        loads = [
            pltpu.make_async_copy(source.at[part], loaded.at[part], arrived.at[index])
            for index, part in enumerate(parts)
        ]
        stores = [
            pltpu.make_async_copy(staging.at[part], out_ref.at[part], copied.at[index])
            for index, part in enumerate(parts)
        ]
        for load in loads:
            load.start()
        for part, load, store in zip(parts, loads, stores):
            load.wait()
            work(part)
            store.start()
        for store in stores:
            store.wait()

    def add_local(part):
        for left in range(0, features, 128):
            cols = slice(left, left + 128)
            staged[part, cols] = (loaded[part, cols].astype(jnp.float32) + local_ref[part, cols]).astype(jnp.bfloat16)

    @pl.when(is_turn)
    def _():
        through(incoming_ref, staged, add_local)

    @pl.when(jnp.logical_not(is_turn))
    def _():
        through(result_ref, loaded, lambda part: None)


def hand_on(turn, chunk, incoming, local, result):
    rows, features = local.shape
    vmem = pl.BlockSpec(memory_space=pltpu.VMEM)
    hbm = pl.BlockSpec(memory_space=pl.ANY)
    return pl.pallas_call(
        functools.partial(hand_kernel, turn, chunk),
        out_shape=jax.ShapeDtypeStruct((rows, features), jnp.bfloat16),
        in_specs=[hbm, vmem, hbm],
        out_specs=hbm,
        scratch_shapes=[
            pltpu.VMEM((rows, features), jnp.bfloat16),
            pltpu.VMEM((rows, features), jnp.bfloat16),
            pltpu.SemaphoreType.DMA((rows // chunk,)),
            pltpu.SemaphoreType.DMA((rows // chunk,)),
        ],
        compiler_params=pltpu.CompilerParams(vmem_limit_bytes=grant(incoming, local, result)),
        cost_estimate=pl.CostEstimate(flops=0, bytes_accessed=0, transcendentals=0),
        name="hand_on",
    )(incoming, local, result)


def sum_kernel(scale, parts_ref, out_ref):
    total = parts_ref[0]
    for index in range(1, parts_ref.shape[0]):
        total = total + parts_ref[index]
    out_ref[...] = total * scale


def sum_scaled(parts, scale):
    vmem = pl.BlockSpec(memory_space=pltpu.VMEM)
    return pl.pallas_call(
        functools.partial(sum_kernel, scale),
        out_shape=jax.ShapeDtypeStruct(parts.shape[1:], jnp.float32),
        in_specs=[vmem],
        out_specs=vmem,
        compiler_params=pltpu.CompilerParams(vmem_limit_bytes=mebibyte),
        cost_estimate=pl.CostEstimate(flops=parts.size, bytes_accessed=4 * parts.size, transcendentals=0),
        name="sum_scaled",
    )(parts)


def sent_back(group_products, line, plane):
    return [group_products[0]] + [
        along_plane(group_products[step], step, line, plane, back=True) for step in range(1, plane)
    ]


def gathered_products(fold, tokens, shard, line, plane):
    held = {0: shard}
    groups = [(0,)]
    first = products(fold, tokens, [shard], 1)
    if line & (line - 1):
        for step in range(1, line):
            held[step] = along_line(shard, step, line, plane)
        groups.append(tuple(range(1, (line + 1) // 2)))
    elif line > 1:
        distance = line // 2
        while distance:
            held[distance] = along_line(shard, distance, line, plane)
            distance //= 2
        groups.append(tuple(sorted(step for step in held if step)))
        far = line // 2
        held[far], own = lax.optimization_barrier((held[far], first[0]))
        first = [own] + list(first[1:])
        distance = line // 4
        while distance:
            for step in sorted(held):
                if step and step % (2 * distance) == 0 and step + distance not in held:
                    held[step + distance] = along_line(held[step], distance, line, plane)
            distance //= 2
    groups.append(tuple(step for step in range(line) if not any(step in group for group in groups)))
    groups = [group for group in groups if group]
    pieces = [sent_back(first, line, plane)]
    for group in groups[1:]:
        shards = [held[step] for step in group]
        made = list(products(fold, tokens, shards, product_cost))
        if len(pieces) == 1:
            made[-1], pieces[0] = lax.optimization_barrier((made[-1], pieces[0]))
        pieces.append(sent_back(made, line, plane))
    return groups, pieces


def on_device(activations, key_grads, top_grad, norm_gains, w_key, lengths):
    micro_count, seq_rows, features = activations.shape[2:]
    rows = micro_count * seq_rows
    fold = math.gcd(rows, 16)
    replicas = lax.axis_size("dp")
    sections = lax.axis_size("section")
    plane = plane_size(replicas)
    line = replicas // plane
    grad_scale = 1.0 / math.sqrt(replicas * rows)
    act = activations.reshape(rows, features)

    key_rows = key_grads.reshape(rows, key_grads.shape[-1])
    inverse, own_rows = lax.optimization_barrier((live_inverse(seq_rows, lengths[0], act), key_rows))
    tokens = [own_rows] + [along_plane(key_rows, step, line, plane) for step in range(1, plane)]
    groups, pieces = gathered_products(fold, tokens, w_key[0], line, plane)
    split = max(1, len(groups) - 1)
    early, late = ([part[step] for step in range(plane) for part in some] for some in (pieces[:split], pieces[split:]))
    early = placed_early(line, plane, groups[:split], fold, inverse, act, norm_gains, early)
    top = top_grad.reshape(rows, features)
    passed, local, gain_blocks = finish(
        line, plane, groups[split:], fold, early, inverse, act, top, norm_gains, late
    )

    result = passed
    for turn in range(sections - 2, -1, -1):
        incoming = lax.ppermute(result, "section", [(turn + 1, turn)])
        result = hand_on(turn, seq_rows, incoming, local, result)

    gain_parts = lax.all_to_all(gain_blocks, "dp", split_axis=0, concat_axis=0, tiled=True)
    gain_parts, result = lax.optimization_barrier((gain_parts, result))
    grad_shard = sum_scaled(gain_parts, grad_scale)
    return (result.reshape(activations.shape), grad_shard)


def solution(mesh):
    placed = (
        P("section", "dp", None, None, None),
        P("section", "dp", None, None, None),
        P("dp", None, None, None),
        P("section", None),
        P("section", "dp", None),
        P("dp", None),
    )
    return jax.shard_map(
        on_device,
        mesh=mesh,
        in_specs=placed,
        out_specs=(P("section", "dp", None, None, None), P("section", "dp")),
        check_vma=False,
    )
```

profile of v0, /device:TPU:0, one launch (start us, length us, event | category | flops | bytes accessed | tf_op | source)
XLA Modules:
  0.0 58.3 jit_solution(16318702547452380493)
XLA Ops:
  0.6 4.1 %collective-permute-start.4 = (bf16[264,640]{1,0:T(8,128)(2,1)}, bf16[264,640]{1,0:T(8,128)(2,1)S(1)}, u32[]{:S(2)}, u32[]{:S(2)}) collective-permute-start(bf16[264,640]{1,0:T(8,128)(2,1)} %bitcast.10), channel_id=1, source_target_pairs={{0,16},{2,18},{4,20},{6,22},{8,24},{10,26},{12,28},{14,30},{16,0},... | collective-permute-start | bytes 1013768 | tf_op jit(solution)/shard_map/ppermute | solution.py:49
  4.7 1.6 %collective-permute-start.3 = (bf16[264,640]{1,0:T(8,128)(2,1)}, bf16[264,640]{1,0:T(8,128)(2,1)S(1)}, u32[]{:S(2)}, u32[]{:S(2)}) collective-permute-start(bf16[264,640]{1,0:T(8,128)(2,1)} %bitcast.11), channel_id=1, source_target_pairs={{0,8},{2,10},{4,12},{6,14},{8,0},{10,2},{12,4},{14,6},{16,24},{18,... | collective-permute-start | bytes 1013768 | tf_op jit(solution)/shard_map/ppermute | solution.py:49
  6.3 2.4 %collective-permute-start.2 = (bf16[192,640]{1,0:T(8,128)(2,1)}, bf16[192,640]{1,0:T(8,128)(2,1)S(1)}, u32[]{:S(2)}, u32[]{:S(2)}) collective-permute-start(bf16[192,640]{1,0:T(8,128)(2,1)} %bitcast.13), channel_id=1, source_target_pairs={{0,6},{2,4},{4,2},{6,0},{8,14},{10,12},{12,10},{14,8},{16,22},{18,... | collective-permute-start | bytes 737288 | tf_op jit(solution)/shard_map/ppermute | solution.py:59
  8.8 0.5 collective-permute-start.1
  9.3 0.5 collective-permute-start
  9.8 1.4 %copy-done = bf16[1,1,4,48,4224]{4,3,2,1,0:T(8,128)(2,1)S(1)} copy-done((bf16[1,1,4,48,4224]{4,3,2,1,0:T(8,128)(2,1)S(1)}, bf16[1,1,4,48,4224]{4,3,2,1,0:T(8,128)(2,1)}, u32[]{:S(2)}) %copy-start) | copy-done | bytes 1622040
  11.2 0.7 %copy-done.6 = s32[1,4]{1,0:T(1,128)S(1)} copy-done((s32[1,4]{1,0:T(1,128)S(1)}, s32[1,4]{1,0:T(1,128)}, u32[]{:S(2)}) %copy-start.6) | copy-done | bytes 40
  11.9 2.0 %live_inverse.1.inverse_ref = f32[192,128]{1,0:T(8,128)S(1)} custom-call(s32[4]{0:T(128)S(1)} %bitcast.19, bf16[192,4224]{1,0:T(8,128)(2,1)S(1)} %bitcast.6), custom_call_target="tpu_custom_call" | custom-call | flops 1622016 | bytes 1622016 | tf_op jit(solution)/shard_map/live_inverse/pallas_call | solution.py:132
  13.9 2.5 %collective-permute-done.2.refs_3_ = bf16[192,640]{1,0:T(8,128)(2,1)S(1)} collective-permute-done((bf16[192,640]{1,0:T(8,128)(2,1)}, bf16[192,640]{1,0:T(8,128)(2,1)S(1)}, u32[]{:S(2)}, u32[]{:S(2)}) %collective-permute-start.2) | collective-permute-done | bytes 245792 | tf_op jit(solution)/shard_map/ppermute | solution.py:59
  16.4 3.5 %collective-permute-done.1.refs_2_ = bf16[192,640]{1,0:T(8,128)(2,1)S(1)} collective-permute-done((bf16[192,640]{1,0:T(8,128)(2,1)}, bf16[192,640]{1,0:T(8,128)(2,1)S(1)}, u32[]{:S(2)}, u32[]{:S(2)}) %collective-permute-start.1) | collective-permute-done | bytes 245792 | tf_op jit(solution)/shard_map/ppermute | solution.py:59
  19.8 0.1 collective-permute-done.refs_1_
  19.9 0.0 copy-done.3
  19.9 0.0 copy-done.4
  19.9 0.9 %token_products.3 = (bf16[1,16,3168]{2,1,0:T(8,128)(2,1)S(1)}, bf16[1,16,3168]{2,1,0:T(8,128)(2,1)S(1)}, bf16[1,16,3168]{2,1,0:T(8,128)(2,1)S(1)}, bf16[1,16,3168]{2,1,0:T(8,128)(2,1)S(1)}) custom-call(bf16[192,640]{1,0:T(8,128)(2,1)S(1)} %bitcast.16, bf16[192,640]{1,0:T(8,128)(2,1)S(1)} %collective-permute-done.refs_1_, ...), custom_call_target="tpu_custom_call" | custom-call | flops 259522560 | bytes 1726464 | tf_op jit(solution)/shard_map/token_products/pallas_call | solution.py:85
  20.8 1.6 %collective-permute-start.5 = (bf16[1,16,3168]{2,1,0:T(8,128)(2,1)S(1)}, bf16[1,16,3168]{2,1,0:T(8,128)(2,1)S(1)}, u32[]{:S(2)}, u32[]{:S(2)}) collective-permute-start(bf16[1,16,3168]{2,1,0:T(8,128)(2,1)S(1)} %get-tuple-element.37), channel_id=1, source_target_pairs={{0,2},{2,0},{4,6},{6,4},{8,10},{10,8},{12,14},{14,12},{16,18},{18,... | collective-permute-start | bytes 304136 | tf_op jit(solution)/shard_map/ppermute | solution.py:59
  22.4 0.7 %collective-permute-start.6 = (bf16[1,16,3168]{2,1,0:T(8,128)(2,1)S(1)}, bf16[1,16,3168]{2,1,0:T(8,128)(2,1)S(1)}, u32[]{:S(2)}, u32[]{:S(2)}) collective-permute-start(bf16[1,16,3168]{2,1,0:T(8,128)(2,1)S(1)} %get-tuple-element.38), channel_id=1, source_target_pairs={{0,4},{2,6},{4,0},{6,2},{8,12},{10,14},{12,8},{14,10},{16,20},{18,... | collective-permute-start | bytes 304136 | tf_op jit(solution)/shard_map/ppermute | solution.py:59
  23.1 1.3 %collective-permute-start.7 = (bf16[1,16,3168]{2,1,0:T(8,128)(2,1)S(1)}, bf16[1,16,3168]{2,1,0:T(8,128)(2,1)S(1)}, u32[]{:S(2)}, u32[]{:S(2)}) collective-permute-start(bf16[1,16,3168]{2,1,0:T(8,128)(2,1)S(1)} %get-tuple-element.39), channel_id=1, source_target_pairs={{0,6},{2,4},{4,2},{6,0},{8,14},{10,12},{12,10},{14,8},{16,22},{18,... | collective-permute-start | bytes 304136 | tf_op jit(solution)/shard_map/ppermute | solution.py:59
  24.4 0.0 collective-permute-done.4.refs_5_
  24.4 0.5 collective-permute-start.11
  24.8 0.0 collective-permute-done.3.refs_4_
  24.8 1.6 %token_products.4 = (bf16[2,16,3168]{2,1,0:T(8,128)(2,1)S(1)}, bf16[2,16,3168]{2,1,0:T(8,128)(2,1)S(1)}, bf16[2,16,3168]{2,1,0:T(8,128)(2,1)S(1)}, bf16[2,16,3168]{2,1,0:T(8,128)(2,1)S(1)}) custom-call(bf16[192,640]{1,0:T(8,128)(2,1)S(1)} %bitcast.17, bf16[192,640]{1,0:T(8,128)(2,1)S(1)} %collective-permute-done.refs_1_, ...), custom_call_target="tpu_custom_call" | custom-call | flops 5190451200 | bytes 2469888 | tf_op jit(solution)/shard_map/token_products/pallas_call | solution.py:85
  26.5 1.6 %collective-permute-start.8 = (bf16[2,16,3168]{2,1,0:T(8,128)(2,1)S(1)}, bf16[2,16,3168]{2,1,0:T(8,128)(2,1)S(1)}, u32[]{:S(2)}, u32[]{:S(2)}) collective-permute-start(bf16[2,16,3168]{2,1,0:T(8,128)(2,1)S(1)} %get-tuple-element.43), channel_id=1, source_target_pairs={{0,2},{2,0},{4,6},{6,4},{8,10},{10,8},{12,14},{14,12},{16,18},{18,... | collective-permute-start | bytes 608264 | tf_op jit(solution)/shard_map/ppermute | solution.py:59
  28.0 0.0 collective-permute-done.5.refs_2_
  28.0 0.7 %collective-permute-start.9 = (bf16[2,16,3168]{2,1,0:T(8,128)(2,1)S(1)}, bf16[2,16,3168]{2,1,0:T(8,128)(2,1)S(1)}, u32[]{:S(2)}, u32[]{:S(2)}) collective-permute-start(bf16[2,16,3168]{2,1,0:T(8,128)(2,1)S(1)} %get-tuple-element.45), channel_id=1, source_target_pairs={{0,4},{2,6},{4,0},{6,2},{8,12},{10,14},{12,8},{14,10},{16,20},{18,... | collective-permute-start | bytes 608264 | tf_op jit(solution)/shard_map/ppermute | solution.py:59
  28.8 0.3 collective-permute-done.6.refs_4_
  29.1 0.0 collective-permute-done.7.refs_6_
  29.1 1.6 %collective-permute-start.10 = (bf16[2,16,3168]{2,1,0:T(8,128)(2,1)S(1)}, bf16[2,16,3168]{2,1,0:T(8,128)(2,1)S(1)}, u32[]{:S(2)}, u32[]{:S(2)}) collective-permute-start(bf16[2,16,3168]{2,1,0:T(8,128)(2,1)S(1)} %get-tuple-element.47), channel_id=1, source_target_pairs={{0,6},{2,4},{4,2},{6,0},{8,14},{10,12},{12,10},{14,8},{16,22},{18,... | collective-permute-start | bytes 608264 | tf_op jit(solution)/shard_map/ppermute | solution.py:59
  30.7 2.7 %collective-permute-done.11.refs_4_ = bf16[264,640]{1,0:T(8,128)(2,1)S(1)} collective-permute-done((bf16[264,640]{1,0:T(8,128)(2,1)S(1)}, bf16[264,640]{1,0:T(8,128)(2,1)S(1)}, u32[]{:S(2)}, u32[]{:S(2)}) %collective-permute-start.11) | collective-permute-done | bytes 337952 | tf_op jit(solution)/shard_map/ppermute | solution.py:49
  33.3 0.9 %token_products.5 = (bf16[1,16,3168]{2,1,0:T(8,128)(2,1)S(1)}, bf16[1,16,3168]{2,1,0:T(8,128)(2,1)S(1)}, bf16[1,16,3168]{2,1,0:T(8,128)(2,1)S(1)}, bf16[1,16,3168]{2,1,0:T(8,128)(2,1)S(1)}) custom-call(bf16[192,640]{1,0:T(8,128)(2,1)S(1)} %bitcast.18, bf16[192,640]{1,0:T(8,128)(2,1)S(1)} %collective-permute-done.refs_1_, ...), custom_call_target="tpu_custom_call" | custom-call | flops 2595225600 | bytes 1726464 | tf_op jit(solution)/shard_map/token_products/pallas_call | solution.py:85
  34.2 0.0 copy-start.2
  34.2 1.6 %collective-permute-start.12 = (bf16[1,16,3168]{2,1,0:T(8,128)(2,1)S(1)}, bf16[1,16,3168]{2,1,0:T(8,128)(2,1)S(1)}, u32[]{:S(2)}, u32[]{:S(2)}) collective-permute-start(bf16[1,16,3168]{2,1,0:T(8,128)(2,1)S(1)} %get-tuple-element.52), channel_id=1, source_target_pairs={{0,2},{2,0},{4,6},{6,4},{8,10},{10,8},{12,14},{14,12},{16,18},{18,... | collective-permute-start | bytes 304136 | tf_op jit(solution)/shard_map/ppermute | solution.py:59
  35.8 0.4 collective-permute-start.13
  36.2 0.0 collective-permute-done.8.refs_3_
  36.2 1.6 %collective-permute-start.14 = (bf16[1,16,3168]{2,1,0:T(8,128)(2,1)S(1)}, bf16[1,16,3168]{2,1,0:T(8,128)(2,1)S(1)}, u32[]{:S(2)}, u32[]{:S(2)}) collective-permute-start(bf16[1,16,3168]{2,1,0:T(8,128)(2,1)S(1)} %get-tuple-element.54), channel_id=1, source_target_pairs={{0,6},{2,4},{4,2},{6,0},{8,14},{10,12},{12,10},{14,8},{16,22},{18,... | collective-permute-start | bytes 304136 | tf_op jit(solution)/shard_map/ppermute | solution.py:59
  37.8 0.0 collective-permute-done.9.refs_5_
  37.8 1.4 %collective-permute-done.10.refs_7_ = bf16[2,16,3168]{2,1,0:T(8,128)(2,1)S(1)} collective-permute-done((bf16[2,16,3168]{2,1,0:T(8,128)(2,1)S(1)}, bf16[2,16,3168]{2,1,0:T(8,128)(2,1)S(1)}, u32[]{:S(2)}, u32[]{:S(2)}) %collective-permute-start.10) | collective-permute-done | bytes 202784 | tf_op jit(solution)/shard_map/ppermute | solution.py:59
  39.2 0.0 copy-done.5
  39.2 1.8 %placed_early.1 = (bf16[192,4224]{1,0:T(8,128)(2,1)S(1)}, f32[192,128]{1,0:T(8,128)S(1)}, f32[8,4224]{1,0:T(8,128)S(1)}) custom-call(f32[192,128]{1,0:T(8,128)S(1)} %live_inverse.1.inverse_ref, bf16[192,4224]{1,0:T(8,128)(2,1)S(1)} %bitcast.7, f32[1,4224]{1,0:T(1,128)S(1)} %copy-done.5, bf16[1,16,3168]{2,1,0:T(8,128)(2,1)S(1)} %get-tuple-element.40.refs_0_, ...), custom_call_target="tpu_custom_call" | custom-call | flops 6488064 | bytes 6488064 | tf_op jit(solution)/shard_map/placed_early/pallas_call | solution.py:219
  41.0 0.0 collective-permute-done.12.refs_1_
  41.1 1.4 %collective-permute-done.13.refs_2_ = bf16[1,16,3168]{2,1,0:T(8,128)(2,1)S(1)} collective-permute-done((bf16[1,16,3168]{2,1,0:T(8,128)(2,1)S(1)}, bf16[1,16,3168]{2,1,0:T(8,128)(2,1)S(1)}, u32[]{:S(2)}, u32[]{:S(2)}) %collective-permute-start.13) | collective-permute-done | bytes 101408 | tf_op jit(solution)/shard_map/ppermute | solution.py:59
  42.4 0.0 collective-permute-done.14.refs_3_
  42.4 2.8 %norm_backward.1 = (bf16[192,4224]{1,0:T(8,128)(2,1)}, f32[192,4224]{1,0:T(8,128)S(1)}, f32[16,1,264]{2,1,0:T(1,128)}) custom-call(bf16[192,4224]{1,0:T(8,128)(2,1)S(1)} %get-tuple-element.48.early_ref, f32[192,128]{1,0:T(8,128)S(1)} %get-tuple-element.49.early_pulls, f32[8,4224]{1,0:T(8,128)S(1)} %get-tuple-element.50.early_gains, ...), custom_call_target="tpu_custom_call" | custom-call | flops 12976128 | bytes 9732096 | tf_op jit(solution)/shard_map/norm_backward/pallas_call | solution.py:313
  45.3 1.3 %collective-permute-start.15 = (bf16[192,4224]{1,0:T(8,128)(2,1)}, bf16[192,4224]{1,0:T(8,128)(2,1)}, u32[]{:S(2)}, u32[]{:S(2)}) collective-permute-start(bf16[192,4224]{1,0:T(8,128)(2,1)} %get-tuple-element.56.result_ref), channel_id=1, source_target_pairs={{1,0},{3,2},{5,4},{7,6},{9,8},{11,10},{13,12},{15,14},{17,16},{19,... | collective-permute-start | bytes 4866056 | tf_op jit(solution)/shard_map/ppermute | solution.py:473
  46.6 3.8 %all-to-all-start = ((f32[16,1,264]{2,1,0:T(1,128)}), f32[16,1,264]{2,1,0:T(1,128)S(1)}, u32[]{:S(2)}, u32[]{:S(2)}) async-start(f32[16,1,264]{2,1,0:T(1,128)} %get-tuple-element.55), calls=%async_computation | async-start | bytes 49152 | tf_op jit(solution)/shard_map/all_to_all | solution.py:476
  50.3 0.6 %collective-permute-done.15.incoming_ref = bf16[192,4224]{1,0:T(8,128)(2,1)} collective-permute-done((bf16[192,4224]{1,0:T(8,128)(2,1)}, bf16[192,4224]{1,0:T(8,128)(2,1)}, u32[]{:S(2)}, u32[]{:S(2)}) %collective-permute-start.15) | collective-permute-done | bytes 1622048 | tf_op jit(solution)/shard_map/ppermute | solution.py:473
  51.0 2.3 %hand_on.1 = bf16[192,4224]{1,0:T(8,128)(2,1)} custom-call(bf16[192,4224]{1,0:T(8,128)(2,1)} %collective-permute-done.15.incoming_ref, f32[192,4224]{1,0:T(8,128)S(1)} %get-tuple-element.57.local_ref, bf16[192,4224]{1,0:T(8,128)(2,1)} %get-tuple-element.56.result_ref), custom_call_target="tpu_custom_call" | custom-call | tf_op jit(solution)/shard_map/hand_on/pallas_call | solution.py:370
  53.3 4.4 %all-to-all-done.parts_ref = f32[16,1,264]{2,1,0:T(1,128)S(1)} async-done(((f32[16,1,264]{2,1,0:T(1,128)}), f32[16,1,264]{2,1,0:T(1,128)S(1)}, u32[]{:S(2)}, u32[]{:S(2)}) %all-to-all-start) | async-done | bytes 16928 | tf_op jit(solution)/shard_map/all_to_all | solution.py:476
  57.7 0.6 sum_scaled.1
  (8 shorter events, 0.0 us)
Async XLA Ops:
  0.6 23.8 %collective-permute-start.4 = (bf16[264,640]{1,0:T(8,128)(2,1)}, bf16[264,640]{1,0:T(8,128)(2,1)S(1)}, u32[]{:S(2)}, u32[]{:S(2)}) collective-permute-start(bf16[264,640]{1,0:T(8,128)(2,1)} %bitcast.10), channel_id=1, source_target_pairs={{0,16},{2,18},{4,20},{6,22},{8,24},{10,26},{12,28},{14,30},{16,0},... | collective-permute-start | bytes 1013768 | tf_op jit(solution)/shard_map/ppermute | solution.py:49
  4.7 20.1 %collective-permute-start.3 = (bf16[264,640]{1,0:T(8,128)(2,1)}, bf16[264,640]{1,0:T(8,128)(2,1)S(1)}, u32[]{:S(2)}, u32[]{:S(2)}) collective-permute-start(bf16[264,640]{1,0:T(8,128)(2,1)} %bitcast.11), channel_id=1, source_target_pairs={{0,8},{2,10},{4,12},{6,14},{8,0},{10,2},{12,4},{14,6},{16,24},{18,... | collective-permute-start | bytes 1013768 | tf_op jit(solution)/shard_map/ppermute | solution.py:49
  6.3 10.0 %collective-permute-start.2 = (bf16[192,640]{1,0:T(8,128)(2,1)}, bf16[192,640]{1,0:T(8,128)(2,1)S(1)}, u32[]{:S(2)}, u32[]{:S(2)}) collective-permute-start(bf16[192,640]{1,0:T(8,128)(2,1)} %bitcast.13), channel_id=1, source_target_pairs={{0,6},{2,4},{4,2},{6,0},{8,14},{10,12},{12,10},{14,8},{16,22},{18,... | collective-permute-start | bytes 737288 | tf_op jit(solution)/shard_map/ppermute | solution.py:59
  8.8 11.1 %collective-permute-start.1 = (bf16[192,640]{1,0:T(8,128)(2,1)}, bf16[192,640]{1,0:T(8,128)(2,1)S(1)}, u32[]{:S(2)}, u32[]{:S(2)}) collective-permute-start(bf16[192,640]{1,0:T(8,128)(2,1)} %bitcast.14), channel_id=1, source_target_pairs={{0,4},{2,6},{4,0},{6,2},{8,12},{10,14},{12,8},{14,10},{16,20},{18,... | collective-permute-start | bytes 737288 | tf_op jit(solution)/shard_map/ppermute | solution.py:59
  9.3 10.7 %collective-permute-start = (bf16[192,640]{1,0:T(8,128)(2,1)}, bf16[192,640]{1,0:T(8,128)(2,1)S(1)}, u32[]{:S(2)}, u32[]{:S(2)}) collective-permute-start(bf16[192,640]{1,0:T(8,128)(2,1)} %bitcast.15), channel_id=1, source_target_pairs={{0,2},{2,0},{4,6},{6,4},{8,10},{10,8},{12,14},{14,12},{16,18},{18,... | collective-permute-start | bytes 737288 | tf_op jit(solution)/shard_map/ppermute | solution.py:59
  9.8 1.4 %copy-start = (bf16[1,1,4,48,4224]{4,3,2,1,0:T(8,128)(2,1)S(1)}, bf16[1,1,4,48,4224]{4,3,2,1,0:T(8,128)(2,1)}, u32[]{:S(2)}) copy-start(bf16[1,1,4,48,4224]{4,3,2,1,0:T(8,128)(2,1)} %param.6) | copy-start | bytes 4866052
  11.2 0.7 %copy-start.6 = (s32[1,4]{1,0:T(1,128)S(1)}, s32[1,4]{1,0:T(1,128)}, u32[]{:S(2)}) copy-start(s32[1,4]{1,0:T(1,128)} %param.11) | copy-start | bytes 52
  11.9 8.0 %copy-start.3 = (bf16[1,264,640]{2,1,0:T(8,128)(2,1)S(1)}, bf16[1,264,640]{2,1,0:T(8,128)(2,1)}, u32[]{:S(2)}) copy-start(bf16[1,264,640]{2,1,0:T(8,128)(2,1)} %param.10) | copy-start | bytes 1013764
  11.9 8.0 %copy-start.4 = (bf16[1,1,4,48,640]{4,3,2,1,0:T(8,128)(2,1)S(1)}, bf16[1,1,4,48,640]{4,3,2,1,0:T(8,128)(2,1)}, u32[]{:S(2)}) copy-start(bf16[1,1,4,48,640]{4,3,2,1,0:T(8,128)(2,1)} %param.7) | copy-start | bytes 737284
  20.8 7.2 %collective-permute-start.5 = (bf16[1,16,3168]{2,1,0:T(8,128)(2,1)S(1)}, bf16[1,16,3168]{2,1,0:T(8,128)(2,1)S(1)}, u32[]{:S(2)}, u32[]{:S(2)}) collective-permute-start(bf16[1,16,3168]{2,1,0:T(8,128)(2,1)S(1)} %get-tuple-element.37), channel_id=1, source_target_pairs={{0,2},{2,0},{4,6},{6,4},{8,10},{10,8},{12,14},{14,12},{16,18},{18,... | collective-permute-start | bytes 304136 | tf_op jit(solution)/shard_map/ppermute | solution.py:59
  22.4 6.7 %collective-permute-start.6 = (bf16[1,16,3168]{2,1,0:T(8,128)(2,1)S(1)}, bf16[1,16,3168]{2,1,0:T(8,128)(2,1)S(1)}, u32[]{:S(2)}, u32[]{:S(2)}) collective-permute-start(bf16[1,16,3168]{2,1,0:T(8,128)(2,1)S(1)} %get-tuple-element.38), channel_id=1, source_target_pairs={{0,4},{2,6},{4,0},{6,2},{8,12},{10,14},{12,8},{14,10},{16,20},{18,... | collective-permute-start | bytes 304136 | tf_op jit(solution)/shard_map/ppermute | solution.py:59
  23.1 6.0 %collective-permute-start.7 = (bf16[1,16,3168]{2,1,0:T(8,128)(2,1)S(1)}, bf16[1,16,3168]{2,1,0:T(8,128)(2,1)S(1)}, u32[]{:S(2)}, u32[]{:S(2)}) collective-permute-start(bf16[1,16,3168]{2,1,0:T(8,128)(2,1)S(1)} %get-tuple-element.39), channel_id=1, source_target_pairs={{0,6},{2,4},{4,2},{6,0},{8,14},{10,12},{12,10},{14,8},{16,22},{18,... | collective-permute-start | bytes 304136 | tf_op jit(solution)/shard_map/ppermute | solution.py:59
  24.4 8.9 %collective-permute-start.11 = (bf16[264,640]{1,0:T(8,128)(2,1)S(1)}, bf16[264,640]{1,0:T(8,128)(2,1)S(1)}, u32[]{:S(2)}, u32[]{:S(2)}) collective-permute-start(bf16[264,640]{1,0:T(8,128)(2,1)S(1)} %collective-permute-done.4.refs_5_), channel_id=1, source_target_pairs={{0,8},{2,10},{4,12},{6,14},{8,0},{10,2},{12,4},{14,6},{16,24},{18,... | collective-permute-start | bytes 1013768 | tf_op jit(solution)/shard_map/ppermute | solution.py:49
  26.5 9.7 %collective-permute-start.8 = (bf16[2,16,3168]{2,1,0:T(8,128)(2,1)S(1)}, bf16[2,16,3168]{2,1,0:T(8,128)(2,1)S(1)}, u32[]{:S(2)}, u32[]{:S(2)}) collective-permute-start(bf16[2,16,3168]{2,1,0:T(8,128)(2,1)S(1)} %get-tuple-element.43), channel_id=1, source_target_pairs={{0,2},{2,0},{4,6},{6,4},{8,10},{10,8},{12,14},{14,12},{16,18},{18,... | collective-permute-start | bytes 608264 | tf_op jit(solution)/shard_map/ppermute | solution.py:59
  28.0 9.8 %collective-permute-start.9 = (bf16[2,16,3168]{2,1,0:T(8,128)(2,1)S(1)}, bf16[2,16,3168]{2,1,0:T(8,128)(2,1)S(1)}, u32[]{:S(2)}, u32[]{:S(2)}) collective-permute-start(bf16[2,16,3168]{2,1,0:T(8,128)(2,1)S(1)} %get-tuple-element.45), channel_id=1, source_target_pairs={{0,4},{2,6},{4,0},{6,2},{8,12},{10,14},{12,8},{14,10},{16,20},{18,... | collective-permute-start | bytes 608264 | tf_op jit(solution)/shard_map/ppermute | solution.py:59
  29.1 10.1 %copy-start.1 = (bf16[1,1,4,48,4224]{4,3,2,1,0:T(8,128)(2,1)S(1)}, bf16[1,1,4,48,4224]{4,3,2,1,0:T(8,128)(2,1)}, u32[]{:S(2)}) copy-start(bf16[1,1,4,48,4224]{4,3,2,1,0:T(8,128)(2,1)} %param.6) | copy-start | bytes 4866052
  29.1 10.1 %copy-start.5 = (f32[1,4224]{1,0:T(1,128)S(1)}, f32[1,4224]{1,0:T(1,128)}, u32[]{:S(2)}) copy-start(f32[1,4224]{1,0:T(1,128)} %gain_ref.3) | copy-start | bytes 50692
  29.1 10.1 %collective-permute-start.10 = (bf16[2,16,3168]{2,1,0:T(8,128)(2,1)S(1)}, bf16[2,16,3168]{2,1,0:T(8,128)(2,1)S(1)}, u32[]{:S(2)}, u32[]{:S(2)}) collective-permute-start(bf16[2,16,3168]{2,1,0:T(8,128)(2,1)S(1)} %get-tuple-element.47), channel_id=1, source_target_pairs={{0,6},{2,4},{4,2},{6,0},{8,14},{10,12},{12,10},{14,8},{16,22},{18,... | collective-permute-start | bytes 608264 | tf_op jit(solution)/shard_map/ppermute | solution.py:59
  34.2 8.2 %copy-start.2 = (bf16[1,4,48,4224]{3,2,1,0:T(8,128)(2,1)S(1)}, bf16[1,4,48,4224]{3,2,1,0:T(8,128)(2,1)}, u32[]{:S(2)}) copy-start(bf16[1,4,48,4224]{3,2,1,0:T(8,128)(2,1)} %param.8) | copy-start | bytes 4866052
  34.2 6.8 %collective-permute-start.12 = (bf16[1,16,3168]{2,1,0:T(8,128)(2,1)S(1)}, bf16[1,16,3168]{2,1,0:T(8,128)(2,1)S(1)}, u32[]{:S(2)}, u32[]{:S(2)}) collective-permute-start(bf16[1,16,3168]{2,1,0:T(8,128)(2,1)S(1)} %get-tuple-element.52), channel_id=1, source_target_pairs={{0,2},{2,0},{4,6},{6,4},{8,10},{10,8},{12,14},{14,12},{16,18},{18,... | collective-permute-start | bytes 304136 | tf_op jit(solution)/shard_map/ppermute | solution.py:59
  35.8 6.6 %collective-permute-start.13 = (bf16[1,16,3168]{2,1,0:T(8,128)(2,1)S(1)}, bf16[1,16,3168]{2,1,0:T(8,128)(2,1)S(1)}, u32[]{:S(2)}, u32[]{:S(2)}) collective-permute-start(bf16[1,16,3168]{2,1,0:T(8,128)(2,1)S(1)} %get-tuple-element.53), channel_id=1, source_target_pairs={{0,4},{2,6},{4,0},{6,2},{8,12},{10,14},{12,8},{14,10},{16,20},{18,... | collective-permute-start | bytes 304136 | tf_op jit(solution)/shard_map/ppermute | solution.py:59
  36.2 6.2 %collective-permute-start.14 = (bf16[1,16,3168]{2,1,0:T(8,128)(2,1)S(1)}, bf16[1,16,3168]{2,1,0:T(8,128)(2,1)S(1)}, u32[]{:S(2)}, u32[]{:S(2)}) collective-permute-start(bf16[1,16,3168]{2,1,0:T(8,128)(2,1)S(1)} %get-tuple-element.54), channel_id=1, source_target_pairs={{0,6},{2,4},{4,2},{6,0},{8,14},{10,12},{12,10},{14,8},{16,22},{18,... | collective-permute-start | bytes 304136 | tf_op jit(solution)/shard_map/ppermute | solution.py:59
  45.3 5.7 %collective-permute-start.15 = (bf16[192,4224]{1,0:T(8,128)(2,1)}, bf16[192,4224]{1,0:T(8,128)(2,1)}, u32[]{:S(2)}, u32[]{:S(2)}) collective-permute-start(bf16[192,4224]{1,0:T(8,128)(2,1)} %get-tuple-element.56.result_ref), channel_id=1, source_target_pairs={{1,0},{3,2},{5,4},{7,6},{9,8},{11,10},{13,12},{15,14},{17,16},{19,... | collective-permute-start | bytes 4866056 | tf_op jit(solution)/shard_map/ppermute | solution.py:473
  46.6 11.1 %all-to-all-start = ((f32[16,1,264]{2,1,0:T(1,128)}), f32[16,1,264]{2,1,0:T(1,128)S(1)}, u32[]{:S(2)}, u32[]{:S(2)}) async-start(f32[16,1,264]{2,1,0:T(1,128)} %get-tuple-element.55), calls=%async_computation | async-start | bytes 49152 | tf_op jit(solution)/shard_map/all_to_all | solution.py:476
where the time goes:
time: 58.9 us; the launch traced here: 58.3 us
  starting transfers between devices  25.6 us (43%)
  waiting for transfers between devices  16.9 us (29%)
  Pallas kernels  12.9 us (22%)
  local copies, waits for them, and re-layouts  2.1 us (4%)
  between operations  0.73 us (1%)
    ppermute x12, starting transfers between devices, along_plane(): return lax.ppermute(value, 'dp', pairs)  14.4 us
    ppermute x12, waiting for transfers between devices, along_plane(): return lax.ppermute(value, 'dp', pairs)  9.17 us
    ppermute x3, starting transfers between devices, along_line(): return lax.ppermute(value, 'dp', pairs)  6.13 us
    all_to_all x1, waiting for transfers between devices, on_device(): lax.all_to_all(gain_blocks, 'dp', split_axis=0, concat_axis=0, tiled=True)  4.41 us
    all_to_all x1, starting transfers between devices, on_device(): lax.all_to_all(gain_blocks, 'dp', split_axis=0, concat_axis=0, tiled=True)  3.76 us
    pallas_call x3, Pallas kernels, products(): pl.pallas_call(functools.partial(product_kernel, len(tokens), count, fold...  3.43 us
    pallas_call x1, Pallas kernels, finish(): pl.pallas_call(functools.partial(finish_kernel, line, plane, groups, fold...  2.82 us
    ppermute x3, waiting for transfers between devices, along_line(): return lax.ppermute(value, 'dp', pairs)  2.66 us
  transfers between devices with their start and end apart: 17, of which 9 were waited for; matrix products, arithmetic and copies ran while one was open for 0% of the time, Pallas kernels for 16%

commit v1 on v0

--- a/solution.py
+++ b/solution.py
@@ -470,7 +470,7 @@
 
     result = passed
     for turn in range(sections - 2, -1, -1):
-        incoming = lax.ppermute(result, "section", [(turn + 1, turn)])
+        incoming = lax.ppermute(result, "section", [(turn + 1, turn), (turn, turn + 1)])
         result = hand_on(turn, seq_rows, incoming, local, result)
 
     gain_parts = lax.all_to_all(gain_blocks, "dp", split_axis=0, concat_axis=0, tiled=True)

time: 58.9 us -> 57.3 us (0.973)
  starting transfers between devices: 25.6 us -> 24.4 us
    ppermute x1, starting transfers between devices: 1.29 us -> 0.07 us  [on_device(): lax.ppermute(result, 'section', [(turn + 1, turn), (turn, turn + 1)])]
    all_to_all x1, waiting for transfers between devices: 4.41 us -> 5.02 us  [on_device(): lax.all_to_all(gain_blocks, 'dp', split_axis=0, concat_axis=0, tiled=True)]
    ppermute x1, waiting for transfers between devices: 0.65 us -> 0.04 us  [on_device(): lax.ppermute(result, 'section', [(turn + 1, turn), (turn, turn + 1)])]
  transfers between devices with their start and end apart: 17 -> 17, of which waited for: 9 -> 8; matrix products, arithmetic and copies ran while one was open for 0% -> 0% of each run, Pallas kernels for 16% -> 17%
where the time goes in v1:
time: 57.3 us; the launch traced here: 57.1 us
  starting transfers between devices  24.4 us (43%)
  waiting for transfers between devices  16.9 us (29%)
  Pallas kernels  12.9 us (23%)
  local copies, waits for them, and re-layouts  2.1 us (4%)
  between operations  0.73 us (1%)
    ppermute x12, starting transfers between devices, along_plane(): return lax.ppermute(value, 'dp', pairs)  14.4 us
    ppermute x12, waiting for transfers between devices, along_plane(): return lax.ppermute(value, 'dp', pairs)  9.17 us
    ppermute x3, starting transfers between devices, along_line(): return lax.ppermute(value, 'dp', pairs)  6.13 us
    all_to_all x1, waiting for transfers between devices, on_device(): lax.all_to_all(gain_blocks, 'dp', split_axis=0, concat_axis=0, tiled=True)  5.02 us
    all_to_all x1, starting transfers between devices, on_device(): lax.all_to_all(gain_blocks, 'dp', split_axis=0, concat_axis=0, tiled=True)  3.76 us
    pallas_call x3, Pallas kernels, products(): pl.pallas_call(functools.partial(product_kernel, len(tokens), count, fold...  3.43 us
    pallas_call x1, Pallas kernels, finish(): pl.pallas_call(functools.partial(finish_kernel, line, plane, groups, fold...  2.82 us
    ppermute x3, waiting for transfers between devices, along_line(): return lax.ppermute(value, 'dp', pairs)  2.66 us
  transfers between devices with their start and end apart: 17, of which 8 were waited for; matrix products, arithmetic and copies ran while one was open for 0% of the time, Pallas kernels for 17%

profile of v1, /device:TPU:0, one launch (start us, length us, event | category | flops | bytes accessed | tf_op | source)
XLA Modules:
  0.0 57.1 jit_solution(8356760382239340250)
XLA Ops:
  0.6 4.1 %collective-permute-start.4 = (bf16[264,640]{1,0:T(8,128)(2,1)}, bf16[264,640]{1,0:T(8,128)(2,1)S(1)}, u32[]{:S(2)}, u32[]{:S(2)}) collective-permute-start(bf16[264,640]{1,0:T(8,128)(2,1)} %bitcast.10), channel_id=1, source_target_pairs={{0,16},{2,18},{4,20},{6,22},{8,24},{10,26},{12,28},{14,30},{16,0},... | collective-permute-start | bytes 1013768 | tf_op jit(solution)/shard_map/ppermute | solution.py:49
  4.7 1.6 %collective-permute-start.3 = (bf16[264,640]{1,0:T(8,128)(2,1)}, bf16[264,640]{1,0:T(8,128)(2,1)S(1)}, u32[]{:S(2)}, u32[]{:S(2)}) collective-permute-start(bf16[264,640]{1,0:T(8,128)(2,1)} %bitcast.11), channel_id=1, source_target_pairs={{0,8},{2,10},{4,12},{6,14},{8,0},{10,2},{12,4},{14,6},{16,24},{18,... | collective-permute-start | bytes 1013768 | tf_op jit(solution)/shard_map/ppermute | solution.py:49
  6.3 2.4 %collective-permute-start.2 = (bf16[192,640]{1,0:T(8,128)(2,1)}, bf16[192,640]{1,0:T(8,128)(2,1)S(1)}, u32[]{:S(2)}, u32[]{:S(2)}) collective-permute-start(bf16[192,640]{1,0:T(8,128)(2,1)} %bitcast.13), channel_id=1, source_target_pairs={{0,6},{2,4},{4,2},{6,0},{8,14},{10,12},{12,10},{14,8},{16,22},{18,... | collective-permute-start | bytes 737288 | tf_op jit(solution)/shard_map/ppermute | solution.py:59
  8.8 0.5 collective-permute-start.1
  9.3 0.5 collective-permute-start
  9.8 1.4 %copy-done = bf16[1,1,4,48,4224]{4,3,2,1,0:T(8,128)(2,1)S(1)} copy-done((bf16[1,1,4,48,4224]{4,3,2,1,0:T(8,128)(2,1)S(1)}, bf16[1,1,4,48,4224]{4,3,2,1,0:T(8,128)(2,1)}, u32[]{:S(2)}) %copy-start) | copy-done | bytes 1622040
  11.2 0.7 %copy-done.6 = s32[1,4]{1,0:T(1,128)S(1)} copy-done((s32[1,4]{1,0:T(1,128)S(1)}, s32[1,4]{1,0:T(1,128)}, u32[]{:S(2)}) %copy-start.6) | copy-done | bytes 40
  11.9 2.0 %live_inverse.1.inverse_ref = f32[192,128]{1,0:T(8,128)S(1)} custom-call(s32[4]{0:T(128)S(1)} %bitcast.19, bf16[192,4224]{1,0:T(8,128)(2,1)S(1)} %bitcast.6), custom_call_target="tpu_custom_call" | custom-call | flops 1622016 | bytes 1622016 | tf_op jit(solution)/shard_map/live_inverse/pallas_call | solution.py:132
  13.9 2.5 %collective-permute-done.2.refs_3_ = bf16[192,640]{1,0:T(8,128)(2,1)S(1)} collective-permute-done((bf16[192,640]{1,0:T(8,128)(2,1)}, bf16[192,640]{1,0:T(8,128)(2,1)S(1)}, u32[]{:S(2)}, u32[]{:S(2)}) %collective-permute-start.2) | collective-permute-done | bytes 245792 | tf_op jit(solution)/shard_map/ppermute | solution.py:59
  16.4 3.5 %collective-permute-done.1.refs_2_ = bf16[192,640]{1,0:T(8,128)(2,1)S(1)} collective-permute-done((bf16[192,640]{1,0:T(8,128)(2,1)}, bf16[192,640]{1,0:T(8,128)(2,1)S(1)}, u32[]{:S(2)}, u32[]{:S(2)}) %collective-permute-start.1) | collective-permute-done | bytes 245792 | tf_op jit(solution)/shard_map/ppermute | solution.py:59
  19.8 0.1 collective-permute-done.refs_1_
  19.9 0.0 copy-done.3
  19.9 0.0 copy-done.4
  19.9 0.9 %token_products.3 = (bf16[1,16,3168]{2,1,0:T(8,128)(2,1)S(1)}, bf16[1,16,3168]{2,1,0:T(8,128)(2,1)S(1)}, bf16[1,16,3168]{2,1,0:T(8,128)(2,1)S(1)}, bf16[1,16,3168]{2,1,0:T(8,128)(2,1)S(1)}) custom-call(bf16[192,640]{1,0:T(8,128)(2,1)S(1)} %bitcast.16, bf16[192,640]{1,0:T(8,128)(2,1)S(1)} %collective-permute-done.refs_1_, ...), custom_call_target="tpu_custom_call" | custom-call | flops 259522560 | bytes 1726464 | tf_op jit(solution)/shard_map/token_products/pallas_call | solution.py:85
  20.8 1.6 %collective-permute-start.5 = (bf16[1,16,3168]{2,1,0:T(8,128)(2,1)S(1)}, bf16[1,16,3168]{2,1,0:T(8,128)(2,1)S(1)}, u32[]{:S(2)}, u32[]{:S(2)}) collective-permute-start(bf16[1,16,3168]{2,1,0:T(8,128)(2,1)S(1)} %get-tuple-element.37), channel_id=1, source_target_pairs={{0,2},{2,0},{4,6},{6,4},{8,10},{10,8},{12,14},{14,12},{16,18},{18,... | collective-permute-start | bytes 304136 | tf_op jit(solution)/shard_map/ppermute | solution.py:59
  22.4 0.7 %collective-permute-start.6 = (bf16[1,16,3168]{2,1,0:T(8,128)(2,1)S(1)}, bf16[1,16,3168]{2,1,0:T(8,128)(2,1)S(1)}, u32[]{:S(2)}, u32[]{:S(2)}) collective-permute-start(bf16[1,16,3168]{2,1,0:T(8,128)(2,1)S(1)} %get-tuple-element.38), channel_id=1, source_target_pairs={{0,4},{2,6},{4,0},{6,2},{8,12},{10,14},{12,8},{14,10},{16,20},{18,... | collective-permute-start | bytes 304136 | tf_op jit(solution)/shard_map/ppermute | solution.py:59
  23.1 1.3 %collective-permute-start.7 = (bf16[1,16,3168]{2,1,0:T(8,128)(2,1)S(1)}, bf16[1,16,3168]{2,1,0:T(8,128)(2,1)S(1)}, u32[]{:S(2)}, u32[]{:S(2)}) collective-permute-start(bf16[1,16,3168]{2,1,0:T(8,128)(2,1)S(1)} %get-tuple-element.39), channel_id=1, source_target_pairs={{0,6},{2,4},{4,2},{6,0},{8,14},{10,12},{12,10},{14,8},{16,22},{18,... | collective-permute-start | bytes 304136 | tf_op jit(solution)/shard_map/ppermute | solution.py:59
  24.4 0.0 collective-permute-done.4.refs_5_
  24.4 0.5 collective-permute-start.11
  24.8 0.0 collective-permute-done.3.refs_4_
  24.8 1.6 %token_products.4 = (bf16[2,16,3168]{2,1,0:T(8,128)(2,1)S(1)}, bf16[2,16,3168]{2,1,0:T(8,128)(2,1)S(1)}, bf16[2,16,3168]{2,1,0:T(8,128)(2,1)S(1)}, bf16[2,16,3168]{2,1,0:T(8,128)(2,1)S(1)}) custom-call(bf16[192,640]{1,0:T(8,128)(2,1)S(1)} %bitcast.17, bf16[192,640]{1,0:T(8,128)(2,1)S(1)} %collective-permute-done.refs_1_, ...), custom_call_target="tpu_custom_call" | custom-call | flops 5190451200 | bytes 2469888 | tf_op jit(solution)/shard_map/token_products/pallas_call | solution.py:85
  26.5 1.6 %collective-permute-start.8 = (bf16[2,16,3168]{2,1,0:T(8,128)(2,1)S(1)}, bf16[2,16,3168]{2,1,0:T(8,128)(2,1)S(1)}, u32[]{:S(2)}, u32[]{:S(2)}) collective-permute-start(bf16[2,16,3168]{2,1,0:T(8,128)(2,1)S(1)} %get-tuple-element.43), channel_id=1, source_target_pairs={{0,2},{2,0},{4,6},{6,4},{8,10},{10,8},{12,14},{14,12},{16,18},{18,... | collective-permute-start | bytes 608264 | tf_op jit(solution)/shard_map/ppermute | solution.py:59
  28.0 0.0 collective-permute-done.5.refs_2_
  28.0 0.7 %collective-permute-start.9 = (bf16[2,16,3168]{2,1,0:T(8,128)(2,1)S(1)}, bf16[2,16,3168]{2,1,0:T(8,128)(2,1)S(1)}, u32[]{:S(2)}, u32[]{:S(2)}) collective-permute-start(bf16[2,16,3168]{2,1,0:T(8,128)(2,1)S(1)} %get-tuple-element.45), channel_id=1, source_target_pairs={{0,4},{2,6},{4,0},{6,2},{8,12},{10,14},{12,8},{14,10},{16,20},{18,... | collective-permute-start | bytes 608264 | tf_op jit(solution)/shard_map/ppermute | solution.py:59
  28.8 0.3 collective-permute-done.6.refs_4_
  29.1 0.0 collective-permute-done.7.refs_6_
  29.1 1.6 %collective-permute-start.10 = (bf16[2,16,3168]{2,1,0:T(8,128)(2,1)S(1)}, bf16[2,16,3168]{2,1,0:T(8,128)(2,1)S(1)}, u32[]{:S(2)}, u32[]{:S(2)}) collective-permute-start(bf16[2,16,3168]{2,1,0:T(8,128)(2,1)S(1)} %get-tuple-element.47), channel_id=1, source_target_pairs={{0,6},{2,4},{4,2},{6,0},{8,14},{10,12},{12,10},{14,8},{16,22},{18,... | collective-permute-start | bytes 608264 | tf_op jit(solution)/shard_map/ppermute | solution.py:59
  30.7 2.7 %collective-permute-done.11.refs_4_ = bf16[264,640]{1,0:T(8,128)(2,1)S(1)} collective-permute-done((bf16[264,640]{1,0:T(8,128)(2,1)S(1)}, bf16[264,640]{1,0:T(8,128)(2,1)S(1)}, u32[]{:S(2)}, u32[]{:S(2)}) %collective-permute-start.11) | collective-permute-done | bytes 337952 | tf_op jit(solution)/shard_map/ppermute | solution.py:49
  33.3 0.9 %token_products.5 = (bf16[1,16,3168]{2,1,0:T(8,128)(2,1)S(1)}, bf16[1,16,3168]{2,1,0:T(8,128)(2,1)S(1)}, bf16[1,16,3168]{2,1,0:T(8,128)(2,1)S(1)}, bf16[1,16,3168]{2,1,0:T(8,128)(2,1)S(1)}) custom-call(bf16[192,640]{1,0:T(8,128)(2,1)S(1)} %bitcast.18, bf16[192,640]{1,0:T(8,128)(2,1)S(1)} %collective-permute-done.refs_1_, ...), custom_call_target="tpu_custom_call" | custom-call | flops 2595225600 | bytes 1726464 | tf_op jit(solution)/shard_map/token_products/pallas_call | solution.py:85
  34.2 0.0 copy-start.2
  34.2 1.6 %collective-permute-start.12 = (bf16[1,16,3168]{2,1,0:T(8,128)(2,1)S(1)}, bf16[1,16,3168]{2,1,0:T(8,128)(2,1)S(1)}, u32[]{:S(2)}, u32[]{:S(2)}) collective-permute-start(bf16[1,16,3168]{2,1,0:T(8,128)(2,1)S(1)} %get-tuple-element.52), channel_id=1, source_target_pairs={{0,2},{2,0},{4,6},{6,4},{8,10},{10,8},{12,14},{14,12},{16,18},{18,... | collective-permute-start | bytes 304136 | tf_op jit(solution)/shard_map/ppermute | solution.py:59
  35.8 0.4 collective-permute-start.13
  36.2 0.0 collective-permute-done.8.refs_3_
  36.2 1.6 %collective-permute-start.14 = (bf16[1,16,3168]{2,1,0:T(8,128)(2,1)S(1)}, bf16[1,16,3168]{2,1,0:T(8,128)(2,1)S(1)}, u32[]{:S(2)}, u32[]{:S(2)}) collective-permute-start(bf16[1,16,3168]{2,1,0:T(8,128)(2,1)S(1)} %get-tuple-element.54), channel_id=1, source_target_pairs={{0,6},{2,4},{4,2},{6,0},{8,14},{10,12},{12,10},{14,8},{16,22},{18,... | collective-permute-start | bytes 304136 | tf_op jit(solution)/shard_map/ppermute | solution.py:59
  37.8 0.0 collective-permute-done.9.refs_5_
  37.8 1.4 %collective-permute-done.10.refs_7_ = bf16[2,16,3168]{2,1,0:T(8,128)(2,1)S(1)} collective-permute-done((bf16[2,16,3168]{2,1,0:T(8,128)(2,1)S(1)}, bf16[2,16,3168]{2,1,0:T(8,128)(2,1)S(1)}, u32[]{:S(2)}, u32[]{:S(2)}) %collective-permute-start.10) | collective-permute-done | bytes 202784 | tf_op jit(solution)/shard_map/ppermute | solution.py:59
  39.2 0.0 copy-done.5
  39.2 1.8 %placed_early.1 = (bf16[192,4224]{1,0:T(8,128)(2,1)S(1)}, f32[192,128]{1,0:T(8,128)S(1)}, f32[8,4224]{1,0:T(8,128)S(1)}) custom-call(f32[192,128]{1,0:T(8,128)S(1)} %live_inverse.1.inverse_ref, bf16[192,4224]{1,0:T(8,128)(2,1)S(1)} %bitcast.7, f32[1,4224]{1,0:T(1,128)S(1)} %copy-done.5, bf16[1,16,3168]{2,1,0:T(8,128)(2,1)S(1)} %get-tuple-element.40.refs_0_, ...), custom_call_target="tpu_custom_call" | custom-call | flops 6488064 | bytes 6488064 | tf_op jit(solution)/shard_map/placed_early/pallas_call | solution.py:219
  41.0 0.0 collective-permute-done.12.refs_1_
  41.1 1.4 %collective-permute-done.13.refs_2_ = bf16[1,16,3168]{2,1,0:T(8,128)(2,1)S(1)} collective-permute-done((bf16[1,16,3168]{2,1,0:T(8,128)(2,1)S(1)}, bf16[1,16,3168]{2,1,0:T(8,128)(2,1)S(1)}, u32[]{:S(2)}, u32[]{:S(2)}) %collective-permute-start.13) | collective-permute-done | bytes 101408 | tf_op jit(solution)/shard_map/ppermute | solution.py:59
  42.4 0.0 collective-permute-done.14.refs_3_
  42.4 2.8 %norm_backward.1 = (bf16[192,4224]{1,0:T(8,128)(2,1)}, f32[192,4224]{1,0:T(8,128)S(1)}, f32[16,1,264]{2,1,0:T(1,128)}) custom-call(bf16[192,4224]{1,0:T(8,128)(2,1)S(1)} %get-tuple-element.48.early_ref, f32[192,128]{1,0:T(8,128)S(1)} %get-tuple-element.49.early_pulls, f32[8,4224]{1,0:T(8,128)S(1)} %get-tuple-element.50.early_gains, ...), custom_call_target="tpu_custom_call" | custom-call | flops 12976128 | bytes 9732096 | tf_op jit(solution)/shard_map/norm_backward/pallas_call | solution.py:313
  45.3 0.1 collective-permute-start.15
  45.3 3.8 %all-to-all-start = ((f32[16,1,264]{2,1,0:T(1,128)}), f32[16,1,264]{2,1,0:T(1,128)S(1)}, u32[]{:S(2)}, u32[]{:S(2)}) async-start(f32[16,1,264]{2,1,0:T(1,128)} %get-tuple-element.55), calls=%async_computation | async-start | bytes 49152 | tf_op jit(solution)/shard_map/all_to_all | solution.py:476
  49.1 0.0 collective-permute-done.15.incoming_ref
  49.1 2.3 %hand_on.1 = bf16[192,4224]{1,0:T(8,128)(2,1)} custom-call(bf16[192,4224]{1,0:T(8,128)(2,1)} %collective-permute-done.15.incoming_ref, f32[192,4224]{1,0:T(8,128)S(1)} %get-tuple-element.57.local_ref, bf16[192,4224]{1,0:T(8,128)(2,1)} %get-tuple-element.56.result_ref), custom_call_target="tpu_custom_call" | custom-call | tf_op jit(solution)/shard_map/hand_on/pallas_call | solution.py:370
  51.5 5.0 %all-to-all-done.parts_ref = f32[16,1,264]{2,1,0:T(1,128)S(1)} async-done(((f32[16,1,264]{2,1,0:T(1,128)}), f32[16,1,264]{2,1,0:T(1,128)S(1)}, u32[]{:S(2)}, u32[]{:S(2)}) %all-to-all-start) | async-done | bytes 16928 | tf_op jit(solution)/shard_map/all_to_all | solution.py:476
  56.5 0.6 %sum_scaled.1 = f32[1,264]{1,0:T(1,128)} custom-call(f32[16,1,264]{2,1,0:T(1,128)S(1)} %all-to-all-done.parts_ref), custom_call_target="tpu_custom_call" | custom-call | flops 4224 | bytes 16896 | tf_op jit(solution)/shard_map/sum_scaled/pallas_call | solution.py:396
  (8 shorter events, 0.0 us)
Async XLA Ops:
  0.6 23.8 %collective-permute-start.4 = (bf16[264,640]{1,0:T(8,128)(2,1)}, bf16[264,640]{1,0:T(8,128)(2,1)S(1)}, u32[]{:S(2)}, u32[]{:S(2)}) collective-permute-start(bf16[264,640]{1,0:T(8,128)(2,1)} %bitcast.10), channel_id=1, source_target_pairs={{0,16},{2,18},{4,20},{6,22},{8,24},{10,26},{12,28},{14,30},{16,0},... | collective-permute-start | bytes 1013768 | tf_op jit(solution)/shard_map/ppermute | solution.py:49
  4.7 20.1 %collective-permute-start.3 = (bf16[264,640]{1,0:T(8,128)(2,1)}, bf16[264,640]{1,0:T(8,128)(2,1)S(1)}, u32[]{:S(2)}, u32[]{:S(2)}) collective-permute-start(bf16[264,640]{1,0:T(8,128)(2,1)} %bitcast.11), channel_id=1, source_target_pairs={{0,8},{2,10},{4,12},{6,14},{8,0},{10,2},{12,4},{14,6},{16,24},{18,... | collective-permute-start | bytes 1013768 | tf_op jit(solution)/shard_map/ppermute | solution.py:49
  6.3 10.0 %collective-permute-start.2 = (bf16[192,640]{1,0:T(8,128)(2,1)}, bf16[192,640]{1,0:T(8,128)(2,1)S(1)}, u32[]{:S(2)}, u32[]{:S(2)}) collective-permute-start(bf16[192,640]{1,0:T(8,128)(2,1)} %bitcast.13), channel_id=1, source_target_pairs={{0,6},{2,4},{4,2},{6,0},{8,14},{10,12},{12,10},{14,8},{16,22},{18,... | collective-permute-start | bytes 737288 | tf_op jit(solution)/shard_map/ppermute | solution.py:59
  8.8 11.1 %collective-permute-start.1 = (bf16[192,640]{1,0:T(8,128)(2,1)}, bf16[192,640]{1,0:T(8,128)(2,1)S(1)}, u32[]{:S(2)}, u32[]{:S(2)}) collective-permute-start(bf16[192,640]{1,0:T(8,128)(2,1)} %bitcast.14), channel_id=1, source_target_pairs={{0,4},{2,6},{4,0},{6,2},{8,12},{10,14},{12,8},{14,10},{16,20},{18,... | collective-permute-start | bytes 737288 | tf_op jit(solution)/shard_map/ppermute | solution.py:59
  9.3 10.7 %collective-permute-start = (bf16[192,640]{1,0:T(8,128)(2,1)}, bf16[192,640]{1,0:T(8,128)(2,1)S(1)}, u32[]{:S(2)}, u32[]{:S(2)}) collective-permute-start(bf16[192,640]{1,0:T(8,128)(2,1)} %bitcast.15), channel_id=1, source_target_pairs={{0,2},{2,0},{4,6},{6,4},{8,10},{10,8},{12,14},{14,12},{16,18},{18,... | collective-permute-start | bytes 737288 | tf_op jit(solution)/shard_map/ppermute | solution.py:59
  9.8 1.4 %copy-start = (bf16[1,1,4,48,4224]{4,3,2,1,0:T(8,128)(2,1)S(1)}, bf16[1,1,4,48,4224]{4,3,2,1,0:T(8,128)(2,1)}, u32[]{:S(2)}) copy-start(bf16[1,1,4,48,4224]{4,3,2,1,0:T(8,128)(2,1)} %param.6) | copy-start | bytes 4866052
  11.2 0.7 %copy-start.6 = (s32[1,4]{1,0:T(1,128)S(1)}, s32[1,4]{1,0:T(1,128)}, u32[]{:S(2)}) copy-start(s32[1,4]{1,0:T(1,128)} %param.11) | copy-start | bytes 52
  11.9 8.0 %copy-start.3 = (bf16[1,264,640]{2,1,0:T(8,128)(2,1)S(1)}, bf16[1,264,640]{2,1,0:T(8,128)(2,1)}, u32[]{:S(2)}) copy-start(bf16[1,264,640]{2,1,0:T(8,128)(2,1)} %param.10) | copy-start | bytes 1013764
  11.9 8.0 %copy-start.4 = (bf16[1,1,4,48,640]{4,3,2,1,0:T(8,128)(2,1)S(1)}, bf16[1,1,4,48,640]{4,3,2,1,0:T(8,128)(2,1)}, u32[]{:S(2)}) copy-start(bf16[1,1,4,48,640]{4,3,2,1,0:T(8,128)(2,1)} %param.7) | copy-start | bytes 737284
  20.8 7.2 %collective-permute-start.5 = (bf16[1,16,3168]{2,1,0:T(8,128)(2,1)S(1)}, bf16[1,16,3168]{2,1,0:T(8,128)(2,1)S(1)}, u32[]{:S(2)}, u32[]{:S(2)}) collective-permute-start(bf16[1,16,3168]{2,1,0:T(8,128)(2,1)S(1)} %get-tuple-element.37), channel_id=1, source_target_pairs={{0,2},{2,0},{4,6},{6,4},{8,10},{10,8},{12,14},{14,12},{16,18},{18,... | collective-permute-start | bytes 304136 | tf_op jit(solution)/shard_map/ppermute | solution.py:59
  22.4 6.7 %collective-permute-start.6 = (bf16[1,16,3168]{2,1,0:T(8,128)(2,1)S(1)}, bf16[1,16,3168]{2,1,0:T(8,128)(2,1)S(1)}, u32[]{:S(2)}, u32[]{:S(2)}) collective-permute-start(bf16[1,16,3168]{2,1,0:T(8,128)(2,1)S(1)} %get-tuple-element.38), channel_id=1, source_target_pairs={{0,4},{2,6},{4,0},{6,2},{8,12},{10,14},{12,8},{14,10},{16,20},{18,... | collective-permute-start | bytes 304136 | tf_op jit(solution)/shard_map/ppermute | solution.py:59
  23.1 6.0 %collective-permute-start.7 = (bf16[1,16,3168]{2,1,0:T(8,128)(2,1)S(1)}, bf16[1,16,3168]{2,1,0:T(8,128)(2,1)S(1)}, u32[]{:S(2)}, u32[]{:S(2)}) collective-permute-start(bf16[1,16,3168]{2,1,0:T(8,128)(2,1)S(1)} %get-tuple-element.39), channel_id=1, source_target_pairs={{0,6},{2,4},{4,2},{6,0},{8,14},{10,12},{12,10},{14,8},{16,22},{18,... | collective-permute-start | bytes 304136 | tf_op jit(solution)/shard_map/ppermute | solution.py:59
  24.4 8.9 %collective-permute-start.11 = (bf16[264,640]{1,0:T(8,128)(2,1)S(1)}, bf16[264,640]{1,0:T(8,128)(2,1)S(1)}, u32[]{:S(2)}, u32[]{:S(2)}) collective-permute-start(bf16[264,640]{1,0:T(8,128)(2,1)S(1)} %collective-permute-done.4.refs_5_), channel_id=1, source_target_pairs={{0,8},{2,10},{4,12},{6,14},{8,0},{10,2},{12,4},{14,6},{16,24},{18,... | collective-permute-start | bytes 1013768 | tf_op jit(solution)/shard_map/ppermute | solution.py:49
  26.5 9.7 %collective-permute-start.8 = (bf16[2,16,3168]{2,1,0:T(8,128)(2,1)S(1)}, bf16[2,16,3168]{2,1,0:T(8,128)(2,1)S(1)}, u32[]{:S(2)}, u32[]{:S(2)}) collective-permute-start(bf16[2,16,3168]{2,1,0:T(8,128)(2,1)S(1)} %get-tuple-element.43), channel_id=1, source_target_pairs={{0,2},{2,0},{4,6},{6,4},{8,10},{10,8},{12,14},{14,12},{16,18},{18,... | collective-permute-start | bytes 608264 | tf_op jit(solution)/shard_map/ppermute | solution.py:59
  28.0 9.8 %collective-permute-start.9 = (bf16[2,16,3168]{2,1,0:T(8,128)(2,1)S(1)}, bf16[2,16,3168]{2,1,0:T(8,128)(2,1)S(1)}, u32[]{:S(2)}, u32[]{:S(2)}) collective-permute-start(bf16[2,16,3168]{2,1,0:T(8,128)(2,1)S(1)} %get-tuple-element.45), channel_id=1, source_target_pairs={{0,4},{2,6},{4,0},{6,2},{8,12},{10,14},{12,8},{14,10},{16,20},{18,... | collective-permute-start | bytes 608264 | tf_op jit(solution)/shard_map/ppermute | solution.py:59
  29.1 10.1 %copy-start.1 = (bf16[1,1,4,48,4224]{4,3,2,1,0:T(8,128)(2,1)S(1)}, bf16[1,1,4,48,4224]{4,3,2,1,0:T(8,128)(2,1)}, u32[]{:S(2)}) copy-start(bf16[1,1,4,48,4224]{4,3,2,1,0:T(8,128)(2,1)} %param.6) | copy-start | bytes 4866052
  29.1 10.1 %copy-start.5 = (f32[1,4224]{1,0:T(1,128)S(1)}, f32[1,4224]{1,0:T(1,128)}, u32[]{:S(2)}) copy-start(f32[1,4224]{1,0:T(1,128)} %gain_ref.3) | copy-start | bytes 50692
  29.1 10.1 %collective-permute-start.10 = (bf16[2,16,3168]{2,1,0:T(8,128)(2,1)S(1)}, bf16[2,16,3168]{2,1,0:T(8,128)(2,1)S(1)}, u32[]{:S(2)}, u32[]{:S(2)}) collective-permute-start(bf16[2,16,3168]{2,1,0:T(8,128)(2,1)S(1)} %get-tuple-element.47), channel_id=1, source_target_pairs={{0,6},{2,4},{4,2},{6,0},{8,14},{10,12},{12,10},{14,8},{16,22},{18,... | collective-permute-start | bytes 608264 | tf_op jit(solution)/shard_map/ppermute | solution.py:59
  34.2 8.2 %copy-start.2 = (bf16[1,4,48,4224]{3,2,1,0:T(8,128)(2,1)S(1)}, bf16[1,4,48,4224]{3,2,1,0:T(8,128)(2,1)}, u32[]{:S(2)}) copy-start(bf16[1,4,48,4224]{3,2,1,0:T(8,128)(2,1)} %param.8) | copy-start | bytes 4866052
  34.2 6.8 %collective-permute-start.12 = (bf16[1,16,3168]{2,1,0:T(8,128)(2,1)S(1)}, bf16[1,16,3168]{2,1,0:T(8,128)(2,1)S(1)}, u32[]{:S(2)}, u32[]{:S(2)}) collective-permute-start(bf16[1,16,3168]{2,1,0:T(8,128)(2,1)S(1)} %get-tuple-element.52), channel_id=1, source_target_pairs={{0,2},{2,0},{4,6},{6,4},{8,10},{10,8},{12,14},{14,12},{16,18},{18,... | collective-permute-start | bytes 304136 | tf_op jit(solution)/shard_map/ppermute | solution.py:59
  35.8 6.6 %collective-permute-start.13 = (bf16[1,16,3168]{2,1,0:T(8,128)(2,1)S(1)}, bf16[1,16,3168]{2,1,0:T(8,128)(2,1)S(1)}, u32[]{:S(2)}, u32[]{:S(2)}) collective-permute-start(bf16[1,16,3168]{2,1,0:T(8,128)(2,1)S(1)} %get-tuple-element.53), channel_id=1, source_target_pairs={{0,4},{2,6},{4,0},{6,2},{8,12},{10,14},{12,8},{14,10},{16,20},{18,... | collective-permute-start | bytes 304136 | tf_op jit(solution)/shard_map/ppermute | solution.py:59
  36.2 6.2 %collective-permute-start.14 = (bf16[1,16,3168]{2,1,0:T(8,128)(2,1)S(1)}, bf16[1,16,3168]{2,1,0:T(8,128)(2,1)S(1)}, u32[]{:S(2)}, u32[]{:S(2)}) collective-permute-start(bf16[1,16,3168]{2,1,0:T(8,128)(2,1)S(1)} %get-tuple-element.54), channel_id=1, source_target_pairs={{0,6},{2,4},{4,2},{6,0},{8,14},{10,12},{12,10},{14,8},{16,22},{18,... | collective-permute-start | bytes 304136 | tf_op jit(solution)/shard_map/ppermute | solution.py:59
  45.3 3.9 %collective-permute-start.15 = (bf16[192,4224]{1,0:T(8,128)(2,1)}, bf16[192,4224]{1,0:T(8,128)(2,1)}, u32[]{:S(2)}, u32[]{:S(2)}) collective-permute-start(bf16[192,4224]{1,0:T(8,128)(2,1)} %get-tuple-element.56.result_ref), channel_id=1, source_target_pairs={{1,0},{0,1},{3,2},{2,3},{5,4},{4,5},{7,6},{6,7},{9,8},{8,9},{11,10... | collective-permute-start | bytes 4866056 | tf_op jit(solution)/shard_map/ppermute | solution.py:473
  45.3 11.1 %all-to-all-start = ((f32[16,1,264]{2,1,0:T(1,128)}), f32[16,1,264]{2,1,0:T(1,128)S(1)}, u32[]{:S(2)}, u32[]{:S(2)}) async-start(f32[16,1,264]{2,1,0:T(1,128)} %get-tuple-element.55), calls=%async_computation | async-start | bytes 49152 | tf_op jit(solution)/shard_map/all_to_all | solution.py:476

commit v2 on v1

--- a/solution.py
+++ b/solution.py
@@ -233,7 +233,20 @@
 
 
 def finish_kernel(
-    line, plane, groups, fold, chunk, early_ref, early_pulls, early_gains, inverse_ref, act_ref, top_ref, gain_ref, *refs
+    line,
+    plane,
+    groups,
+    fold,
+    last,
+    chunk,
+    early_ref,
+    early_pulls,
+    early_gains,
+    inverse_ref,
+    act_ref,
+    top_ref,
+    gain_ref,
+    *refs,
 ):
     pieces = refs[:-10]
     passed_ref, local_ref, gain_out, held, back, gain_sum, pulls, passing, gain_blocks, copied = refs[-10:]
@@ -241,6 +254,7 @@
     width = features // (line * plane)
     late_steps = [step for group in groups for step in group]
     late_z = behind(lax.div(lax.axis_index("dp"), plane), late_steps[0], line)
+    is_last = lax.axis_index("section") == last
     back[...] = early_ref[...]
     place_pieces(line, plane, groups, fold, pieces, held, back)
     gain_sum[...] = early_gains[...]
@@ -272,13 +286,24 @@
         inverse = inverse_ref[part, :]
         pull = jnp.sum(pulls[part, :], axis=1, keepdims=True) / features
         pull = jnp.broadcast_to(pull, inverse.shape) * inverse * inverse * inverse
-        for left in range(0, features, 128):
-            cols = slice(left, left + 128)
+
+        def local_term(cols):
             scaled = back[part, cols].astype(jnp.float32) * gain_ref[:, cols]
-            local = inverse * scaled - act_ref[part, cols].astype(jnp.float32) * pull
-            local_ref[part, cols] = local
-            passing[part, cols] = (top_ref[part, cols].astype(jnp.float32) + local).astype(jnp.bfloat16)
-        out_copy(index).start()
+            return inverse * scaled - act_ref[part, cols].astype(jnp.float32) * pull
+
+        @pl.when(is_last)
+        def _():
+            for left in range(0, features, 128):
+                cols = slice(left, left + 128)
+                passing[part, cols] = (top_ref[part, cols].astype(jnp.float32) + local_term(cols)).astype(jnp.bfloat16)
+            out_copy(index).start()
+
+        @pl.when(jnp.logical_not(is_last))
+        def _():
+            for left in range(0, features, 128):
+                cols = slice(left, left + 128)
+                local_ref[part, cols] = local_term(cols)
+
         return 0
 
     lax.fori_loop(0, rows // chunk, one_chunk, 0)
@@ -287,12 +312,16 @@
         gain_blocks[block] = total[:, block * width : (block + 1) * width]
     gain_copy = pltpu.make_async_copy(gain_blocks, gain_out, copied.at[rows // chunk])
     gain_copy.start()
-    for index in range(rows // chunk):
-        out_copy(index).wait()
+
+    @pl.when(is_last)
+    def _():
+        for index in range(rows // chunk):
+            out_copy(index).wait()
+
     gain_copy.wait()
 
 
-def finish(line, plane, groups, fold, early, inverse, act, top, gain, pieces):
+def finish(line, plane, groups, fold, last, early, inverse, act, top, gain, pieces):
     rows, features = act.shape
     blocks = line * plane
     vmem = pl.BlockSpec(memory_space=pltpu.VMEM)
@@ -311,7 +340,7 @@
     ]
     chunk = math.gcd(rows, 32)
     return pl.pallas_call(
-        functools.partial(finish_kernel, line, plane, groups, fold, chunk),
+        functools.partial(finish_kernel, line, plane, groups, fold, last, chunk),
         out_shape=outs,
         in_specs=[vmem] * (4 + len(early) + len(pieces)),
         out_specs=[pl.BlockSpec(memory_space=pl.ANY), vmem, pl.BlockSpec(memory_space=pl.ANY)],
@@ -465,7 +494,7 @@
     early = placed_early(line, plane, groups[:split], fold, inverse, act, norm_gains, early)
     top = top_grad.reshape(rows, features)
     passed, local, gain_blocks = finish(
-        line, plane, groups[split:], fold, early, inverse, act, top, norm_gains, late
+        line, plane, groups[split:], fold, sections - 1, early, inverse, act, top, norm_gains, late
     )
 
     result = passed

time: 57.3 us -> 57.3 us (level)
  no operation moved by 1% of the time
where the time goes in v2:
time: 57.3 us; the launch traced here: 57 us
  starting transfers between devices  24.4 us (43%)
  waiting for transfers between devices  16.9 us (29%)
  Pallas kernels  12.9 us (23%)
  local copies, waits for them, and re-layouts  2.1 us (4%)
  between operations  0.73 us (1%)
    ppermute x12, starting transfers between devices, along_plane(): return lax.ppermute(value, 'dp', pairs)  14.4 us
    ppermute x12, waiting for transfers between devices, along_plane(): return lax.ppermute(value, 'dp', pairs)  9.17 us
    ppermute x3, starting transfers between devices, along_line(): return lax.ppermute(value, 'dp', pairs)  6.13 us
    all_to_all x1, waiting for transfers between devices, on_device(): lax.all_to_all(gain_blocks, 'dp', split_axis=0, concat_axis=0, tiled=True)  5.02 us
    all_to_all x1, starting transfers between devices, on_device(): lax.all_to_all(gain_blocks, 'dp', split_axis=0, concat_axis=0, tiled=True)  3.76 us
    pallas_call x3, Pallas kernels, products(): pl.pallas_call(functools.partial(product_kernel, len(tokens), count, fold...  3.43 us
    pallas_call x1, Pallas kernels, finish(): pl.pallas_call(functools.partial(finish_kernel, line, plane, groups, fold...  2.8 us
    ppermute x3, waiting for transfers between devices, along_line(): return lax.ppermute(value, 'dp', pairs)  2.66 us
  transfers between devices with their start and end apart: 17, of which 8 were waited for; matrix products, arithmetic and copies ran while one was open for 0% of the time, Pallas kernels for 17%

profile of v2, /device:TPU:0, one launch (start us, length us, event | category | flops | bytes accessed | tf_op | source)
XLA Modules:
  0.0 57.0 jit_solution(5879516442515063607)
XLA Ops:
  0.6 4.1 %collective-permute-start.4 = (bf16[264,640]{1,0:T(8,128)(2,1)}, bf16[264,640]{1,0:T(8,128)(2,1)S(1)}, u32[]{:S(2)}, u32[]{:S(2)}) collective-permute-start(bf16[264,640]{1,0:T(8,128)(2,1)} %bitcast.10), channel_id=1, source_target_pairs={{0,16},{2,18},{4,20},{6,22},{8,24},{10,26},{12,28},{14,30},{16,0},... | collective-permute-start | bytes 1013768 | tf_op jit(solution)/shard_map/ppermute | solution.py:49
  4.7 1.6 %collective-permute-start.3 = (bf16[264,640]{1,0:T(8,128)(2,1)}, bf16[264,640]{1,0:T(8,128)(2,1)S(1)}, u32[]{:S(2)}, u32[]{:S(2)}) collective-permute-start(bf16[264,640]{1,0:T(8,128)(2,1)} %bitcast.11), channel_id=1, source_target_pairs={{0,8},{2,10},{4,12},{6,14},{8,0},{10,2},{12,4},{14,6},{16,24},{18,... | collective-permute-start | bytes 1013768 | tf_op jit(solution)/shard_map/ppermute | solution.py:49
  6.3 2.4 %collective-permute-start.2 = (bf16[192,640]{1,0:T(8,128)(2,1)}, bf16[192,640]{1,0:T(8,128)(2,1)S(1)}, u32[]{:S(2)}, u32[]{:S(2)}) collective-permute-start(bf16[192,640]{1,0:T(8,128)(2,1)} %bitcast.13), channel_id=1, source_target_pairs={{0,6},{2,4},{4,2},{6,0},{8,14},{10,12},{12,10},{14,8},{16,22},{18,... | collective-permute-start | bytes 737288 | tf_op jit(solution)/shard_map/ppermute | solution.py:59
  8.8 0.5 collective-permute-start.1
  9.3 0.5 collective-permute-start
  9.8 1.4 %copy-done = bf16[1,1,4,48,4224]{4,3,2,1,0:T(8,128)(2,1)S(1)} copy-done((bf16[1,1,4,48,4224]{4,3,2,1,0:T(8,128)(2,1)S(1)}, bf16[1,1,4,48,4224]{4,3,2,1,0:T(8,128)(2,1)}, u32[]{:S(2)}) %copy-start) | copy-done | bytes 1622040
  11.2 0.7 %copy-done.6 = s32[1,4]{1,0:T(1,128)S(1)} copy-done((s32[1,4]{1,0:T(1,128)S(1)}, s32[1,4]{1,0:T(1,128)}, u32[]{:S(2)}) %copy-start.6) | copy-done | bytes 40
  11.9 2.0 %live_inverse.1.inverse_ref = f32[192,128]{1,0:T(8,128)S(1)} custom-call(s32[4]{0:T(128)S(1)} %bitcast.19, bf16[192,4224]{1,0:T(8,128)(2,1)S(1)} %bitcast.6), custom_call_target="tpu_custom_call" | custom-call | flops 1622016 | bytes 1622016 | tf_op jit(solution)/shard_map/live_inverse/pallas_call | solution.py:132
  13.9 2.5 %collective-permute-done.2.refs_3_ = bf16[192,640]{1,0:T(8,128)(2,1)S(1)} collective-permute-done((bf16[192,640]{1,0:T(8,128)(2,1)}, bf16[192,640]{1,0:T(8,128)(2,1)S(1)}, u32[]{:S(2)}, u32[]{:S(2)}) %collective-permute-start.2) | collective-permute-done | bytes 245792 | tf_op jit(solution)/shard_map/ppermute | solution.py:59
  16.4 3.5 %collective-permute-done.1.refs_2_ = bf16[192,640]{1,0:T(8,128)(2,1)S(1)} collective-permute-done((bf16[192,640]{1,0:T(8,128)(2,1)}, bf16[192,640]{1,0:T(8,128)(2,1)S(1)}, u32[]{:S(2)}, u32[]{:S(2)}) %collective-permute-start.1) | collective-permute-done | bytes 245792 | tf_op jit(solution)/shard_map/ppermute | solution.py:59
  19.8 0.1 collective-permute-done.refs_1_
  19.9 0.0 copy-done.3
  19.9 0.0 copy-done.4
  19.9 0.9 %token_products.3 = (bf16[1,16,3168]{2,1,0:T(8,128)(2,1)S(1)}, bf16[1,16,3168]{2,1,0:T(8,128)(2,1)S(1)}, bf16[1,16,3168]{2,1,0:T(8,128)(2,1)S(1)}, bf16[1,16,3168]{2,1,0:T(8,128)(2,1)S(1)}) custom-call(bf16[192,640]{1,0:T(8,128)(2,1)S(1)} %bitcast.16, bf16[192,640]{1,0:T(8,128)(2,1)S(1)} %collective-permute-done.refs_1_, ...), custom_call_target="tpu_custom_call" | custom-call | flops 259522560 | bytes 1726464 | tf_op jit(solution)/shard_map/token_products/pallas_call | solution.py:85
  20.8 1.6 %collective-permute-start.5 = (bf16[1,16,3168]{2,1,0:T(8,128)(2,1)S(1)}, bf16[1,16,3168]{2,1,0:T(8,128)(2,1)S(1)}, u32[]{:S(2)}, u32[]{:S(2)}) collective-permute-start(bf16[1,16,3168]{2,1,0:T(8,128)(2,1)S(1)} %get-tuple-element.37), channel_id=1, source_target_pairs={{0,2},{2,0},{4,6},{6,4},{8,10},{10,8},{12,14},{14,12},{16,18},{18,... | collective-permute-start | bytes 304136 | tf_op jit(solution)/shard_map/ppermute | solution.py:59
  22.4 0.7 %collective-permute-start.6 = (bf16[1,16,3168]{2,1,0:T(8,128)(2,1)S(1)}, bf16[1,16,3168]{2,1,0:T(8,128)(2,1)S(1)}, u32[]{:S(2)}, u32[]{:S(2)}) collective-permute-start(bf16[1,16,3168]{2,1,0:T(8,128)(2,1)S(1)} %get-tuple-element.38), channel_id=1, source_target_pairs={{0,4},{2,6},{4,0},{6,2},{8,12},{10,14},{12,8},{14,10},{16,20},{18,... | collective-permute-start | bytes 304136 | tf_op jit(solution)/shard_map/ppermute | solution.py:59
  23.1 1.3 %collective-permute-start.7 = (bf16[1,16,3168]{2,1,0:T(8,128)(2,1)S(1)}, bf16[1,16,3168]{2,1,0:T(8,128)(2,1)S(1)}, u32[]{:S(2)}, u32[]{:S(2)}) collective-permute-start(bf16[1,16,3168]{2,1,0:T(8,128)(2,1)S(1)} %get-tuple-element.39), channel_id=1, source_target_pairs={{0,6},{2,4},{4,2},{6,0},{8,14},{10,12},{12,10},{14,8},{16,22},{18,... | collective-permute-start | bytes 304136 | tf_op jit(solution)/shard_map/ppermute | solution.py:59
  24.4 0.0 collective-permute-done.4.refs_5_
  24.4 0.5 collective-permute-start.11
  24.8 0.0 collective-permute-done.3.refs_4_
  24.8 1.6 %token_products.4 = (bf16[2,16,3168]{2,1,0:T(8,128)(2,1)S(1)}, bf16[2,16,3168]{2,1,0:T(8,128)(2,1)S(1)}, bf16[2,16,3168]{2,1,0:T(8,128)(2,1)S(1)}, bf16[2,16,3168]{2,1,0:T(8,128)(2,1)S(1)}) custom-call(bf16[192,640]{1,0:T(8,128)(2,1)S(1)} %bitcast.17, bf16[192,640]{1,0:T(8,128)(2,1)S(1)} %collective-permute-done.refs_1_, ...), custom_call_target="tpu_custom_call" | custom-call | flops 5190451200 | bytes 2469888 | tf_op jit(solution)/shard_map/token_products/pallas_call | solution.py:85
  26.5 1.6 %collective-permute-start.8 = (bf16[2,16,3168]{2,1,0:T(8,128)(2,1)S(1)}, bf16[2,16,3168]{2,1,0:T(8,128)(2,1)S(1)}, u32[]{:S(2)}, u32[]{:S(2)}) collective-permute-start(bf16[2,16,3168]{2,1,0:T(8,128)(2,1)S(1)} %get-tuple-element.43), channel_id=1, source_target_pairs={{0,2},{2,0},{4,6},{6,4},{8,10},{10,8},{12,14},{14,12},{16,18},{18,... | collective-permute-start | bytes 608264 | tf_op jit(solution)/shard_map/ppermute | solution.py:59
  28.0 0.0 collective-permute-done.5.refs_2_
  28.0 0.7 %collective-permute-start.9 = (bf16[2,16,3168]{2,1,0:T(8,128)(2,1)S(1)}, bf16[2,16,3168]{2,1,0:T(8,128)(2,1)S(1)}, u32[]{:S(2)}, u32[]{:S(2)}) collective-permute-start(bf16[2,16,3168]{2,1,0:T(8,128)(2,1)S(1)} %get-tuple-element.45), channel_id=1, source_target_pairs={{0,4},{2,6},{4,0},{6,2},{8,12},{10,14},{12,8},{14,10},{16,20},{18,... | collective-permute-start | bytes 608264 | tf_op jit(solution)/shard_map/ppermute | solution.py:59
  28.8 0.3 collective-permute-done.6.refs_4_
  29.1 0.0 collective-permute-done.7.refs_6_
  29.1 1.6 %collective-permute-start.10 = (bf16[2,16,3168]{2,1,0:T(8,128)(2,1)S(1)}, bf16[2,16,3168]{2,1,0:T(8,128)(2,1)S(1)}, u32[]{:S(2)}, u32[]{:S(2)}) collective-permute-start(bf16[2,16,3168]{2,1,0:T(8,128)(2,1)S(1)} %get-tuple-element.47), channel_id=1, source_target_pairs={{0,6},{2,4},{4,2},{6,0},{8,14},{10,12},{12,10},{14,8},{16,22},{18,... | collective-permute-start | bytes 608264 | tf_op jit(solution)/shard_map/ppermute | solution.py:59
  30.7 2.7 %collective-permute-done.11.refs_4_ = bf16[264,640]{1,0:T(8,128)(2,1)S(1)} collective-permute-done((bf16[264,640]{1,0:T(8,128)(2,1)S(1)}, bf16[264,640]{1,0:T(8,128)(2,1)S(1)}, u32[]{:S(2)}, u32[]{:S(2)}) %collective-permute-start.11) | collective-permute-done | bytes 337952 | tf_op jit(solution)/shard_map/ppermute | solution.py:49
  33.3 0.9 %token_products.5 = (bf16[1,16,3168]{2,1,0:T(8,128)(2,1)S(1)}, bf16[1,16,3168]{2,1,0:T(8,128)(2,1)S(1)}, bf16[1,16,3168]{2,1,0:T(8,128)(2,1)S(1)}, bf16[1,16,3168]{2,1,0:T(8,128)(2,1)S(1)}) custom-call(bf16[192,640]{1,0:T(8,128)(2,1)S(1)} %bitcast.18, bf16[192,640]{1,0:T(8,128)(2,1)S(1)} %collective-permute-done.refs_1_, ...), custom_call_target="tpu_custom_call" | custom-call | flops 2595225600 | bytes 1726464 | tf_op jit(solution)/shard_map/token_products/pallas_call | solution.py:85
  34.2 0.0 copy-start.2
  34.2 1.6 %collective-permute-start.12 = (bf16[1,16,3168]{2,1,0:T(8,128)(2,1)S(1)}, bf16[1,16,3168]{2,1,0:T(8,128)(2,1)S(1)}, u32[]{:S(2)}, u32[]{:S(2)}) collective-permute-start(bf16[1,16,3168]{2,1,0:T(8,128)(2,1)S(1)} %get-tuple-element.52), channel_id=1, source_target_pairs={{0,2},{2,0},{4,6},{6,4},{8,10},{10,8},{12,14},{14,12},{16,18},{18,... | collective-permute-start | bytes 304136 | tf_op jit(solution)/shard_map/ppermute | solution.py:59
  35.8 0.4 collective-permute-start.13
  36.2 0.0 collective-permute-done.8.refs_3_
  36.2 1.6 %collective-permute-start.14 = (bf16[1,16,3168]{2,1,0:T(8,128)(2,1)S(1)}, bf16[1,16,3168]{2,1,0:T(8,128)(2,1)S(1)}, u32[]{:S(2)}, u32[]{:S(2)}) collective-permute-start(bf16[1,16,3168]{2,1,0:T(8,128)(2,1)S(1)} %get-tuple-element.54), channel_id=1, source_target_pairs={{0,6},{2,4},{4,2},{6,0},{8,14},{10,12},{12,10},{14,8},{16,22},{18,... | collective-permute-start | bytes 304136 | tf_op jit(solution)/shard_map/ppermute | solution.py:59
  37.8 0.0 collective-permute-done.9.refs_5_
  37.8 1.4 %collective-permute-done.10.refs_7_ = bf16[2,16,3168]{2,1,0:T(8,128)(2,1)S(1)} collective-permute-done((bf16[2,16,3168]{2,1,0:T(8,128)(2,1)S(1)}, bf16[2,16,3168]{2,1,0:T(8,128)(2,1)S(1)}, u32[]{:S(2)}, u32[]{:S(2)}) %collective-permute-start.10) | collective-permute-done | bytes 202784 | tf_op jit(solution)/shard_map/ppermute | solution.py:59
  39.2 0.0 copy-done.5
  39.2 1.8 %placed_early.1 = (bf16[192,4224]{1,0:T(8,128)(2,1)S(1)}, f32[192,128]{1,0:T(8,128)S(1)}, f32[8,4224]{1,0:T(8,128)S(1)}) custom-call(f32[192,128]{1,0:T(8,128)S(1)} %live_inverse.1.inverse_ref, bf16[192,4224]{1,0:T(8,128)(2,1)S(1)} %bitcast.7, f32[1,4224]{1,0:T(1,128)S(1)} %copy-done.5, bf16[1,16,3168]{2,1,0:T(8,128)(2,1)S(1)} %get-tuple-element.40.refs_0_, ...), custom_call_target="tpu_custom_call" | custom-call | flops 6488064 | bytes 6488064 | tf_op jit(solution)/shard_map/placed_early/pallas_call | solution.py:219
  41.0 0.0 collective-permute-done.12.refs_1_
  41.1 1.4 %collective-permute-done.13.refs_2_ = bf16[1,16,3168]{2,1,0:T(8,128)(2,1)S(1)} collective-permute-done((bf16[1,16,3168]{2,1,0:T(8,128)(2,1)S(1)}, bf16[1,16,3168]{2,1,0:T(8,128)(2,1)S(1)}, u32[]{:S(2)}, u32[]{:S(2)}) %collective-permute-start.13) | collective-permute-done | bytes 101408 | tf_op jit(solution)/shard_map/ppermute | solution.py:59
  42.4 0.0 collective-permute-done.14.refs_3_
  42.4 2.8 %norm_backward.1 = (bf16[192,4224]{1,0:T(8,128)(2,1)}, f32[192,4224]{1,0:T(8,128)S(1)}, f32[16,1,264]{2,1,0:T(1,128)}) custom-call(bf16[192,4224]{1,0:T(8,128)(2,1)S(1)} %get-tuple-element.48.early_ref, f32[192,128]{1,0:T(8,128)S(1)} %get-tuple-element.49.early_pulls, f32[8,4224]{1,0:T(8,128)S(1)} %get-tuple-element.50.early_gains, ...), custom_call_target="tpu_custom_call" | custom-call | flops 12976128 | bytes 9732096 | tf_op jit(solution)/shard_map/norm_backward/pallas_call | solution.py:342
  45.2 0.1 collective-permute-start.15
  45.3 3.8 %all-to-all-start = ((f32[16,1,264]{2,1,0:T(1,128)}), f32[16,1,264]{2,1,0:T(1,128)S(1)}, u32[]{:S(2)}, u32[]{:S(2)}) async-start(f32[16,1,264]{2,1,0:T(1,128)} %get-tuple-element.55), calls=%async_computation | async-start | bytes 49152 | tf_op jit(solution)/shard_map/all_to_all | solution.py:505
  49.1 0.0 collective-permute-done.15.incoming_ref
  49.1 2.3 %hand_on.1 = bf16[192,4224]{1,0:T(8,128)(2,1)} custom-call(bf16[192,4224]{1,0:T(8,128)(2,1)} %collective-permute-done.15.incoming_ref, f32[192,4224]{1,0:T(8,128)S(1)} %get-tuple-element.57.local_ref, bf16[192,4224]{1,0:T(8,128)(2,1)} %get-tuple-element.56.result_ref), custom_call_target="tpu_custom_call" | custom-call | tf_op jit(solution)/shard_map/hand_on/pallas_call | solution.py:399
  51.4 5.0 %all-to-all-done.parts_ref = f32[16,1,264]{2,1,0:T(1,128)S(1)} async-done(((f32[16,1,264]{2,1,0:T(1,128)}), f32[16,1,264]{2,1,0:T(1,128)S(1)}, u32[]{:S(2)}, u32[]{:S(2)}) %all-to-all-start) | async-done | bytes 16928 | tf_op jit(solution)/shard_map/all_to_all | solution.py:505
  56.4 0.6 %sum_scaled.1 = f32[1,264]{1,0:T(1,128)} custom-call(f32[16,1,264]{2,1,0:T(1,128)S(1)} %all-to-all-done.parts_ref), custom_call_target="tpu_custom_call" | custom-call | flops 4224 | bytes 16896 | tf_op jit(solution)/shard_map/sum_scaled/pallas_call | solution.py:425
  (8 shorter events, 0.0 us)
Async XLA Ops:
  0.6 23.8 %collective-permute-start.4 = (bf16[264,640]{1,0:T(8,128)(2,1)}, bf16[264,640]{1,0:T(8,128)(2,1)S(1)}, u32[]{:S(2)}, u32[]{:S(2)}) collective-permute-start(bf16[264,640]{1,0:T(8,128)(2,1)} %bitcast.10), channel_id=1, source_target_pairs={{0,16},{2,18},{4,20},{6,22},{8,24},{10,26},{12,28},{14,30},{16,0},... | collective-permute-start | bytes 1013768 | tf_op jit(solution)/shard_map/ppermute | solution.py:49
  4.7 20.1 %collective-permute-start.3 = (bf16[264,640]{1,0:T(8,128)(2,1)}, bf16[264,640]{1,0:T(8,128)(2,1)S(1)}, u32[]{:S(2)}, u32[]{:S(2)}) collective-permute-start(bf16[264,640]{1,0:T(8,128)(2,1)} %bitcast.11), channel_id=1, source_target_pairs={{0,8},{2,10},{4,12},{6,14},{8,0},{10,2},{12,4},{14,6},{16,24},{18,... | collective-permute-start | bytes 1013768 | tf_op jit(solution)/shard_map/ppermute | solution.py:49
  6.3 10.0 %collective-permute-start.2 = (bf16[192,640]{1,0:T(8,128)(2,1)}, bf16[192,640]{1,0:T(8,128)(2,1)S(1)}, u32[]{:S(2)}, u32[]{:S(2)}) collective-permute-start(bf16[192,640]{1,0:T(8,128)(2,1)} %bitcast.13), channel_id=1, source_target_pairs={{0,6},{2,4},{4,2},{6,0},{8,14},{10,12},{12,10},{14,8},{16,22},{18,... | collective-permute-start | bytes 737288 | tf_op jit(solution)/shard_map/ppermute | solution.py:59
  8.8 11.1 %collective-permute-start.1 = (bf16[192,640]{1,0:T(8,128)(2,1)}, bf16[192,640]{1,0:T(8,128)(2,1)S(1)}, u32[]{:S(2)}, u32[]{:S(2)}) collective-permute-start(bf16[192,640]{1,0:T(8,128)(2,1)} %bitcast.14), channel_id=1, source_target_pairs={{0,4},{2,6},{4,0},{6,2},{8,12},{10,14},{12,8},{14,10},{16,20},{18,... | collective-permute-start | bytes 737288 | tf_op jit(solution)/shard_map/ppermute | solution.py:59
  9.3 10.7 %collective-permute-start = (bf16[192,640]{1,0:T(8,128)(2,1)}, bf16[192,640]{1,0:T(8,128)(2,1)S(1)}, u32[]{:S(2)}, u32[]{:S(2)}) collective-permute-start(bf16[192,640]{1,0:T(8,128)(2,1)} %bitcast.15), channel_id=1, source_target_pairs={{0,2},{2,0},{4,6},{6,4},{8,10},{10,8},{12,14},{14,12},{16,18},{18,... | collective-permute-start | bytes 737288 | tf_op jit(solution)/shard_map/ppermute | solution.py:59
  9.8 1.4 %copy-start = (bf16[1,1,4,48,4224]{4,3,2,1,0:T(8,128)(2,1)S(1)}, bf16[1,1,4,48,4224]{4,3,2,1,0:T(8,128)(2,1)}, u32[]{:S(2)}) copy-start(bf16[1,1,4,48,4224]{4,3,2,1,0:T(8,128)(2,1)} %param.6) | copy-start | bytes 4866052
  11.2 0.7 %copy-start.6 = (s32[1,4]{1,0:T(1,128)S(1)}, s32[1,4]{1,0:T(1,128)}, u32[]{:S(2)}) copy-start(s32[1,4]{1,0:T(1,128)} %param.11) | copy-start | bytes 52
  11.9 8.0 %copy-start.3 = (bf16[1,264,640]{2,1,0:T(8,128)(2,1)S(1)}, bf16[1,264,640]{2,1,0:T(8,128)(2,1)}, u32[]{:S(2)}) copy-start(bf16[1,264,640]{2,1,0:T(8,128)(2,1)} %param.10) | copy-start | bytes 1013764
  11.9 8.0 %copy-start.4 = (bf16[1,1,4,48,640]{4,3,2,1,0:T(8,128)(2,1)S(1)}, bf16[1,1,4,48,640]{4,3,2,1,0:T(8,128)(2,1)}, u32[]{:S(2)}) copy-start(bf16[1,1,4,48,640]{4,3,2,1,0:T(8,128)(2,1)} %param.7) | copy-start | bytes 737284
  20.8 7.2 %collective-permute-start.5 = (bf16[1,16,3168]{2,1,0:T(8,128)(2,1)S(1)}, bf16[1,16,3168]{2,1,0:T(8,128)(2,1)S(1)}, u32[]{:S(2)}, u32[]{:S(2)}) collective-permute-start(bf16[1,16,3168]{2,1,0:T(8,128)(2,1)S(1)} %get-tuple-element.37), channel_id=1, source_target_pairs={{0,2},{2,0},{4,6},{6,4},{8,10},{10,8},{12,14},{14,12},{16,18},{18,... | collective-permute-start | bytes 304136 | tf_op jit(solution)/shard_map/ppermute | solution.py:59
  22.4 6.7 %collective-permute-start.6 = (bf16[1,16,3168]{2,1,0:T(8,128)(2,1)S(1)}, bf16[1,16,3168]{2,1,0:T(8,128)(2,1)S(1)}, u32[]{:S(2)}, u32[]{:S(2)}) collective-permute-start(bf16[1,16,3168]{2,1,0:T(8,128)(2,1)S(1)} %get-tuple-element.38), channel_id=1, source_target_pairs={{0,4},{2,6},{4,0},{6,2},{8,12},{10,14},{12,8},{14,10},{16,20},{18,... | collective-permute-start | bytes 304136 | tf_op jit(solution)/shard_map/ppermute | solution.py:59
  23.1 6.0 %collective-permute-start.7 = (bf16[1,16,3168]{2,1,0:T(8,128)(2,1)S(1)}, bf16[1,16,3168]{2,1,0:T(8,128)(2,1)S(1)}, u32[]{:S(2)}, u32[]{:S(2)}) collective-permute-start(bf16[1,16,3168]{2,1,0:T(8,128)(2,1)S(1)} %get-tuple-element.39), channel_id=1, source_target_pairs={{0,6},{2,4},{4,2},{6,0},{8,14},{10,12},{12,10},{14,8},{16,22},{18,... | collective-permute-start | bytes 304136 | tf_op jit(solution)/shard_map/ppermute | solution.py:59
  24.4 8.9 %collective-permute-start.11 = (bf16[264,640]{1,0:T(8,128)(2,1)S(1)}, bf16[264,640]{1,0:T(8,128)(2,1)S(1)}, u32[]{:S(2)}, u32[]{:S(2)}) collective-permute-start(bf16[264,640]{1,0:T(8,128)(2,1)S(1)} %collective-permute-done.4.refs_5_), channel_id=1, source_target_pairs={{0,8},{2,10},{4,12},{6,14},{8,0},{10,2},{12,4},{14,6},{16,24},{18,... | collective-permute-start | bytes 1013768 | tf_op jit(solution)/shard_map/ppermute | solution.py:49
  26.5 9.7 %collective-permute-start.8 = (bf16[2,16,3168]{2,1,0:T(8,128)(2,1)S(1)}, bf16[2,16,3168]{2,1,0:T(8,128)(2,1)S(1)}, u32[]{:S(2)}, u32[]{:S(2)}) collective-permute-start(bf16[2,16,3168]{2,1,0:T(8,128)(2,1)S(1)} %get-tuple-element.43), channel_id=1, source_target_pairs={{0,2},{2,0},{4,6},{6,4},{8,10},{10,8},{12,14},{14,12},{16,18},{18,... | collective-permute-start | bytes 608264 | tf_op jit(solution)/shard_map/ppermute | solution.py:59
  28.0 9.8 %collective-permute-start.9 = (bf16[2,16,3168]{2,1,0:T(8,128)(2,1)S(1)}, bf16[2,16,3168]{2,1,0:T(8,128)(2,1)S(1)}, u32[]{:S(2)}, u32[]{:S(2)}) collective-permute-start(bf16[2,16,3168]{2,1,0:T(8,128)(2,1)S(1)} %get-tuple-element.45), channel_id=1, source_target_pairs={{0,4},{2,6},{4,0},{6,2},{8,12},{10,14},{12,8},{14,10},{16,20},{18,... | collective-permute-start | bytes 608264 | tf_op jit(solution)/shard_map/ppermute | solution.py:59
  29.1 10.1 %copy-start.1 = (bf16[1,1,4,48,4224]{4,3,2,1,0:T(8,128)(2,1)S(1)}, bf16[1,1,4,48,4224]{4,3,2,1,0:T(8,128)(2,1)}, u32[]{:S(2)}) copy-start(bf16[1,1,4,48,4224]{4,3,2,1,0:T(8,128)(2,1)} %param.6) | copy-start | bytes 4866052
  29.1 10.1 %copy-start.5 = (f32[1,4224]{1,0:T(1,128)S(1)}, f32[1,4224]{1,0:T(1,128)}, u32[]{:S(2)}) copy-start(f32[1,4224]{1,0:T(1,128)} %gain_ref.3) | copy-start | bytes 50692
  29.1 10.1 %collective-permute-start.10 = (bf16[2,16,3168]{2,1,0:T(8,128)(2,1)S(1)}, bf16[2,16,3168]{2,1,0:T(8,128)(2,1)S(1)}, u32[]{:S(2)}, u32[]{:S(2)}) collective-permute-start(bf16[2,16,3168]{2,1,0:T(8,128)(2,1)S(1)} %get-tuple-element.47), channel_id=1, source_target_pairs={{0,6},{2,4},{4,2},{6,0},{8,14},{10,12},{12,10},{14,8},{16,22},{18,... | collective-permute-start | bytes 608264 | tf_op jit(solution)/shard_map/ppermute | solution.py:59
  34.2 8.2 %copy-start.2 = (bf16[1,4,48,4224]{3,2,1,0:T(8,128)(2,1)S(1)}, bf16[1,4,48,4224]{3,2,1,0:T(8,128)(2,1)}, u32[]{:S(2)}) copy-start(bf16[1,4,48,4224]{3,2,1,0:T(8,128)(2,1)} %param.8) | copy-start | bytes 4866052
  34.2 6.8 %collective-permute-start.12 = (bf16[1,16,3168]{2,1,0:T(8,128)(2,1)S(1)}, bf16[1,16,3168]{2,1,0:T(8,128)(2,1)S(1)}, u32[]{:S(2)}, u32[]{:S(2)}) collective-permute-start(bf16[1,16,3168]{2,1,0:T(8,128)(2,1)S(1)} %get-tuple-element.52), channel_id=1, source_target_pairs={{0,2},{2,0},{4,6},{6,4},{8,10},{10,8},{12,14},{14,12},{16,18},{18,... | collective-permute-start | bytes 304136 | tf_op jit(solution)/shard_map/ppermute | solution.py:59
  35.8 6.6 %collective-permute-start.13 = (bf16[1,16,3168]{2,1,0:T(8,128)(2,1)S(1)}, bf16[1,16,3168]{2,1,0:T(8,128)(2,1)S(1)}, u32[]{:S(2)}, u32[]{:S(2)}) collective-permute-start(bf16[1,16,3168]{2,1,0:T(8,128)(2,1)S(1)} %get-tuple-element.53), channel_id=1, source_target_pairs={{0,4},{2,6},{4,0},{6,2},{8,12},{10,14},{12,8},{14,10},{16,20},{18,... | collective-permute-start | bytes 304136 | tf_op jit(solution)/shard_map/ppermute | solution.py:59
  36.2 6.2 %collective-permute-start.14 = (bf16[1,16,3168]{2,1,0:T(8,128)(2,1)S(1)}, bf16[1,16,3168]{2,1,0:T(8,128)(2,1)S(1)}, u32[]{:S(2)}, u32[]{:S(2)}) collective-permute-start(bf16[1,16,3168]{2,1,0:T(8,128)(2,1)S(1)} %get-tuple-element.54), channel_id=1, source_target_pairs={{0,6},{2,4},{4,2},{6,0},{8,14},{10,12},{12,10},{14,8},{16,22},{18,... | collective-permute-start | bytes 304136 | tf_op jit(solution)/shard_map/ppermute | solution.py:59
  45.2 3.9 %collective-permute-start.15 = (bf16[192,4224]{1,0:T(8,128)(2,1)}, bf16[192,4224]{1,0:T(8,128)(2,1)}, u32[]{:S(2)}, u32[]{:S(2)}) collective-permute-start(bf16[192,4224]{1,0:T(8,128)(2,1)} %get-tuple-element.56.result_ref), channel_id=1, source_target_pairs={{1,0},{0,1},{3,2},{2,3},{5,4},{4,5},{7,6},{6,7},{9,8},{8,9},{11,10... | collective-permute-start | bytes 4866056 | tf_op jit(solution)/shard_map/ppermute | solution.py:502
  45.3 11.1 %all-to-all-start = ((f32[16,1,264]{2,1,0:T(1,128)}), f32[16,1,264]{2,1,0:T(1,128)S(1)}, u32[]{:S(2)}, u32[]{:S(2)}) async-start(f32[16,1,264]{2,1,0:T(1,128)} %get-tuple-element.55), calls=%async_computation | async-start | bytes 49152 | tf_op jit(solution)/shard_map/all_to_all | solution.py:505

commit v3 on v2

--- a/solution.py
+++ b/solution.py
@@ -270,7 +270,7 @@
         part = pl.ds(pl.multiple_of(index * chunk, chunk), chunk)
         return pltpu.make_async_copy(passing.at[part], passed_ref.at[part], copied.at[index])
 
-    def one_chunk(index, _):
+    def late_sums(index, _):
         part = pl.ds(pl.multiple_of(index * chunk, chunk), chunk)
         if len(late_steps) > 1:
             add_late(part, range(0, features, 128))
@@ -283,6 +283,10 @@
                 def _():
                     add_late(part, range(first, after, 128))
 
+        return 0
+
+    def terms(index, _):
+        part = pl.ds(pl.multiple_of(index * chunk, chunk), chunk)
         inverse = inverse_ref[part, :]
         pull = jnp.sum(pulls[part, :], axis=1, keepdims=True) / features
         pull = jnp.broadcast_to(pull, inverse.shape) * inverse * inverse * inverse
@@ -306,12 +310,13 @@
 
         return 0
 
-    lax.fori_loop(0, rows // chunk, one_chunk, 0)
+    lax.fori_loop(0, rows // chunk, late_sums, 0)
     total = jnp.sum(gain_sum[...], axis=0, keepdims=True)
     for block in range(line * plane):
         gain_blocks[block] = total[:, block * width : (block + 1) * width]
     gain_copy = pltpu.make_async_copy(gain_blocks, gain_out, copied.at[rows // chunk])
     gain_copy.start()
+    lax.fori_loop(0, rows // chunk, terms, 0)
 
     @pl.when(is_last)
     def _():

time: 57.3 us -> 56.7 us (0.990)
  Pallas kernels: 12.9 us -> 12.3 us
    pallas_call x1, Pallas kernels: 2.8 us -> 2.2 us  [finish(): pl.pallas_call(functools.partial(finish_kernel, line, plane, groups, fold...]
where the time goes in v3:
time: 56.7 us; the launch traced here: 56.4 us
  starting transfers between devices  24.4 us (43%)
  waiting for transfers between devices  16.9 us (30%)
  Pallas kernels  12.3 us (22%)
  local copies, waits for them, and re-layouts  2.1 us (4%)
  between operations  0.73 us (1%)
    ppermute x12, starting transfers between devices, along_plane(): return lax.ppermute(value, 'dp', pairs)  14.4 us
    ppermute x12, waiting for transfers between devices, along_plane(): return lax.ppermute(value, 'dp', pairs)  9.17 us
    ppermute x3, starting transfers between devices, along_line(): return lax.ppermute(value, 'dp', pairs)  6.13 us
    all_to_all x1, waiting for transfers between devices, on_device(): lax.all_to_all(gain_blocks, 'dp', split_axis=0, concat_axis=0, tiled=True)  5.04 us
    all_to_all x1, starting transfers between devices, on_device(): lax.all_to_all(gain_blocks, 'dp', split_axis=0, concat_axis=0, tiled=True)  3.78 us
    pallas_call x3, Pallas kernels, products(): pl.pallas_call(functools.partial(product_kernel, len(tokens), count, fold...  3.43 us
    ppermute x3, waiting for transfers between devices, along_line(): return lax.ppermute(value, 'dp', pairs)  2.66 us
    pallas_call x1, Pallas kernels, hand_on(): pl.pallas_call(functools.partial(hand_kernel, turn, chunk), out_shape=jax...  2.3 us
  transfers between devices with their start and end apart: 17, of which 8 were waited for; matrix products, arithmetic and copies ran while one was open for 0% of the time, Pallas kernels for 17%

profile of v3, /device:TPU:0, one launch (start us, length us, event | category | flops | bytes accessed | tf_op | source)
XLA Modules:
  0.0 56.4 jit_solution(13501075697904455111)
XLA Ops:
  0.6 4.1 %collective-permute-start.4 = (bf16[264,640]{1,0:T(8,128)(2,1)}, bf16[264,640]{1,0:T(8,128)(2,1)S(1)}, u32[]{:S(2)}, u32[]{:S(2)}) collective-permute-start(bf16[264,640]{1,0:T(8,128)(2,1)} %bitcast.10), channel_id=1, source_target_pairs={{0,16},{2,18},{4,20},{6,22},{8,24},{10,26},{12,28},{14,30},{16,0},... | collective-permute-start | bytes 1013768 | tf_op jit(solution)/shard_map/ppermute | solution.py:49
  4.7 1.6 %collective-permute-start.3 = (bf16[264,640]{1,0:T(8,128)(2,1)}, bf16[264,640]{1,0:T(8,128)(2,1)S(1)}, u32[]{:S(2)}, u32[]{:S(2)}) collective-permute-start(bf16[264,640]{1,0:T(8,128)(2,1)} %bitcast.11), channel_id=1, source_target_pairs={{0,8},{2,10},{4,12},{6,14},{8,0},{10,2},{12,4},{14,6},{16,24},{18,... | collective-permute-start | bytes 1013768 | tf_op jit(solution)/shard_map/ppermute | solution.py:49
  6.3 2.4 %collective-permute-start.2 = (bf16[192,640]{1,0:T(8,128)(2,1)}, bf16[192,640]{1,0:T(8,128)(2,1)S(1)}, u32[]{:S(2)}, u32[]{:S(2)}) collective-permute-start(bf16[192,640]{1,0:T(8,128)(2,1)} %bitcast.13), channel_id=1, source_target_pairs={{0,6},{2,4},{4,2},{6,0},{8,14},{10,12},{12,10},{14,8},{16,22},{18,... | collective-permute-start | bytes 737288 | tf_op jit(solution)/shard_map/ppermute | solution.py:59
  8.8 0.5 collective-permute-start.1
  9.3 0.5 collective-permute-start
  9.8 1.4 %copy-done = bf16[1,1,4,48,4224]{4,3,2,1,0:T(8,128)(2,1)S(1)} copy-done((bf16[1,1,4,48,4224]{4,3,2,1,0:T(8,128)(2,1)S(1)}, bf16[1,1,4,48,4224]{4,3,2,1,0:T(8,128)(2,1)}, u32[]{:S(2)}) %copy-start) | copy-done | bytes 1622040
  11.2 0.7 %copy-done.6 = s32[1,4]{1,0:T(1,128)S(1)} copy-done((s32[1,4]{1,0:T(1,128)S(1)}, s32[1,4]{1,0:T(1,128)}, u32[]{:S(2)}) %copy-start.6) | copy-done | bytes 40
  11.9 2.0 %live_inverse.1.inverse_ref = f32[192,128]{1,0:T(8,128)S(1)} custom-call(s32[4]{0:T(128)S(1)} %bitcast.19, bf16[192,4224]{1,0:T(8,128)(2,1)S(1)} %bitcast.6), custom_call_target="tpu_custom_call" | custom-call | flops 1622016 | bytes 1622016 | tf_op jit(solution)/shard_map/live_inverse/pallas_call | solution.py:132
  13.9 2.5 %collective-permute-done.2.refs_3_ = bf16[192,640]{1,0:T(8,128)(2,1)S(1)} collective-permute-done((bf16[192,640]{1,0:T(8,128)(2,1)}, bf16[192,640]{1,0:T(8,128)(2,1)S(1)}, u32[]{:S(2)}, u32[]{:S(2)}) %collective-permute-start.2) | collective-permute-done | bytes 245792 | tf_op jit(solution)/shard_map/ppermute | solution.py:59
  16.4 3.5 %collective-permute-done.1.refs_2_ = bf16[192,640]{1,0:T(8,128)(2,1)S(1)} collective-permute-done((bf16[192,640]{1,0:T(8,128)(2,1)}, bf16[192,640]{1,0:T(8,128)(2,1)S(1)}, u32[]{:S(2)}, u32[]{:S(2)}) %collective-permute-start.1) | collective-permute-done | bytes 245792 | tf_op jit(solution)/shard_map/ppermute | solution.py:59
  19.8 0.1 collective-permute-done.refs_1_
  19.9 0.0 copy-done.3
  19.9 0.0 copy-done.4
  19.9 0.9 %token_products.3 = (bf16[1,16,3168]{2,1,0:T(8,128)(2,1)S(1)}, bf16[1,16,3168]{2,1,0:T(8,128)(2,1)S(1)}, bf16[1,16,3168]{2,1,0:T(8,128)(2,1)S(1)}, bf16[1,16,3168]{2,1,0:T(8,128)(2,1)S(1)}) custom-call(bf16[192,640]{1,0:T(8,128)(2,1)S(1)} %bitcast.16, bf16[192,640]{1,0:T(8,128)(2,1)S(1)} %collective-permute-done.refs_1_, ...), custom_call_target="tpu_custom_call" | custom-call | flops 259522560 | bytes 1726464 | tf_op jit(solution)/shard_map/token_products/pallas_call | solution.py:85
  20.8 1.6 %collective-permute-start.5 = (bf16[1,16,3168]{2,1,0:T(8,128)(2,1)S(1)}, bf16[1,16,3168]{2,1,0:T(8,128)(2,1)S(1)}, u32[]{:S(2)}, u32[]{:S(2)}) collective-permute-start(bf16[1,16,3168]{2,1,0:T(8,128)(2,1)S(1)} %get-tuple-element.37), channel_id=1, source_target_pairs={{0,2},{2,0},{4,6},{6,4},{8,10},{10,8},{12,14},{14,12},{16,18},{18,... | collective-permute-start | bytes 304136 | tf_op jit(solution)/shard_map/ppermute | solution.py:59
  22.4 0.7 %collective-permute-start.6 = (bf16[1,16,3168]{2,1,0:T(8,128)(2,1)S(1)}, bf16[1,16,3168]{2,1,0:T(8,128)(2,1)S(1)}, u32[]{:S(2)}, u32[]{:S(2)}) collective-permute-start(bf16[1,16,3168]{2,1,0:T(8,128)(2,1)S(1)} %get-tuple-element.38), channel_id=1, source_target_pairs={{0,4},{2,6},{4,0},{6,2},{8,12},{10,14},{12,8},{14,10},{16,20},{18,... | collective-permute-start | bytes 304136 | tf_op jit(solution)/shard_map/ppermute | solution.py:59
  23.1 1.3 %collective-permute-start.7 = (bf16[1,16,3168]{2,1,0:T(8,128)(2,1)S(1)}, bf16[1,16,3168]{2,1,0:T(8,128)(2,1)S(1)}, u32[]{:S(2)}, u32[]{:S(2)}) collective-permute-start(bf16[1,16,3168]{2,1,0:T(8,128)(2,1)S(1)} %get-tuple-element.39), channel_id=1, source_target_pairs={{0,6},{2,4},{4,2},{6,0},{8,14},{10,12},{12,10},{14,8},{16,22},{18,... | collective-permute-start | bytes 304136 | tf_op jit(solution)/shard_map/ppermute | solution.py:59
  24.4 0.0 collective-permute-done.4.refs_5_
  24.4 0.5 collective-permute-start.11
  24.8 0.0 collective-permute-done.3.refs_4_
  24.8 1.6 %token_products.4 = (bf16[2,16,3168]{2,1,0:T(8,128)(2,1)S(1)}, bf16[2,16,3168]{2,1,0:T(8,128)(2,1)S(1)}, bf16[2,16,3168]{2,1,0:T(8,128)(2,1)S(1)}, bf16[2,16,3168]{2,1,0:T(8,128)(2,1)S(1)}) custom-call(bf16[192,640]{1,0:T(8,128)(2,1)S(1)} %bitcast.17, bf16[192,640]{1,0:T(8,128)(2,1)S(1)} %collective-permute-done.refs_1_, ...), custom_call_target="tpu_custom_call" | custom-call | flops 5190451200 | bytes 2469888 | tf_op jit(solution)/shard_map/token_products/pallas_call | solution.py:85
  26.5 1.6 %collective-permute-start.8 = (bf16[2,16,3168]{2,1,0:T(8,128)(2,1)S(1)}, bf16[2,16,3168]{2,1,0:T(8,128)(2,1)S(1)}, u32[]{:S(2)}, u32[]{:S(2)}) collective-permute-start(bf16[2,16,3168]{2,1,0:T(8,128)(2,1)S(1)} %get-tuple-element.43), channel_id=1, source_target_pairs={{0,2},{2,0},{4,6},{6,4},{8,10},{10,8},{12,14},{14,12},{16,18},{18,... | collective-permute-start | bytes 608264 | tf_op jit(solution)/shard_map/ppermute | solution.py:59
  28.0 0.0 collective-permute-done.5.refs_2_
  28.0 0.7 %collective-permute-start.9 = (bf16[2,16,3168]{2,1,0:T(8,128)(2,1)S(1)}, bf16[2,16,3168]{2,1,0:T(8,128)(2,1)S(1)}, u32[]{:S(2)}, u32[]{:S(2)}) collective-permute-start(bf16[2,16,3168]{2,1,0:T(8,128)(2,1)S(1)} %get-tuple-element.45), channel_id=1, source_target_pairs={{0,4},{2,6},{4,0},{6,2},{8,12},{10,14},{12,8},{14,10},{16,20},{18,... | collective-permute-start | bytes 608264 | tf_op jit(solution)/shard_map/ppermute | solution.py:59
  28.8 0.3 collective-permute-done.6.refs_4_
  29.1 0.0 collective-permute-done.7.refs_6_
  29.1 1.6 %collective-permute-start.10 = (bf16[2,16,3168]{2,1,0:T(8,128)(2,1)S(1)}, bf16[2,16,3168]{2,1,0:T(8,128)(2,1)S(1)}, u32[]{:S(2)}, u32[]{:S(2)}) collective-permute-start(bf16[2,16,3168]{2,1,0:T(8,128)(2,1)S(1)} %get-tuple-element.47), channel_id=1, source_target_pairs={{0,6},{2,4},{4,2},{6,0},{8,14},{10,12},{12,10},{14,8},{16,22},{18,... | collective-permute-start | bytes 608264 | tf_op jit(solution)/shard_map/ppermute | solution.py:59
  30.7 2.7 %collective-permute-done.11.refs_4_ = bf16[264,640]{1,0:T(8,128)(2,1)S(1)} collective-permute-done((bf16[264,640]{1,0:T(8,128)(2,1)S(1)}, bf16[264,640]{1,0:T(8,128)(2,1)S(1)}, u32[]{:S(2)}, u32[]{:S(2)}) %collective-permute-start.11) | collective-permute-done | bytes 337952 | tf_op jit(solution)/shard_map/ppermute | solution.py:49
  33.3 0.9 %token_products.5 = (bf16[1,16,3168]{2,1,0:T(8,128)(2,1)S(1)}, bf16[1,16,3168]{2,1,0:T(8,128)(2,1)S(1)}, bf16[1,16,3168]{2,1,0:T(8,128)(2,1)S(1)}, bf16[1,16,3168]{2,1,0:T(8,128)(2,1)S(1)}) custom-call(bf16[192,640]{1,0:T(8,128)(2,1)S(1)} %bitcast.18, bf16[192,640]{1,0:T(8,128)(2,1)S(1)} %collective-permute-done.refs_1_, ...), custom_call_target="tpu_custom_call" | custom-call | flops 2595225600 | bytes 1726464 | tf_op jit(solution)/shard_map/token_products/pallas_call | solution.py:85
  34.2 0.0 copy-start.2
  34.2 1.6 %collective-permute-start.12 = (bf16[1,16,3168]{2,1,0:T(8,128)(2,1)S(1)}, bf16[1,16,3168]{2,1,0:T(8,128)(2,1)S(1)}, u32[]{:S(2)}, u32[]{:S(2)}) collective-permute-start(bf16[1,16,3168]{2,1,0:T(8,128)(2,1)S(1)} %get-tuple-element.52), channel_id=1, source_target_pairs={{0,2},{2,0},{4,6},{6,4},{8,10},{10,8},{12,14},{14,12},{16,18},{18,... | collective-permute-start | bytes 304136 | tf_op jit(solution)/shard_map/ppermute | solution.py:59
  35.8 0.4 collective-permute-start.13
  36.2 0.0 collective-permute-done.8.refs_3_
  36.2 1.6 %collective-permute-start.14 = (bf16[1,16,3168]{2,1,0:T(8,128)(2,1)S(1)}, bf16[1,16,3168]{2,1,0:T(8,128)(2,1)S(1)}, u32[]{:S(2)}, u32[]{:S(2)}) collective-permute-start(bf16[1,16,3168]{2,1,0:T(8,128)(2,1)S(1)} %get-tuple-element.54), channel_id=1, source_target_pairs={{0,6},{2,4},{4,2},{6,0},{8,14},{10,12},{12,10},{14,8},{16,22},{18,... | collective-permute-start | bytes 304136 | tf_op jit(solution)/shard_map/ppermute | solution.py:59
  37.8 0.0 collective-permute-done.9.refs_5_
  37.8 1.4 %collective-permute-done.10.refs_7_ = bf16[2,16,3168]{2,1,0:T(8,128)(2,1)S(1)} collective-permute-done((bf16[2,16,3168]{2,1,0:T(8,128)(2,1)S(1)}, bf16[2,16,3168]{2,1,0:T(8,128)(2,1)S(1)}, u32[]{:S(2)}, u32[]{:S(2)}) %collective-permute-start.10) | collective-permute-done | bytes 202784 | tf_op jit(solution)/shard_map/ppermute | solution.py:59
  39.2 0.0 copy-done.5
  39.2 1.8 %placed_early.1 = (bf16[192,4224]{1,0:T(8,128)(2,1)S(1)}, f32[192,128]{1,0:T(8,128)S(1)}, f32[8,4224]{1,0:T(8,128)S(1)}) custom-call(f32[192,128]{1,0:T(8,128)S(1)} %live_inverse.1.inverse_ref, bf16[192,4224]{1,0:T(8,128)(2,1)S(1)} %bitcast.7, f32[1,4224]{1,0:T(1,128)S(1)} %copy-done.5, bf16[1,16,3168]{2,1,0:T(8,128)(2,1)S(1)} %get-tuple-element.40.refs_0_, ...), custom_call_target="tpu_custom_call" | custom-call | flops 6488064 | bytes 6488064 | tf_op jit(solution)/shard_map/placed_early/pallas_call | solution.py:219
  41.0 0.0 collective-permute-done.12.refs_1_
  41.1 1.4 %collective-permute-done.13.refs_2_ = bf16[1,16,3168]{2,1,0:T(8,128)(2,1)S(1)} collective-permute-done((bf16[1,16,3168]{2,1,0:T(8,128)(2,1)S(1)}, bf16[1,16,3168]{2,1,0:T(8,128)(2,1)S(1)}, u32[]{:S(2)}, u32[]{:S(2)}) %collective-permute-start.13) | collective-permute-done | bytes 101408 | tf_op jit(solution)/shard_map/ppermute | solution.py:59
  42.4 0.0 collective-permute-done.14.refs_3_
  42.4 2.2 %norm_backward.1 = (bf16[192,4224]{1,0:T(8,128)(2,1)}, f32[192,4224]{1,0:T(8,128)S(1)}, f32[16,1,264]{2,1,0:T(1,128)}) custom-call(bf16[192,4224]{1,0:T(8,128)(2,1)S(1)} %get-tuple-element.48.early_ref, f32[192,128]{1,0:T(8,128)S(1)} %get-tuple-element.49.early_pulls, f32[8,4224]{1,0:T(8,128)S(1)} %get-tuple-element.50.early_gains, ...), custom_call_target="tpu_custom_call" | custom-call | flops 12976128 | bytes 9732096 | tf_op jit(solution)/shard_map/norm_backward/pallas_call | solution.py:347
  44.6 0.1 collective-permute-start.15
  44.7 3.8 %all-to-all-start = ((f32[16,1,264]{2,1,0:T(1,128)}), f32[16,1,264]{2,1,0:T(1,128)S(1)}, u32[]{:S(2)}, u32[]{:S(2)}) async-start(f32[16,1,264]{2,1,0:T(1,128)} %get-tuple-element.55), calls=%async_computation | async-start | bytes 49152 | tf_op jit(solution)/shard_map/all_to_all | solution.py:510
  48.5 0.0 collective-permute-done.15.incoming_ref
  48.5 2.3 %hand_on.1 = bf16[192,4224]{1,0:T(8,128)(2,1)} custom-call(bf16[192,4224]{1,0:T(8,128)(2,1)} %collective-permute-done.15.incoming_ref, f32[192,4224]{1,0:T(8,128)S(1)} %get-tuple-element.57.local_ref, bf16[192,4224]{1,0:T(8,128)(2,1)} %get-tuple-element.56.result_ref), custom_call_target="tpu_custom_call" | custom-call | tf_op jit(solution)/shard_map/hand_on/pallas_call | solution.py:404
  50.8 5.0 %all-to-all-done.parts_ref = f32[16,1,264]{2,1,0:T(1,128)S(1)} async-done(((f32[16,1,264]{2,1,0:T(1,128)}), f32[16,1,264]{2,1,0:T(1,128)S(1)}, u32[]{:S(2)}, u32[]{:S(2)}) %all-to-all-start) | async-done | bytes 16928 | tf_op jit(solution)/shard_map/all_to_all | solution.py:510
  55.9 0.6 %sum_scaled.1 = f32[1,264]{1,0:T(1,128)} custom-call(f32[16,1,264]{2,1,0:T(1,128)S(1)} %all-to-all-done.parts_ref), custom_call_target="tpu_custom_call" | custom-call | flops 4224 | bytes 16896 | tf_op jit(solution)/shard_map/sum_scaled/pallas_call | solution.py:430
  (8 shorter events, 0.0 us)
Async XLA Ops:
  0.6 23.8 %collective-permute-start.4 = (bf16[264,640]{1,0:T(8,128)(2,1)}, bf16[264,640]{1,0:T(8,128)(2,1)S(1)}, u32[]{:S(2)}, u32[]{:S(2)}) collective-permute-start(bf16[264,640]{1,0:T(8,128)(2,1)} %bitcast.10), channel_id=1, source_target_pairs={{0,16},{2,18},{4,20},{6,22},{8,24},{10,26},{12,28},{14,30},{16,0},... | collective-permute-start | bytes 1013768 | tf_op jit(solution)/shard_map/ppermute | solution.py:49
  4.7 20.1 %collective-permute-start.3 = (bf16[264,640]{1,0:T(8,128)(2,1)}, bf16[264,640]{1,0:T(8,128)(2,1)S(1)}, u32[]{:S(2)}, u32[]{:S(2)}) collective-permute-start(bf16[264,640]{1,0:T(8,128)(2,1)} %bitcast.11), channel_id=1, source_target_pairs={{0,8},{2,10},{4,12},{6,14},{8,0},{10,2},{12,4},{14,6},{16,24},{18,... | collective-permute-start | bytes 1013768 | tf_op jit(solution)/shard_map/ppermute | solution.py:49
  6.3 10.0 %collective-permute-start.2 = (bf16[192,640]{1,0:T(8,128)(2,1)}, bf16[192,640]{1,0:T(8,128)(2,1)S(1)}, u32[]{:S(2)}, u32[]{:S(2)}) collective-permute-start(bf16[192,640]{1,0:T(8,128)(2,1)} %bitcast.13), channel_id=1, source_target_pairs={{0,6},{2,4},{4,2},{6,0},{8,14},{10,12},{12,10},{14,8},{16,22},{18,... | collective-permute-start | bytes 737288 | tf_op jit(solution)/shard_map/ppermute | solution.py:59
  8.8 11.1 %collective-permute-start.1 = (bf16[192,640]{1,0:T(8,128)(2,1)}, bf16[192,640]{1,0:T(8,128)(2,1)S(1)}, u32[]{:S(2)}, u32[]{:S(2)}) collective-permute-start(bf16[192,640]{1,0:T(8,128)(2,1)} %bitcast.14), channel_id=1, source_target_pairs={{0,4},{2,6},{4,0},{6,2},{8,12},{10,14},{12,8},{14,10},{16,20},{18,... | collective-permute-start | bytes 737288 | tf_op jit(solution)/shard_map/ppermute | solution.py:59
  9.3 10.7 %collective-permute-start = (bf16[192,640]{1,0:T(8,128)(2,1)}, bf16[192,640]{1,0:T(8,128)(2,1)S(1)}, u32[]{:S(2)}, u32[]{:S(2)}) collective-permute-start(bf16[192,640]{1,0:T(8,128)(2,1)} %bitcast.15), channel_id=1, source_target_pairs={{0,2},{2,0},{4,6},{6,4},{8,10},{10,8},{12,14},{14,12},{16,18},{18,... | collective-permute-start | bytes 737288 | tf_op jit(solution)/shard_map/ppermute | solution.py:59
  9.8 1.4 %copy-start = (bf16[1,1,4,48,4224]{4,3,2,1,0:T(8,128)(2,1)S(1)}, bf16[1,1,4,48,4224]{4,3,2,1,0:T(8,128)(2,1)}, u32[]{:S(2)}) copy-start(bf16[1,1,4,48,4224]{4,3,2,1,0:T(8,128)(2,1)} %param.6) | copy-start | bytes 4866052
  11.2 0.7 %copy-start.6 = (s32[1,4]{1,0:T(1,128)S(1)}, s32[1,4]{1,0:T(1,128)}, u32[]{:S(2)}) copy-start(s32[1,4]{1,0:T(1,128)} %param.11) | copy-start | bytes 52
  11.9 8.0 %copy-start.3 = (bf16[1,264,640]{2,1,0:T(8,128)(2,1)S(1)}, bf16[1,264,640]{2,1,0:T(8,128)(2,1)}, u32[]{:S(2)}) copy-start(bf16[1,264,640]{2,1,0:T(8,128)(2,1)} %param.10) | copy-start | bytes 1013764
  11.9 8.0 %copy-start.4 = (bf16[1,1,4,48,640]{4,3,2,1,0:T(8,128)(2,1)S(1)}, bf16[1,1,4,48,640]{4,3,2,1,0:T(8,128)(2,1)}, u32[]{:S(2)}) copy-start(bf16[1,1,4,48,640]{4,3,2,1,0:T(8,128)(2,1)} %param.7) | copy-start | bytes 737284
  20.8 7.2 %collective-permute-start.5 = (bf16[1,16,3168]{2,1,0:T(8,128)(2,1)S(1)}, bf16[1,16,3168]{2,1,0:T(8,128)(2,1)S(1)}, u32[]{:S(2)}, u32[]{:S(2)}) collective-permute-start(bf16[1,16,3168]{2,1,0:T(8,128)(2,1)S(1)} %get-tuple-element.37), channel_id=1, source_target_pairs={{0,2},{2,0},{4,6},{6,4},{8,10},{10,8},{12,14},{14,12},{16,18},{18,... | collective-permute-start | bytes 304136 | tf_op jit(solution)/shard_map/ppermute | solution.py:59
  22.4 6.7 %collective-permute-start.6 = (bf16[1,16,3168]{2,1,0:T(8,128)(2,1)S(1)}, bf16[1,16,3168]{2,1,0:T(8,128)(2,1)S(1)}, u32[]{:S(2)}, u32[]{:S(2)}) collective-permute-start(bf16[1,16,3168]{2,1,0:T(8,128)(2,1)S(1)} %get-tuple-element.38), channel_id=1, source_target_pairs={{0,4},{2,6},{4,0},{6,2},{8,12},{10,14},{12,8},{14,10},{16,20},{18,... | collective-permute-start | bytes 304136 | tf_op jit(solution)/shard_map/ppermute | solution.py:59
  23.1 6.0 %collective-permute-start.7 = (bf16[1,16,3168]{2,1,0:T(8,128)(2,1)S(1)}, bf16[1,16,3168]{2,1,0:T(8,128)(2,1)S(1)}, u32[]{:S(2)}, u32[]{:S(2)}) collective-permute-start(bf16[1,16,3168]{2,1,0:T(8,128)(2,1)S(1)} %get-tuple-element.39), channel_id=1, source_target_pairs={{0,6},{2,4},{4,2},{6,0},{8,14},{10,12},{12,10},{14,8},{16,22},{18,... | collective-permute-start | bytes 304136 | tf_op jit(solution)/shard_map/ppermute | solution.py:59
  24.4 8.9 %collective-permute-start.11 = (bf16[264,640]{1,0:T(8,128)(2,1)S(1)}, bf16[264,640]{1,0:T(8,128)(2,1)S(1)}, u32[]{:S(2)}, u32[]{:S(2)}) collective-permute-start(bf16[264,640]{1,0:T(8,128)(2,1)S(1)} %collective-permute-done.4.refs_5_), channel_id=1, source_target_pairs={{0,8},{2,10},{4,12},{6,14},{8,0},{10,2},{12,4},{14,6},{16,24},{18,... | collective-permute-start | bytes 1013768 | tf_op jit(solution)/shard_map/ppermute | solution.py:49
  26.5 9.7 %collective-permute-start.8 = (bf16[2,16,3168]{2,1,0:T(8,128)(2,1)S(1)}, bf16[2,16,3168]{2,1,0:T(8,128)(2,1)S(1)}, u32[]{:S(2)}, u32[]{:S(2)}) collective-permute-start(bf16[2,16,3168]{2,1,0:T(8,128)(2,1)S(1)} %get-tuple-element.43), channel_id=1, source_target_pairs={{0,2},{2,0},{4,6},{6,4},{8,10},{10,8},{12,14},{14,12},{16,18},{18,... | collective-permute-start | bytes 608264 | tf_op jit(solution)/shard_map/ppermute | solution.py:59
  28.0 9.8 %collective-permute-start.9 = (bf16[2,16,3168]{2,1,0:T(8,128)(2,1)S(1)}, bf16[2,16,3168]{2,1,0:T(8,128)(2,1)S(1)}, u32[]{:S(2)}, u32[]{:S(2)}) collective-permute-start(bf16[2,16,3168]{2,1,0:T(8,128)(2,1)S(1)} %get-tuple-element.45), channel_id=1, source_target_pairs={{0,4},{2,6},{4,0},{6,2},{8,12},{10,14},{12,8},{14,10},{16,20},{18,... | collective-permute-start | bytes 608264 | tf_op jit(solution)/shard_map/ppermute | solution.py:59
  29.1 10.1 %copy-start.1 = (bf16[1,1,4,48,4224]{4,3,2,1,0:T(8,128)(2,1)S(1)}, bf16[1,1,4,48,4224]{4,3,2,1,0:T(8,128)(2,1)}, u32[]{:S(2)}) copy-start(bf16[1,1,4,48,4224]{4,3,2,1,0:T(8,128)(2,1)} %param.6) | copy-start | bytes 4866052
  29.1 10.1 %copy-start.5 = (f32[1,4224]{1,0:T(1,128)S(1)}, f32[1,4224]{1,0:T(1,128)}, u32[]{:S(2)}) copy-start(f32[1,4224]{1,0:T(1,128)} %gain_ref.3) | copy-start | bytes 50692
  29.1 10.1 %collective-permute-start.10 = (bf16[2,16,3168]{2,1,0:T(8,128)(2,1)S(1)}, bf16[2,16,3168]{2,1,0:T(8,128)(2,1)S(1)}, u32[]{:S(2)}, u32[]{:S(2)}) collective-permute-start(bf16[2,16,3168]{2,1,0:T(8,128)(2,1)S(1)} %get-tuple-element.47), channel_id=1, source_target_pairs={{0,6},{2,4},{4,2},{6,0},{8,14},{10,12},{12,10},{14,8},{16,22},{18,... | collective-permute-start | bytes 608264 | tf_op jit(solution)/shard_map/ppermute | solution.py:59
  34.2 8.2 %copy-start.2 = (bf16[1,4,48,4224]{3,2,1,0:T(8,128)(2,1)S(1)}, bf16[1,4,48,4224]{3,2,1,0:T(8,128)(2,1)}, u32[]{:S(2)}) copy-start(bf16[1,4,48,4224]{3,2,1,0:T(8,128)(2,1)} %param.8) | copy-start | bytes 4866052
  34.2 6.8 %collective-permute-start.12 = (bf16[1,16,3168]{2,1,0:T(8,128)(2,1)S(1)}, bf16[1,16,3168]{2,1,0:T(8,128)(2,1)S(1)}, u32[]{:S(2)}, u32[]{:S(2)}) collective-permute-start(bf16[1,16,3168]{2,1,0:T(8,128)(2,1)S(1)} %get-tuple-element.52), channel_id=1, source_target_pairs={{0,2},{2,0},{4,6},{6,4},{8,10},{10,8},{12,14},{14,12},{16,18},{18,... | collective-permute-start | bytes 304136 | tf_op jit(solution)/shard_map/ppermute | solution.py:59
  35.8 6.6 %collective-permute-start.13 = (bf16[1,16,3168]{2,1,0:T(8,128)(2,1)S(1)}, bf16[1,16,3168]{2,1,0:T(8,128)(2,1)S(1)}, u32[]{:S(2)}, u32[]{:S(2)}) collective-permute-start(bf16[1,16,3168]{2,1,0:T(8,128)(2,1)S(1)} %get-tuple-element.53), channel_id=1, source_target_pairs={{0,4},{2,6},{4,0},{6,2},{8,12},{10,14},{12,8},{14,10},{16,20},{18,... | collective-permute-start | bytes 304136 | tf_op jit(solution)/shard_map/ppermute | solution.py:59
  36.2 6.2 %collective-permute-start.14 = (bf16[1,16,3168]{2,1,0:T(8,128)(2,1)S(1)}, bf16[1,16,3168]{2,1,0:T(8,128)(2,1)S(1)}, u32[]{:S(2)}, u32[]{:S(2)}) collective-permute-start(bf16[1,16,3168]{2,1,0:T(8,128)(2,1)S(1)} %get-tuple-element.54), channel_id=1, source_target_pairs={{0,6},{2,4},{4,2},{6,0},{8,14},{10,12},{12,10},{14,8},{16,22},{18,... | collective-permute-start | bytes 304136 | tf_op jit(solution)/shard_map/ppermute | solution.py:59
  44.6 3.9 %collective-permute-start.15 = (bf16[192,4224]{1,0:T(8,128)(2,1)}, bf16[192,4224]{1,0:T(8,128)(2,1)}, u32[]{:S(2)}, u32[]{:S(2)}) collective-permute-start(bf16[192,4224]{1,0:T(8,128)(2,1)} %get-tuple-element.56.result_ref), channel_id=1, source_target_pairs={{1,0},{0,1},{3,2},{2,3},{5,4},{4,5},{7,6},{6,7},{9,8},{8,9},{11,10... | collective-permute-start | bytes 4866056 | tf_op jit(solution)/shard_map/ppermute | solution.py:507
  44.7 11.2 %all-to-all-start = ((f32[16,1,264]{2,1,0:T(1,128)}), f32[16,1,264]{2,1,0:T(1,128)S(1)}, u32[]{:S(2)}, u32[]{:S(2)}) async-start(f32[16,1,264]{2,1,0:T(1,128)} %get-tuple-element.55), calls=%async_computation | async-start | bytes 49152 | tf_op jit(solution)/shard_map/all_to_all | solution.py:510

commit v4 on v3

--- a/solution.py
+++ b/solution.py
@@ -270,20 +270,23 @@
         part = pl.ds(pl.multiple_of(index * chunk, chunk), chunk)
         return pltpu.make_async_copy(passing.at[part], passed_ref.at[part], copied.at[index])
 
-    def late_sums(index, _):
-        part = pl.ds(pl.multiple_of(index * chunk, chunk), chunk)
-        if len(late_steps) > 1:
-            add_late(part, range(0, features, 128))
-        else:
-            for owner_z in range(line):
-                first = owner_z * plane * width // 128 * 128
-                after = (owner_z + 1) * plane * width
-
-                @pl.when(late_z == owner_z)
-                def _():
-                    add_late(part, range(first, after, 128))
-
-        return 0
+    def late_sums(lefts):
+        def one_chunk(index, _):
+            add_late(pl.ds(pl.multiple_of(index * chunk, chunk), chunk), lefts)
+            return 0
+
+        lax.fori_loop(0, rows // chunk, one_chunk, 0)
+
+    if len(late_steps) > 1:
+        late_sums(range(0, features, 128))
+    else:
+        for owner_z in range(line):
+            first = owner_z * plane * width // 128 * 128
+            after = (owner_z + 1) * plane * width
+
+            @pl.when(late_z == owner_z)
+            def _():
+                late_sums(range(first, after, 128))
 
     def terms(index, _):
         part = pl.ds(pl.multiple_of(index * chunk, chunk), chunk)
@@ -310,7 +313,6 @@
 
         return 0
 
-    lax.fori_loop(0, rows // chunk, late_sums, 0)
     total = jnp.sum(gain_sum[...], axis=0, keepdims=True)
     for block in range(line * plane):
         gain_blocks[block] = total[:, block * width : (block + 1) * width]
@@ -343,7 +345,7 @@
         pltpu.VMEM((rows, features), jnp.bfloat16),
         pltpu.VMEM(outs[2].shape, jnp.float32),
     ]
-    chunk = math.gcd(rows, 32)
+    chunk = math.gcd(rows, 48)
     return pl.pallas_call(
         functools.partial(finish_kernel, line, plane, groups, fold, last, chunk),
         out_shape=outs,

time: 56.7 us -> 56.4 us (level)
  no operation moved by 1% of the time
where the time goes in v4:
time: 56.4 us; the launch traced here: 56.2 us
  starting transfers between devices  24.4 us (43%)
  waiting for transfers between devices  16.9 us (30%)
  Pallas kernels  12 us (21%)
  local copies, waits for them, and re-layouts  2.1 us (4%)
  between operations  0.73 us (1%)
    ppermute x12, starting transfers between devices, along_plane(): return lax.ppermute(value, 'dp', pairs)  14.4 us
    ppermute x12, waiting for transfers between devices, along_plane(): return lax.ppermute(value, 'dp', pairs)  9.17 us
    ppermute x3, starting transfers between devices, along_line(): return lax.ppermute(value, 'dp', pairs)  6.13 us
    all_to_all x1, waiting for transfers between devices, on_device(): lax.all_to_all(gain_blocks, 'dp', split_axis=0, concat_axis=0, tiled=True)  5.04 us
    all_to_all x1, starting transfers between devices, on_device(): lax.all_to_all(gain_blocks, 'dp', split_axis=0, concat_axis=0, tiled=True)  3.78 us
    pallas_call x3, Pallas kernels, products(): pl.pallas_call(functools.partial(product_kernel, len(tokens), count, fold...  3.43 us
    ppermute x3, waiting for transfers between devices, along_line(): return lax.ppermute(value, 'dp', pairs)  2.66 us
    pallas_call x1, Pallas kernels, hand_on(): pl.pallas_call(functools.partial(hand_kernel, turn, chunk), out_shape=jax...  2.3 us
  transfers between devices with their start and end apart: 17, of which 8 were waited for; matrix products, arithmetic and copies ran while one was open for 0% of the time, Pallas kernels for 17%

profile of v4, /device:TPU:0, one launch (start us, length us, event | category | flops | bytes accessed | tf_op | source)
XLA Modules:
  0.0 56.2 jit_solution(6713889118962380659)
XLA Ops:
  0.6 4.1 %collective-permute-start.4 = (bf16[264,640]{1,0:T(8,128)(2,1)}, bf16[264,640]{1,0:T(8,128)(2,1)S(1)}, u32[]{:S(2)}, u32[]{:S(2)}) collective-permute-start(bf16[264,640]{1,0:T(8,128)(2,1)} %bitcast.10), channel_id=1, source_target_pairs={{0,16},{2,18},{4,20},{6,22},{8,24},{10,26},{12,28},{14,30},{16,0},... | collective-permute-start | bytes 1013768 | tf_op jit(solution)/shard_map/ppermute | solution.py:49
  4.7 1.6 %collective-permute-start.3 = (bf16[264,640]{1,0:T(8,128)(2,1)}, bf16[264,640]{1,0:T(8,128)(2,1)S(1)}, u32[]{:S(2)}, u32[]{:S(2)}) collective-permute-start(bf16[264,640]{1,0:T(8,128)(2,1)} %bitcast.11), channel_id=1, source_target_pairs={{0,8},{2,10},{4,12},{6,14},{8,0},{10,2},{12,4},{14,6},{16,24},{18,... | collective-permute-start | bytes 1013768 | tf_op jit(solution)/shard_map/ppermute | solution.py:49
  6.3 2.4 %collective-permute-start.2 = (bf16[192,640]{1,0:T(8,128)(2,1)}, bf16[192,640]{1,0:T(8,128)(2,1)S(1)}, u32[]{:S(2)}, u32[]{:S(2)}) collective-permute-start(bf16[192,640]{1,0:T(8,128)(2,1)} %bitcast.13), channel_id=1, source_target_pairs={{0,6},{2,4},{4,2},{6,0},{8,14},{10,12},{12,10},{14,8},{16,22},{18,... | collective-permute-start | bytes 737288 | tf_op jit(solution)/shard_map/ppermute | solution.py:59
  8.8 0.5 collective-permute-start.1
  9.3 0.5 collective-permute-start
  9.8 1.4 %copy-done = bf16[1,1,4,48,4224]{4,3,2,1,0:T(8,128)(2,1)S(1)} copy-done((bf16[1,1,4,48,4224]{4,3,2,1,0:T(8,128)(2,1)S(1)}, bf16[1,1,4,48,4224]{4,3,2,1,0:T(8,128)(2,1)}, u32[]{:S(2)}) %copy-start) | copy-done | bytes 1622040
  11.2 0.7 %copy-done.6 = s32[1,4]{1,0:T(1,128)S(1)} copy-done((s32[1,4]{1,0:T(1,128)S(1)}, s32[1,4]{1,0:T(1,128)}, u32[]{:S(2)}) %copy-start.6) | copy-done | bytes 40
  11.9 2.0 %live_inverse.1.inverse_ref = f32[192,128]{1,0:T(8,128)S(1)} custom-call(s32[4]{0:T(128)S(1)} %bitcast.19, bf16[192,4224]{1,0:T(8,128)(2,1)S(1)} %bitcast.6), custom_call_target="tpu_custom_call" | custom-call | flops 1622016 | bytes 1622016 | tf_op jit(solution)/shard_map/live_inverse/pallas_call | solution.py:132
  13.9 2.5 %collective-permute-done.2.refs_3_ = bf16[192,640]{1,0:T(8,128)(2,1)S(1)} collective-permute-done((bf16[192,640]{1,0:T(8,128)(2,1)}, bf16[192,640]{1,0:T(8,128)(2,1)S(1)}, u32[]{:S(2)}, u32[]{:S(2)}) %collective-permute-start.2) | collective-permute-done | bytes 245792 | tf_op jit(solution)/shard_map/ppermute | solution.py:59
  16.4 3.5 %collective-permute-done.1.refs_2_ = bf16[192,640]{1,0:T(8,128)(2,1)S(1)} collective-permute-done((bf16[192,640]{1,0:T(8,128)(2,1)}, bf16[192,640]{1,0:T(8,128)(2,1)S(1)}, u32[]{:S(2)}, u32[]{:S(2)}) %collective-permute-start.1) | collective-permute-done | bytes 245792 | tf_op jit(solution)/shard_map/ppermute | solution.py:59
  19.8 0.1 collective-permute-done.refs_1_
  19.9 0.0 copy-done.3
  19.9 0.0 copy-done.4
  19.9 0.9 %token_products.3 = (bf16[1,16,3168]{2,1,0:T(8,128)(2,1)S(1)}, bf16[1,16,3168]{2,1,0:T(8,128)(2,1)S(1)}, bf16[1,16,3168]{2,1,0:T(8,128)(2,1)S(1)}, bf16[1,16,3168]{2,1,0:T(8,128)(2,1)S(1)}) custom-call(bf16[192,640]{1,0:T(8,128)(2,1)S(1)} %bitcast.16, bf16[192,640]{1,0:T(8,128)(2,1)S(1)} %collective-permute-done.refs_1_, ...), custom_call_target="tpu_custom_call" | custom-call | flops 259522560 | bytes 1726464 | tf_op jit(solution)/shard_map/token_products/pallas_call | solution.py:85
  20.8 1.6 %collective-permute-start.5 = (bf16[1,16,3168]{2,1,0:T(8,128)(2,1)S(1)}, bf16[1,16,3168]{2,1,0:T(8,128)(2,1)S(1)}, u32[]{:S(2)}, u32[]{:S(2)}) collective-permute-start(bf16[1,16,3168]{2,1,0:T(8,128)(2,1)S(1)} %get-tuple-element.37), channel_id=1, source_target_pairs={{0,2},{2,0},{4,6},{6,4},{8,10},{10,8},{12,14},{14,12},{16,18},{18,... | collective-permute-start | bytes 304136 | tf_op jit(solution)/shard_map/ppermute | solution.py:59
  22.4 0.7 %collective-permute-start.6 = (bf16[1,16,3168]{2,1,0:T(8,128)(2,1)S(1)}, bf16[1,16,3168]{2,1,0:T(8,128)(2,1)S(1)}, u32[]{:S(2)}, u32[]{:S(2)}) collective-permute-start(bf16[1,16,3168]{2,1,0:T(8,128)(2,1)S(1)} %get-tuple-element.38), channel_id=1, source_target_pairs={{0,4},{2,6},{4,0},{6,2},{8,12},{10,14},{12,8},{14,10},{16,20},{18,... | collective-permute-start | bytes 304136 | tf_op jit(solution)/shard_map/ppermute | solution.py:59
  23.1 1.3 %collective-permute-start.7 = (bf16[1,16,3168]{2,1,0:T(8,128)(2,1)S(1)}, bf16[1,16,3168]{2,1,0:T(8,128)(2,1)S(1)}, u32[]{:S(2)}, u32[]{:S(2)}) collective-permute-start(bf16[1,16,3168]{2,1,0:T(8,128)(2,1)S(1)} %get-tuple-element.39), channel_id=1, source_target_pairs={{0,6},{2,4},{4,2},{6,0},{8,14},{10,12},{12,10},{14,8},{16,22},{18,... | collective-permute-start | bytes 304136 | tf_op jit(solution)/shard_map/ppermute | solution.py:59
  24.4 0.0 collective-permute-done.4.refs_5_
  24.4 0.5 collective-permute-start.11
  24.8 0.0 collective-permute-done.3.refs_4_
  24.8 1.6 %token_products.4 = (bf16[2,16,3168]{2,1,0:T(8,128)(2,1)S(1)}, bf16[2,16,3168]{2,1,0:T(8,128)(2,1)S(1)}, bf16[2,16,3168]{2,1,0:T(8,128)(2,1)S(1)}, bf16[2,16,3168]{2,1,0:T(8,128)(2,1)S(1)}) custom-call(bf16[192,640]{1,0:T(8,128)(2,1)S(1)} %bitcast.17, bf16[192,640]{1,0:T(8,128)(2,1)S(1)} %collective-permute-done.refs_1_, ...), custom_call_target="tpu_custom_call" | custom-call | flops 5190451200 | bytes 2469888 | tf_op jit(solution)/shard_map/token_products/pallas_call | solution.py:85
  26.5 1.6 %collective-permute-start.8 = (bf16[2,16,3168]{2,1,0:T(8,128)(2,1)S(1)}, bf16[2,16,3168]{2,1,0:T(8,128)(2,1)S(1)}, u32[]{:S(2)}, u32[]{:S(2)}) collective-permute-start(bf16[2,16,3168]{2,1,0:T(8,128)(2,1)S(1)} %get-tuple-element.43), channel_id=1, source_target_pairs={{0,2},{2,0},{4,6},{6,4},{8,10},{10,8},{12,14},{14,12},{16,18},{18,... | collective-permute-start | bytes 608264 | tf_op jit(solution)/shard_map/ppermute | solution.py:59
  28.0 0.0 collective-permute-done.5.refs_2_
  28.0 0.7 %collective-permute-start.9 = (bf16[2,16,3168]{2,1,0:T(8,128)(2,1)S(1)}, bf16[2,16,3168]{2,1,0:T(8,128)(2,1)S(1)}, u32[]{:S(2)}, u32[]{:S(2)}) collective-permute-start(bf16[2,16,3168]{2,1,0:T(8,128)(2,1)S(1)} %get-tuple-element.45), channel_id=1, source_target_pairs={{0,4},{2,6},{4,0},{6,2},{8,12},{10,14},{12,8},{14,10},{16,20},{18,... | collective-permute-start | bytes 608264 | tf_op jit(solution)/shard_map/ppermute | solution.py:59
  28.8 0.3 collective-permute-done.6.refs_4_
  29.1 0.0 collective-permute-done.7.refs_6_
  29.1 1.6 %collective-permute-start.10 = (bf16[2,16,3168]{2,1,0:T(8,128)(2,1)S(1)}, bf16[2,16,3168]{2,1,0:T(8,128)(2,1)S(1)}, u32[]{:S(2)}, u32[]{:S(2)}) collective-permute-start(bf16[2,16,3168]{2,1,0:T(8,128)(2,1)S(1)} %get-tuple-element.47), channel_id=1, source_target_pairs={{0,6},{2,4},{4,2},{6,0},{8,14},{10,12},{12,10},{14,8},{16,22},{18,... | collective-permute-start | bytes 608264 | tf_op jit(solution)/shard_map/ppermute | solution.py:59
  30.7 2.7 %collective-permute-done.11.refs_4_ = bf16[264,640]{1,0:T(8,128)(2,1)S(1)} collective-permute-done((bf16[264,640]{1,0:T(8,128)(2,1)S(1)}, bf16[264,640]{1,0:T(8,128)(2,1)S(1)}, u32[]{:S(2)}, u32[]{:S(2)}) %collective-permute-start.11) | collective-permute-done | bytes 337952 | tf_op jit(solution)/shard_map/ppermute | solution.py:49
  33.3 0.9 %token_products.5 = (bf16[1,16,3168]{2,1,0:T(8,128)(2,1)S(1)}, bf16[1,16,3168]{2,1,0:T(8,128)(2,1)S(1)}, bf16[1,16,3168]{2,1,0:T(8,128)(2,1)S(1)}, bf16[1,16,3168]{2,1,0:T(8,128)(2,1)S(1)}) custom-call(bf16[192,640]{1,0:T(8,128)(2,1)S(1)} %bitcast.18, bf16[192,640]{1,0:T(8,128)(2,1)S(1)} %collective-permute-done.refs_1_, ...), custom_call_target="tpu_custom_call" | custom-call | flops 2595225600 | bytes 1726464 | tf_op jit(solution)/shard_map/token_products/pallas_call | solution.py:85
  34.2 0.0 copy-start.2
  34.2 1.6 %collective-permute-start.12 = (bf16[1,16,3168]{2,1,0:T(8,128)(2,1)S(1)}, bf16[1,16,3168]{2,1,0:T(8,128)(2,1)S(1)}, u32[]{:S(2)}, u32[]{:S(2)}) collective-permute-start(bf16[1,16,3168]{2,1,0:T(8,128)(2,1)S(1)} %get-tuple-element.52), channel_id=1, source_target_pairs={{0,2},{2,0},{4,6},{6,4},{8,10},{10,8},{12,14},{14,12},{16,18},{18,... | collective-permute-start | bytes 304136 | tf_op jit(solution)/shard_map/ppermute | solution.py:59
  35.8 0.4 collective-permute-start.13
  36.2 0.0 collective-permute-done.8.refs_3_
  36.2 1.6 %collective-permute-start.14 = (bf16[1,16,3168]{2,1,0:T(8,128)(2,1)S(1)}, bf16[1,16,3168]{2,1,0:T(8,128)(2,1)S(1)}, u32[]{:S(2)}, u32[]{:S(2)}) collective-permute-start(bf16[1,16,3168]{2,1,0:T(8,128)(2,1)S(1)} %get-tuple-element.54), channel_id=1, source_target_pairs={{0,6},{2,4},{4,2},{6,0},{8,14},{10,12},{12,10},{14,8},{16,22},{18,... | collective-permute-start | bytes 304136 | tf_op jit(solution)/shard_map/ppermute | solution.py:59
  37.8 0.0 collective-permute-done.9.refs_5_
  37.8 1.4 %collective-permute-done.10.refs_7_ = bf16[2,16,3168]{2,1,0:T(8,128)(2,1)S(1)} collective-permute-done((bf16[2,16,3168]{2,1,0:T(8,128)(2,1)S(1)}, bf16[2,16,3168]{2,1,0:T(8,128)(2,1)S(1)}, u32[]{:S(2)}, u32[]{:S(2)}) %collective-permute-start.10) | collective-permute-done | bytes 202784 | tf_op jit(solution)/shard_map/ppermute | solution.py:59
  39.2 0.0 copy-done.5
  39.2 1.8 %placed_early.1 = (bf16[192,4224]{1,0:T(8,128)(2,1)S(1)}, f32[192,128]{1,0:T(8,128)S(1)}, f32[8,4224]{1,0:T(8,128)S(1)}) custom-call(f32[192,128]{1,0:T(8,128)S(1)} %live_inverse.1.inverse_ref, bf16[192,4224]{1,0:T(8,128)(2,1)S(1)} %bitcast.7, f32[1,4224]{1,0:T(1,128)S(1)} %copy-done.5, bf16[1,16,3168]{2,1,0:T(8,128)(2,1)S(1)} %get-tuple-element.40.refs_0_, ...), custom_call_target="tpu_custom_call" | custom-call | flops 6488064 | bytes 6488064 | tf_op jit(solution)/shard_map/placed_early/pallas_call | solution.py:219
  41.0 0.0 collective-permute-done.12.refs_1_
  41.1 1.4 %collective-permute-done.13.refs_2_ = bf16[1,16,3168]{2,1,0:T(8,128)(2,1)S(1)} collective-permute-done((bf16[1,16,3168]{2,1,0:T(8,128)(2,1)S(1)}, bf16[1,16,3168]{2,1,0:T(8,128)(2,1)S(1)}, u32[]{:S(2)}, u32[]{:S(2)}) %collective-permute-start.13) | collective-permute-done | bytes 101408 | tf_op jit(solution)/shard_map/ppermute | solution.py:59
  42.4 0.0 collective-permute-done.14.refs_3_
  42.4 1.9 %norm_backward.1 = (bf16[192,4224]{1,0:T(8,128)(2,1)}, f32[192,4224]{1,0:T(8,128)S(1)}, f32[16,1,264]{2,1,0:T(1,128)}) custom-call(bf16[192,4224]{1,0:T(8,128)(2,1)S(1)} %get-tuple-element.48.early_ref, f32[192,128]{1,0:T(8,128)S(1)} %get-tuple-element.49.early_pulls, f32[8,4224]{1,0:T(8,128)S(1)} %get-tuple-element.50.early_gains, ...), custom_call_target="tpu_custom_call" | custom-call | flops 12976128 | bytes 9732096 | tf_op jit(solution)/shard_map/norm_backward/pallas_call | solution.py:349
  44.4 0.1 collective-permute-start.15
  44.4 3.8 %all-to-all-start = ((f32[16,1,264]{2,1,0:T(1,128)}), f32[16,1,264]{2,1,0:T(1,128)S(1)}, u32[]{:S(2)}, u32[]{:S(2)}) async-start(f32[16,1,264]{2,1,0:T(1,128)} %get-tuple-element.55), calls=%async_computation | async-start | bytes 49152 | tf_op jit(solution)/shard_map/all_to_all | solution.py:512
  48.2 0.0 collective-permute-done.15.incoming_ref
  48.2 2.3 %hand_on.1 = bf16[192,4224]{1,0:T(8,128)(2,1)} custom-call(bf16[192,4224]{1,0:T(8,128)(2,1)} %collective-permute-done.15.incoming_ref, f32[192,4224]{1,0:T(8,128)S(1)} %get-tuple-element.57.local_ref, bf16[192,4224]{1,0:T(8,128)(2,1)} %get-tuple-element.56.result_ref), custom_call_target="tpu_custom_call" | custom-call | tf_op jit(solution)/shard_map/hand_on/pallas_call | solution.py:406
  50.5 5.0 %all-to-all-done.parts_ref = f32[16,1,264]{2,1,0:T(1,128)S(1)} async-done(((f32[16,1,264]{2,1,0:T(1,128)}), f32[16,1,264]{2,1,0:T(1,128)S(1)}, u32[]{:S(2)}, u32[]{:S(2)}) %all-to-all-start) | async-done | bytes 16928 | tf_op jit(solution)/shard_map/all_to_all | solution.py:512
  55.6 0.6 %sum_scaled.1 = f32[1,264]{1,0:T(1,128)} custom-call(f32[16,1,264]{2,1,0:T(1,128)S(1)} %all-to-all-done.parts_ref), custom_call_target="tpu_custom_call" | custom-call | flops 4224 | bytes 16896 | tf_op jit(solution)/shard_map/sum_scaled/pallas_call | solution.py:432
  (8 shorter events, 0.0 us)
Async XLA Ops:
  0.6 23.8 %collective-permute-start.4 = (bf16[264,640]{1,0:T(8,128)(2,1)}, bf16[264,640]{1,0:T(8,128)(2,1)S(1)}, u32[]{:S(2)}, u32[]{:S(2)}) collective-permute-start(bf16[264,640]{1,0:T(8,128)(2,1)} %bitcast.10), channel_id=1, source_target_pairs={{0,16},{2,18},{4,20},{6,22},{8,24},{10,26},{12,28},{14,30},{16,0},... | collective-permute-start | bytes 1013768 | tf_op jit(solution)/shard_map/ppermute | solution.py:49
  4.7 20.1 %collective-permute-start.3 = (bf16[264,640]{1,0:T(8,128)(2,1)}, bf16[264,640]{1,0:T(8,128)(2,1)S(1)}, u32[]{:S(2)}, u32[]{:S(2)}) collective-permute-start(bf16[264,640]{1,0:T(8,128)(2,1)} %bitcast.11), channel_id=1, source_target_pairs={{0,8},{2,10},{4,12},{6,14},{8,0},{10,2},{12,4},{14,6},{16,24},{18,... | collective-permute-start | bytes 1013768 | tf_op jit(solution)/shard_map/ppermute | solution.py:49
  6.3 10.0 %collective-permute-start.2 = (bf16[192,640]{1,0:T(8,128)(2,1)}, bf16[192,640]{1,0:T(8,128)(2,1)S(1)}, u32[]{:S(2)}, u32[]{:S(2)}) collective-permute-start(bf16[192,640]{1,0:T(8,128)(2,1)} %bitcast.13), channel_id=1, source_target_pairs={{0,6},{2,4},{4,2},{6,0},{8,14},{10,12},{12,10},{14,8},{16,22},{18,... | collective-permute-start | bytes 737288 | tf_op jit(solution)/shard_map/ppermute | solution.py:59
  8.8 11.1 %collective-permute-start.1 = (bf16[192,640]{1,0:T(8,128)(2,1)}, bf16[192,640]{1,0:T(8,128)(2,1)S(1)}, u32[]{:S(2)}, u32[]{:S(2)}) collective-permute-start(bf16[192,640]{1,0:T(8,128)(2,1)} %bitcast.14), channel_id=1, source_target_pairs={{0,4},{2,6},{4,0},{6,2},{8,12},{10,14},{12,8},{14,10},{16,20},{18,... | collective-permute-start | bytes 737288 | tf_op jit(solution)/shard_map/ppermute | solution.py:59
  9.3 10.7 %collective-permute-start = (bf16[192,640]{1,0:T(8,128)(2,1)}, bf16[192,640]{1,0:T(8,128)(2,1)S(1)}, u32[]{:S(2)}, u32[]{:S(2)}) collective-permute-start(bf16[192,640]{1,0:T(8,128)(2,1)} %bitcast.15), channel_id=1, source_target_pairs={{0,2},{2,0},{4,6},{6,4},{8,10},{10,8},{12,14},{14,12},{16,18},{18,... | collective-permute-start | bytes 737288 | tf_op jit(solution)/shard_map/ppermute | solution.py:59
  9.8 1.4 %copy-start = (bf16[1,1,4,48,4224]{4,3,2,1,0:T(8,128)(2,1)S(1)}, bf16[1,1,4,48,4224]{4,3,2,1,0:T(8,128)(2,1)}, u32[]{:S(2)}) copy-start(bf16[1,1,4,48,4224]{4,3,2,1,0:T(8,128)(2,1)} %param.6) | copy-start | bytes 4866052
  11.2 0.7 %copy-start.6 = (s32[1,4]{1,0:T(1,128)S(1)}, s32[1,4]{1,0:T(1,128)}, u32[]{:S(2)}) copy-start(s32[1,4]{1,0:T(1,128)} %param.11) | copy-start | bytes 52
  11.9 8.0 %copy-start.3 = (bf16[1,264,640]{2,1,0:T(8,128)(2,1)S(1)}, bf16[1,264,640]{2,1,0:T(8,128)(2,1)}, u32[]{:S(2)}) copy-start(bf16[1,264,640]{2,1,0:T(8,128)(2,1)} %param.10) | copy-start | bytes 1013764
  11.9 8.0 %copy-start.4 = (bf16[1,1,4,48,640]{4,3,2,1,0:T(8,128)(2,1)S(1)}, bf16[1,1,4,48,640]{4,3,2,1,0:T(8,128)(2,1)}, u32[]{:S(2)}) copy-start(bf16[1,1,4,48,640]{4,3,2,1,0:T(8,128)(2,1)} %param.7) | copy-start | bytes 737284
  20.8 7.2 %collective-permute-start.5 = (bf16[1,16,3168]{2,1,0:T(8,128)(2,1)S(1)}, bf16[1,16,3168]{2,1,0:T(8,128)(2,1)S(1)}, u32[]{:S(2)}, u32[]{:S(2)}) collective-permute-start(bf16[1,16,3168]{2,1,0:T(8,128)(2,1)S(1)} %get-tuple-element.37), channel_id=1, source_target_pairs={{0,2},{2,0},{4,6},{6,4},{8,10},{10,8},{12,14},{14,12},{16,18},{18,... | collective-permute-start | bytes 304136 | tf_op jit(solution)/shard_map/ppermute | solution.py:59
  22.4 6.7 %collective-permute-start.6 = (bf16[1,16,3168]{2,1,0:T(8,128)(2,1)S(1)}, bf16[1,16,3168]{2,1,0:T(8,128)(2,1)S(1)}, u32[]{:S(2)}, u32[]{:S(2)}) collective-permute-start(bf16[1,16,3168]{2,1,0:T(8,128)(2,1)S(1)} %get-tuple-element.38), channel_id=1, source_target_pairs={{0,4},{2,6},{4,0},{6,2},{8,12},{10,14},{12,8},{14,10},{16,20},{18,... | collective-permute-start | bytes 304136 | tf_op jit(solution)/shard_map/ppermute | solution.py:59
  23.1 6.0 %collective-permute-start.7 = (bf16[1,16,3168]{2,1,0:T(8,128)(2,1)S(1)}, bf16[1,16,3168]{2,1,0:T(8,128)(2,1)S(1)}, u32[]{:S(2)}, u32[]{:S(2)}) collective-permute-start(bf16[1,16,3168]{2,1,0:T(8,128)(2,1)S(1)} %get-tuple-element.39), channel_id=1, source_target_pairs={{0,6},{2,4},{4,2},{6,0},{8,14},{10,12},{12,10},{14,8},{16,22},{18,... | collective-permute-start | bytes 304136 | tf_op jit(solution)/shard_map/ppermute | solution.py:59
  24.4 8.9 %collective-permute-start.11 = (bf16[264,640]{1,0:T(8,128)(2,1)S(1)}, bf16[264,640]{1,0:T(8,128)(2,1)S(1)}, u32[]{:S(2)}, u32[]{:S(2)}) collective-permute-start(bf16[264,640]{1,0:T(8,128)(2,1)S(1)} %collective-permute-done.4.refs_5_), channel_id=1, source_target_pairs={{0,8},{2,10},{4,12},{6,14},{8,0},{10,2},{12,4},{14,6},{16,24},{18,... | collective-permute-start | bytes 1013768 | tf_op jit(solution)/shard_map/ppermute | solution.py:49
  26.5 9.7 %collective-permute-start.8 = (bf16[2,16,3168]{2,1,0:T(8,128)(2,1)S(1)}, bf16[2,16,3168]{2,1,0:T(8,128)(2,1)S(1)}, u32[]{:S(2)}, u32[]{:S(2)}) collective-permute-start(bf16[2,16,3168]{2,1,0:T(8,128)(2,1)S(1)} %get-tuple-element.43), channel_id=1, source_target_pairs={{0,2},{2,0},{4,6},{6,4},{8,10},{10,8},{12,14},{14,12},{16,18},{18,... | collective-permute-start | bytes 608264 | tf_op jit(solution)/shard_map/ppermute | solution.py:59
  28.0 9.8 %collective-permute-start.9 = (bf16[2,16,3168]{2,1,0:T(8,128)(2,1)S(1)}, bf16[2,16,3168]{2,1,0:T(8,128)(2,1)S(1)}, u32[]{:S(2)}, u32[]{:S(2)}) collective-permute-start(bf16[2,16,3168]{2,1,0:T(8,128)(2,1)S(1)} %get-tuple-element.45), channel_id=1, source_target_pairs={{0,4},{2,6},{4,0},{6,2},{8,12},{10,14},{12,8},{14,10},{16,20},{18,... | collective-permute-start | bytes 608264 | tf_op jit(solution)/shard_map/ppermute | solution.py:59
  29.1 10.1 %copy-start.1 = (bf16[1,1,4,48,4224]{4,3,2,1,0:T(8,128)(2,1)S(1)}, bf16[1,1,4,48,4224]{4,3,2,1,0:T(8,128)(2,1)}, u32[]{:S(2)}) copy-start(bf16[1,1,4,48,4224]{4,3,2,1,0:T(8,128)(2,1)} %param.6) | copy-start | bytes 4866052
  29.1 10.1 %copy-start.5 = (f32[1,4224]{1,0:T(1,128)S(1)}, f32[1,4224]{1,0:T(1,128)}, u32[]{:S(2)}) copy-start(f32[1,4224]{1,0:T(1,128)} %gain_ref.3) | copy-start | bytes 50692
  29.1 10.1 %collective-permute-start.10 = (bf16[2,16,3168]{2,1,0:T(8,128)(2,1)S(1)}, bf16[2,16,3168]{2,1,0:T(8,128)(2,1)S(1)}, u32[]{:S(2)}, u32[]{:S(2)}) collective-permute-start(bf16[2,16,3168]{2,1,0:T(8,128)(2,1)S(1)} %get-tuple-element.47), channel_id=1, source_target_pairs={{0,6},{2,4},{4,2},{6,0},{8,14},{10,12},{12,10},{14,8},{16,22},{18,... | collective-permute-start | bytes 608264 | tf_op jit(solution)/shard_map/ppermute | solution.py:59
  34.2 8.2 %copy-start.2 = (bf16[1,4,48,4224]{3,2,1,0:T(8,128)(2,1)S(1)}, bf16[1,4,48,4224]{3,2,1,0:T(8,128)(2,1)}, u32[]{:S(2)}) copy-start(bf16[1,4,48,4224]{3,2,1,0:T(8,128)(2,1)} %param.8) | copy-start | bytes 4866052
  34.2 6.8 %collective-permute-start.12 = (bf16[1,16,3168]{2,1,0:T(8,128)(2,1)S(1)}, bf16[1,16,3168]{2,1,0:T(8,128)(2,1)S(1)}, u32[]{:S(2)}, u32[]{:S(2)}) collective-permute-start(bf16[1,16,3168]{2,1,0:T(8,128)(2,1)S(1)} %get-tuple-element.52), channel_id=1, source_target_pairs={{0,2},{2,0},{4,6},{6,4},{8,10},{10,8},{12,14},{14,12},{16,18},{18,... | collective-permute-start | bytes 304136 | tf_op jit(solution)/shard_map/ppermute | solution.py:59
  35.8 6.6 %collective-permute-start.13 = (bf16[1,16,3168]{2,1,0:T(8,128)(2,1)S(1)}, bf16[1,16,3168]{2,1,0:T(8,128)(2,1)S(1)}, u32[]{:S(2)}, u32[]{:S(2)}) collective-permute-start(bf16[1,16,3168]{2,1,0:T(8,128)(2,1)S(1)} %get-tuple-element.53), channel_id=1, source_target_pairs={{0,4},{2,6},{4,0},{6,2},{8,12},{10,14},{12,8},{14,10},{16,20},{18,... | collective-permute-start | bytes 304136 | tf_op jit(solution)/shard_map/ppermute | solution.py:59
  36.2 6.2 %collective-permute-start.14 = (bf16[1,16,3168]{2,1,0:T(8,128)(2,1)S(1)}, bf16[1,16,3168]{2,1,0:T(8,128)(2,1)S(1)}, u32[]{:S(2)}, u32[]{:S(2)}) collective-permute-start(bf16[1,16,3168]{2,1,0:T(8,128)(2,1)S(1)} %get-tuple-element.54), channel_id=1, source_target_pairs={{0,6},{2,4},{4,2},{6,0},{8,14},{10,12},{12,10},{14,8},{16,22},{18,... | collective-permute-start | bytes 304136 | tf_op jit(solution)/shard_map/ppermute | solution.py:59
  44.4 3.9 %collective-permute-start.15 = (bf16[192,4224]{1,0:T(8,128)(2,1)}, bf16[192,4224]{1,0:T(8,128)(2,1)}, u32[]{:S(2)}, u32[]{:S(2)}) collective-permute-start(bf16[192,4224]{1,0:T(8,128)(2,1)} %get-tuple-element.56.result_ref), channel_id=1, source_target_pairs={{1,0},{0,1},{3,2},{2,3},{5,4},{4,5},{7,6},{6,7},{9,8},{8,9},{11,10... | collective-permute-start | bytes 4866056 | tf_op jit(solution)/shard_map/ppermute | solution.py:509
  44.4 11.2 %all-to-all-start = ((f32[16,1,264]{2,1,0:T(1,128)}), f32[16,1,264]{2,1,0:T(1,128)S(1)}, u32[]{:S(2)}, u32[]{:S(2)}) async-start(f32[16,1,264]{2,1,0:T(1,128)} %get-tuple-element.55), calls=%async_computation | async-start | bytes 49152 | tf_op jit(solution)/shard_map/all_to_all | solution.py:512

commit v5 on v4

--- a/solution.py
+++ b/solution.py
@@ -217,7 +217,7 @@
     ]
     scratch = [pltpu.VMEM((line * plane,) + pieces[0].shape[1:], jnp.bfloat16)]
     return pl.pallas_call(
-        functools.partial(early_kernel, line, plane, groups, fold, math.gcd(rows, 32)),
+        functools.partial(early_kernel, line, plane, groups, fold, math.gcd(rows, 48)),
         out_shape=outs,
         in_specs=[vmem] * (3 + len(pieces)),
         out_specs=[vmem] * len(outs),

time: 56.4 us -> 56.4 us (level)
  no operation moved by 1% of the time
where the time goes in v5:
time: 56.4 us; the launch traced here: 56.2 us
  starting transfers between devices  24.4 us (43%)
  waiting for transfers between devices  16.9 us (30%)
  Pallas kernels  12.1 us (21%)
  local copies, waits for them, and re-layouts  2.1 us (4%)
  between operations  0.73 us (1%)
    ppermute x12, starting transfers between devices, along_plane(): return lax.ppermute(value, 'dp', pairs)  14.4 us
    ppermute x12, waiting for transfers between devices, along_plane(): return lax.ppermute(value, 'dp', pairs)  9.13 us
    ppermute x3, starting transfers between devices, along_line(): return lax.ppermute(value, 'dp', pairs)  6.13 us
    all_to_all x1, waiting for transfers between devices, on_device(): lax.all_to_all(gain_blocks, 'dp', split_axis=0, concat_axis=0, tiled=True)  5.04 us
    all_to_all x1, starting transfers between devices, on_device(): lax.all_to_all(gain_blocks, 'dp', split_axis=0, concat_axis=0, tiled=True)  3.78 us
    pallas_call x3, Pallas kernels, products(): pl.pallas_call(functools.partial(product_kernel, len(tokens), count, fold...  3.43 us
    ppermute x3, waiting for transfers between devices, along_line(): return lax.ppermute(value, 'dp', pairs)  2.66 us
    pallas_call x1, Pallas kernels, hand_on(): pl.pallas_call(functools.partial(hand_kernel, turn, chunk), out_shape=jax...  2.3 us
  transfers between devices with their start and end apart: 17, of which 8 were waited for; matrix products, arithmetic and copies ran while one was open for 0% of the time, Pallas kernels for 17%

profile of v5, /device:TPU:0, one launch (start us, length us, event | category | flops | bytes accessed | tf_op | source)
XLA Modules:
  0.0 56.2 jit_solution(16513329781919210674)
XLA Ops:
  0.6 4.1 %collective-permute-start.4 = (bf16[264,640]{1,0:T(8,128)(2,1)}, bf16[264,640]{1,0:T(8,128)(2,1)S(1)}, u32[]{:S(2)}, u32[]{:S(2)}) collective-permute-start(bf16[264,640]{1,0:T(8,128)(2,1)} %bitcast.10), channel_id=1, source_target_pairs={{0,16},{2,18},{4,20},{6,22},{8,24},{10,26},{12,28},{14,30},{16,0},... | collective-permute-start | bytes 1013768 | tf_op jit(solution)/shard_map/ppermute | solution.py:49
  4.7 1.6 %collective-permute-start.3 = (bf16[264,640]{1,0:T(8,128)(2,1)}, bf16[264,640]{1,0:T(8,128)(2,1)S(1)}, u32[]{:S(2)}, u32[]{:S(2)}) collective-permute-start(bf16[264,640]{1,0:T(8,128)(2,1)} %bitcast.11), channel_id=1, source_target_pairs={{0,8},{2,10},{4,12},{6,14},{8,0},{10,2},{12,4},{14,6},{16,24},{18,... | collective-permute-start | bytes 1013768 | tf_op jit(solution)/shard_map/ppermute | solution.py:49
  6.3 2.4 %collective-permute-start.2 = (bf16[192,640]{1,0:T(8,128)(2,1)}, bf16[192,640]{1,0:T(8,128)(2,1)S(1)}, u32[]{:S(2)}, u32[]{:S(2)}) collective-permute-start(bf16[192,640]{1,0:T(8,128)(2,1)} %bitcast.13), channel_id=1, source_target_pairs={{0,6},{2,4},{4,2},{6,0},{8,14},{10,12},{12,10},{14,8},{16,22},{18,... | collective-permute-start | bytes 737288 | tf_op jit(solution)/shard_map/ppermute | solution.py:59
  8.8 0.5 collective-permute-start.1
  9.3 0.5 collective-permute-start
  9.8 1.4 %copy-done = bf16[1,1,4,48,4224]{4,3,2,1,0:T(8,128)(2,1)S(1)} copy-done((bf16[1,1,4,48,4224]{4,3,2,1,0:T(8,128)(2,1)S(1)}, bf16[1,1,4,48,4224]{4,3,2,1,0:T(8,128)(2,1)}, u32[]{:S(2)}) %copy-start) | copy-done | bytes 1622040
  11.2 0.7 %copy-done.6 = s32[1,4]{1,0:T(1,128)S(1)} copy-done((s32[1,4]{1,0:T(1,128)S(1)}, s32[1,4]{1,0:T(1,128)}, u32[]{:S(2)}) %copy-start.6) | copy-done | bytes 40
  11.9 2.0 %live_inverse.1.inverse_ref = f32[192,128]{1,0:T(8,128)S(1)} custom-call(s32[4]{0:T(128)S(1)} %bitcast.19, bf16[192,4224]{1,0:T(8,128)(2,1)S(1)} %bitcast.6), custom_call_target="tpu_custom_call" | custom-call | flops 1622016 | bytes 1622016 | tf_op jit(solution)/shard_map/live_inverse/pallas_call | solution.py:132
  13.9 2.5 %collective-permute-done.2.refs_3_ = bf16[192,640]{1,0:T(8,128)(2,1)S(1)} collective-permute-done((bf16[192,640]{1,0:T(8,128)(2,1)}, bf16[192,640]{1,0:T(8,128)(2,1)S(1)}, u32[]{:S(2)}, u32[]{:S(2)}) %collective-permute-start.2) | collective-permute-done | bytes 245792 | tf_op jit(solution)/shard_map/ppermute | solution.py:59
  16.4 3.5 %collective-permute-done.1.refs_2_ = bf16[192,640]{1,0:T(8,128)(2,1)S(1)} collective-permute-done((bf16[192,640]{1,0:T(8,128)(2,1)}, bf16[192,640]{1,0:T(8,128)(2,1)S(1)}, u32[]{:S(2)}, u32[]{:S(2)}) %collective-permute-start.1) | collective-permute-done | bytes 245792 | tf_op jit(solution)/shard_map/ppermute | solution.py:59
  19.8 0.1 collective-permute-done.refs_1_
  19.9 0.0 copy-done.3
  19.9 0.0 copy-done.4
  19.9 0.9 %token_products.3 = (bf16[1,16,3168]{2,1,0:T(8,128)(2,1)S(1)}, bf16[1,16,3168]{2,1,0:T(8,128)(2,1)S(1)}, bf16[1,16,3168]{2,1,0:T(8,128)(2,1)S(1)}, bf16[1,16,3168]{2,1,0:T(8,128)(2,1)S(1)}) custom-call(bf16[192,640]{1,0:T(8,128)(2,1)S(1)} %bitcast.16, bf16[192,640]{1,0:T(8,128)(2,1)S(1)} %collective-permute-done.refs_1_, ...), custom_call_target="tpu_custom_call" | custom-call | flops 259522560 | bytes 1726464 | tf_op jit(solution)/shard_map/token_products/pallas_call | solution.py:85
  20.8 1.6 %collective-permute-start.5 = (bf16[1,16,3168]{2,1,0:T(8,128)(2,1)S(1)}, bf16[1,16,3168]{2,1,0:T(8,128)(2,1)S(1)}, u32[]{:S(2)}, u32[]{:S(2)}) collective-permute-start(bf16[1,16,3168]{2,1,0:T(8,128)(2,1)S(1)} %get-tuple-element.37), channel_id=1, source_target_pairs={{0,2},{2,0},{4,6},{6,4},{8,10},{10,8},{12,14},{14,12},{16,18},{18,... | collective-permute-start | bytes 304136 | tf_op jit(solution)/shard_map/ppermute | solution.py:59
  22.4 0.7 %collective-permute-start.6 = (bf16[1,16,3168]{2,1,0:T(8,128)(2,1)S(1)}, bf16[1,16,3168]{2,1,0:T(8,128)(2,1)S(1)}, u32[]{:S(2)}, u32[]{:S(2)}) collective-permute-start(bf16[1,16,3168]{2,1,0:T(8,128)(2,1)S(1)} %get-tuple-element.38), channel_id=1, source_target_pairs={{0,4},{2,6},{4,0},{6,2},{8,12},{10,14},{12,8},{14,10},{16,20},{18,... | collective-permute-start | bytes 304136 | tf_op jit(solution)/shard_map/ppermute | solution.py:59
  23.1 1.3 %collective-permute-start.7 = (bf16[1,16,3168]{2,1,0:T(8,128)(2,1)S(1)}, bf16[1,16,3168]{2,1,0:T(8,128)(2,1)S(1)}, u32[]{:S(2)}, u32[]{:S(2)}) collective-permute-start(bf16[1,16,3168]{2,1,0:T(8,128)(2,1)S(1)} %get-tuple-element.39), channel_id=1, source_target_pairs={{0,6},{2,4},{4,2},{6,0},{8,14},{10,12},{12,10},{14,8},{16,22},{18,... | collective-permute-start | bytes 304136 | tf_op jit(solution)/shard_map/ppermute | solution.py:59
  24.4 0.0 collective-permute-done.4.refs_5_
  24.4 0.5 collective-permute-start.11
  24.8 0.0 collective-permute-done.3.refs_4_
  24.8 1.6 %token_products.4 = (bf16[2,16,3168]{2,1,0:T(8,128)(2,1)S(1)}, bf16[2,16,3168]{2,1,0:T(8,128)(2,1)S(1)}, bf16[2,16,3168]{2,1,0:T(8,128)(2,1)S(1)}, bf16[2,16,3168]{2,1,0:T(8,128)(2,1)S(1)}) custom-call(bf16[192,640]{1,0:T(8,128)(2,1)S(1)} %bitcast.17, bf16[192,640]{1,0:T(8,128)(2,1)S(1)} %collective-permute-done.refs_1_, ...), custom_call_target="tpu_custom_call" | custom-call | flops 5190451200 | bytes 2469888 | tf_op jit(solution)/shard_map/token_products/pallas_call | solution.py:85
  26.5 1.6 %collective-permute-start.8 = (bf16[2,16,3168]{2,1,0:T(8,128)(2,1)S(1)}, bf16[2,16,3168]{2,1,0:T(8,128)(2,1)S(1)}, u32[]{:S(2)}, u32[]{:S(2)}) collective-permute-start(bf16[2,16,3168]{2,1,0:T(8,128)(2,1)S(1)} %get-tuple-element.43), channel_id=1, source_target_pairs={{0,2},{2,0},{4,6},{6,4},{8,10},{10,8},{12,14},{14,12},{16,18},{18,... | collective-permute-start | bytes 608264 | tf_op jit(solution)/shard_map/ppermute | solution.py:59
  28.0 0.0 collective-permute-done.5.refs_2_
  28.0 0.7 %collective-permute-start.9 = (bf16[2,16,3168]{2,1,0:T(8,128)(2,1)S(1)}, bf16[2,16,3168]{2,1,0:T(8,128)(2,1)S(1)}, u32[]{:S(2)}, u32[]{:S(2)}) collective-permute-start(bf16[2,16,3168]{2,1,0:T(8,128)(2,1)S(1)} %get-tuple-element.45), channel_id=1, source_target_pairs={{0,4},{2,6},{4,0},{6,2},{8,12},{10,14},{12,8},{14,10},{16,20},{18,... | collective-permute-start | bytes 608264 | tf_op jit(solution)/shard_map/ppermute | solution.py:59
  28.8 0.3 collective-permute-done.6.refs_4_
  29.1 0.0 collective-permute-done.7.refs_6_
  29.1 1.6 %collective-permute-start.10 = (bf16[2,16,3168]{2,1,0:T(8,128)(2,1)S(1)}, bf16[2,16,3168]{2,1,0:T(8,128)(2,1)S(1)}, u32[]{:S(2)}, u32[]{:S(2)}) collective-permute-start(bf16[2,16,3168]{2,1,0:T(8,128)(2,1)S(1)} %get-tuple-element.47), channel_id=1, source_target_pairs={{0,6},{2,4},{4,2},{6,0},{8,14},{10,12},{12,10},{14,8},{16,22},{18,... | collective-permute-start | bytes 608264 | tf_op jit(solution)/shard_map/ppermute | solution.py:59
  30.7 2.7 %collective-permute-done.11.refs_4_ = bf16[264,640]{1,0:T(8,128)(2,1)S(1)} collective-permute-done((bf16[264,640]{1,0:T(8,128)(2,1)S(1)}, bf16[264,640]{1,0:T(8,128)(2,1)S(1)}, u32[]{:S(2)}, u32[]{:S(2)}) %collective-permute-start.11) | collective-permute-done | bytes 337952 | tf_op jit(solution)/shard_map/ppermute | solution.py:49
  33.3 0.9 %token_products.5 = (bf16[1,16,3168]{2,1,0:T(8,128)(2,1)S(1)}, bf16[1,16,3168]{2,1,0:T(8,128)(2,1)S(1)}, bf16[1,16,3168]{2,1,0:T(8,128)(2,1)S(1)}, bf16[1,16,3168]{2,1,0:T(8,128)(2,1)S(1)}) custom-call(bf16[192,640]{1,0:T(8,128)(2,1)S(1)} %bitcast.18, bf16[192,640]{1,0:T(8,128)(2,1)S(1)} %collective-permute-done.refs_1_, ...), custom_call_target="tpu_custom_call" | custom-call | flops 2595225600 | bytes 1726464 | tf_op jit(solution)/shard_map/token_products/pallas_call | solution.py:85
  34.2 0.0 copy-start.2
  34.2 1.6 %collective-permute-start.12 = (bf16[1,16,3168]{2,1,0:T(8,128)(2,1)S(1)}, bf16[1,16,3168]{2,1,0:T(8,128)(2,1)S(1)}, u32[]{:S(2)}, u32[]{:S(2)}) collective-permute-start(bf16[1,16,3168]{2,1,0:T(8,128)(2,1)S(1)} %get-tuple-element.52), channel_id=1, source_target_pairs={{0,2},{2,0},{4,6},{6,4},{8,10},{10,8},{12,14},{14,12},{16,18},{18,... | collective-permute-start | bytes 304136 | tf_op jit(solution)/shard_map/ppermute | solution.py:59
  35.8 0.4 collective-permute-start.13
  36.2 0.0 collective-permute-done.8.refs_3_
  36.2 1.6 %collective-permute-start.14 = (bf16[1,16,3168]{2,1,0:T(8,128)(2,1)S(1)}, bf16[1,16,3168]{2,1,0:T(8,128)(2,1)S(1)}, u32[]{:S(2)}, u32[]{:S(2)}) collective-permute-start(bf16[1,16,3168]{2,1,0:T(8,128)(2,1)S(1)} %get-tuple-element.54), channel_id=1, source_target_pairs={{0,6},{2,4},{4,2},{6,0},{8,14},{10,12},{12,10},{14,8},{16,22},{18,... | collective-permute-start | bytes 304136 | tf_op jit(solution)/shard_map/ppermute | solution.py:59
  37.8 0.0 collective-permute-done.9.refs_5_
  37.8 1.4 %collective-permute-done.10.refs_7_ = bf16[2,16,3168]{2,1,0:T(8,128)(2,1)S(1)} collective-permute-done((bf16[2,16,3168]{2,1,0:T(8,128)(2,1)S(1)}, bf16[2,16,3168]{2,1,0:T(8,128)(2,1)S(1)}, u32[]{:S(2)}, u32[]{:S(2)}) %collective-permute-start.10) | collective-permute-done | bytes 202784 | tf_op jit(solution)/shard_map/ppermute | solution.py:59
  39.2 0.0 copy-done.5
  39.2 1.8 %placed_early.1 = (bf16[192,4224]{1,0:T(8,128)(2,1)S(1)}, f32[192,128]{1,0:T(8,128)S(1)}, f32[8,4224]{1,0:T(8,128)S(1)}) custom-call(f32[192,128]{1,0:T(8,128)S(1)} %live_inverse.1.inverse_ref, bf16[192,4224]{1,0:T(8,128)(2,1)S(1)} %bitcast.7, f32[1,4224]{1,0:T(1,128)S(1)} %copy-done.5, bf16[1,16,3168]{2,1,0:T(8,128)(2,1)S(1)} %get-tuple-element.40.refs_0_, ...), custom_call_target="tpu_custom_call" | custom-call | flops 6488064 | bytes 6488064 | tf_op jit(solution)/shard_map/placed_early/pallas_call | solution.py:219
  41.1 0.0 collective-permute-done.12.refs_1_
  41.1 1.3 %collective-permute-done.13.refs_2_ = bf16[1,16,3168]{2,1,0:T(8,128)(2,1)S(1)} collective-permute-done((bf16[1,16,3168]{2,1,0:T(8,128)(2,1)S(1)}, bf16[1,16,3168]{2,1,0:T(8,128)(2,1)S(1)}, u32[]{:S(2)}, u32[]{:S(2)}) %collective-permute-start.13) | collective-permute-done | bytes 101408 | tf_op jit(solution)/shard_map/ppermute | solution.py:59
  42.4 0.0 collective-permute-done.14.refs_3_
  42.4 1.9 %norm_backward.1 = (bf16[192,4224]{1,0:T(8,128)(2,1)}, f32[192,4224]{1,0:T(8,128)S(1)}, f32[16,1,264]{2,1,0:T(1,128)}) custom-call(bf16[192,4224]{1,0:T(8,128)(2,1)S(1)} %get-tuple-element.48.early_ref, f32[192,128]{1,0:T(8,128)S(1)} %get-tuple-element.49.early_pulls, f32[8,4224]{1,0:T(8,128)S(1)} %get-tuple-element.50.early_gains, ...), custom_call_target="tpu_custom_call" | custom-call | flops 12976128 | bytes 9732096 | tf_op jit(solution)/shard_map/norm_backward/pallas_call | solution.py:349
  44.4 0.1 collective-permute-start.15
  44.4 3.8 %all-to-all-start = ((f32[16,1,264]{2,1,0:T(1,128)}), f32[16,1,264]{2,1,0:T(1,128)S(1)}, u32[]{:S(2)}, u32[]{:S(2)}) async-start(f32[16,1,264]{2,1,0:T(1,128)} %get-tuple-element.55), calls=%async_computation | async-start | bytes 49152 | tf_op jit(solution)/shard_map/all_to_all | solution.py:512
  48.2 0.0 collective-permute-done.15.incoming_ref
  48.2 2.3 %hand_on.1 = bf16[192,4224]{1,0:T(8,128)(2,1)} custom-call(bf16[192,4224]{1,0:T(8,128)(2,1)} %collective-permute-done.15.incoming_ref, f32[192,4224]{1,0:T(8,128)S(1)} %get-tuple-element.57.local_ref, bf16[192,4224]{1,0:T(8,128)(2,1)} %get-tuple-element.56.result_ref), custom_call_target="tpu_custom_call" | custom-call | tf_op jit(solution)/shard_map/hand_on/pallas_call | solution.py:406
  50.5 5.0 %all-to-all-done.parts_ref = f32[16,1,264]{2,1,0:T(1,128)S(1)} async-done(((f32[16,1,264]{2,1,0:T(1,128)}), f32[16,1,264]{2,1,0:T(1,128)S(1)}, u32[]{:S(2)}, u32[]{:S(2)}) %all-to-all-start) | async-done | bytes 16928 | tf_op jit(solution)/shard_map/all_to_all | solution.py:512
  55.6 0.6 %sum_scaled.1 = f32[1,264]{1,0:T(1,128)} custom-call(f32[16,1,264]{2,1,0:T(1,128)S(1)} %all-to-all-done.parts_ref), custom_call_target="tpu_custom_call" | custom-call | flops 4224 | bytes 16896 | tf_op jit(solution)/shard_map/sum_scaled/pallas_call | solution.py:432
  (8 shorter events, 0.0 us)
Async XLA Ops:
  0.6 23.8 %collective-permute-start.4 = (bf16[264,640]{1,0:T(8,128)(2,1)}, bf16[264,640]{1,0:T(8,128)(2,1)S(1)}, u32[]{:S(2)}, u32[]{:S(2)}) collective-permute-start(bf16[264,640]{1,0:T(8,128)(2,1)} %bitcast.10), channel_id=1, source_target_pairs={{0,16},{2,18},{4,20},{6,22},{8,24},{10,26},{12,28},{14,30},{16,0},... | collective-permute-start | bytes 1013768 | tf_op jit(solution)/shard_map/ppermute | solution.py:49
  4.7 20.1 %collective-permute-start.3 = (bf16[264,640]{1,0:T(8,128)(2,1)}, bf16[264,640]{1,0:T(8,128)(2,1)S(1)}, u32[]{:S(2)}, u32[]{:S(2)}) collective-permute-start(bf16[264,640]{1,0:T(8,128)(2,1)} %bitcast.11), channel_id=1, source_target_pairs={{0,8},{2,10},{4,12},{6,14},{8,0},{10,2},{12,4},{14,6},{16,24},{18,... | collective-permute-start | bytes 1013768 | tf_op jit(solution)/shard_map/ppermute | solution.py:49
  6.3 10.0 %collective-permute-start.2 = (bf16[192,640]{1,0:T(8,128)(2,1)}, bf16[192,640]{1,0:T(8,128)(2,1)S(1)}, u32[]{:S(2)}, u32[]{:S(2)}) collective-permute-start(bf16[192,640]{1,0:T(8,128)(2,1)} %bitcast.13), channel_id=1, source_target_pairs={{0,6},{2,4},{4,2},{6,0},{8,14},{10,12},{12,10},{14,8},{16,22},{18,... | collective-permute-start | bytes 737288 | tf_op jit(solution)/shard_map/ppermute | solution.py:59
  8.8 11.1 %collective-permute-start.1 = (bf16[192,640]{1,0:T(8,128)(2,1)}, bf16[192,640]{1,0:T(8,128)(2,1)S(1)}, u32[]{:S(2)}, u32[]{:S(2)}) collective-permute-start(bf16[192,640]{1,0:T(8,128)(2,1)} %bitcast.14), channel_id=1, source_target_pairs={{0,4},{2,6},{4,0},{6,2},{8,12},{10,14},{12,8},{14,10},{16,20},{18,... | collective-permute-start | bytes 737288 | tf_op jit(solution)/shard_map/ppermute | solution.py:59
  9.3 10.7 %collective-permute-start = (bf16[192,640]{1,0:T(8,128)(2,1)}, bf16[192,640]{1,0:T(8,128)(2,1)S(1)}, u32[]{:S(2)}, u32[]{:S(2)}) collective-permute-start(bf16[192,640]{1,0:T(8,128)(2,1)} %bitcast.15), channel_id=1, source_target_pairs={{0,2},{2,0},{4,6},{6,4},{8,10},{10,8},{12,14},{14,12},{16,18},{18,... | collective-permute-start | bytes 737288 | tf_op jit(solution)/shard_map/ppermute | solution.py:59
  9.8 1.4 %copy-start = (bf16[1,1,4,48,4224]{4,3,2,1,0:T(8,128)(2,1)S(1)}, bf16[1,1,4,48,4224]{4,3,2,1,0:T(8,128)(2,1)}, u32[]{:S(2)}) copy-start(bf16[1,1,4,48,4224]{4,3,2,1,0:T(8,128)(2,1)} %param.6) | copy-start | bytes 4866052
  11.2 0.7 %copy-start.6 = (s32[1,4]{1,0:T(1,128)S(1)}, s32[1,4]{1,0:T(1,128)}, u32[]{:S(2)}) copy-start(s32[1,4]{1,0:T(1,128)} %param.11) | copy-start | bytes 52
  11.9 8.0 %copy-start.3 = (bf16[1,264,640]{2,1,0:T(8,128)(2,1)S(1)}, bf16[1,264,640]{2,1,0:T(8,128)(2,1)}, u32[]{:S(2)}) copy-start(bf16[1,264,640]{2,1,0:T(8,128)(2,1)} %param.10) | copy-start | bytes 1013764
  11.9 8.0 %copy-start.4 = (bf16[1,1,4,48,640]{4,3,2,1,0:T(8,128)(2,1)S(1)}, bf16[1,1,4,48,640]{4,3,2,1,0:T(8,128)(2,1)}, u32[]{:S(2)}) copy-start(bf16[1,1,4,48,640]{4,3,2,1,0:T(8,128)(2,1)} %param.7) | copy-start | bytes 737284
  20.8 7.2 %collective-permute-start.5 = (bf16[1,16,3168]{2,1,0:T(8,128)(2,1)S(1)}, bf16[1,16,3168]{2,1,0:T(8,128)(2,1)S(1)}, u32[]{:S(2)}, u32[]{:S(2)}) collective-permute-start(bf16[1,16,3168]{2,1,0:T(8,128)(2,1)S(1)} %get-tuple-element.37), channel_id=1, source_target_pairs={{0,2},{2,0},{4,6},{6,4},{8,10},{10,8},{12,14},{14,12},{16,18},{18,... | collective-permute-start | bytes 304136 | tf_op jit(solution)/shard_map/ppermute | solution.py:59
  22.4 6.7 %collective-permute-start.6 = (bf16[1,16,3168]{2,1,0:T(8,128)(2,1)S(1)}, bf16[1,16,3168]{2,1,0:T(8,128)(2,1)S(1)}, u32[]{:S(2)}, u32[]{:S(2)}) collective-permute-start(bf16[1,16,3168]{2,1,0:T(8,128)(2,1)S(1)} %get-tuple-element.38), channel_id=1, source_target_pairs={{0,4},{2,6},{4,0},{6,2},{8,12},{10,14},{12,8},{14,10},{16,20},{18,... | collective-permute-start | bytes 304136 | tf_op jit(solution)/shard_map/ppermute | solution.py:59
  23.1 6.0 %collective-permute-start.7 = (bf16[1,16,3168]{2,1,0:T(8,128)(2,1)S(1)}, bf16[1,16,3168]{2,1,0:T(8,128)(2,1)S(1)}, u32[]{:S(2)}, u32[]{:S(2)}) collective-permute-start(bf16[1,16,3168]{2,1,0:T(8,128)(2,1)S(1)} %get-tuple-element.39), channel_id=1, source_target_pairs={{0,6},{2,4},{4,2},{6,0},{8,14},{10,12},{12,10},{14,8},{16,22},{18,... | collective-permute-start | bytes 304136 | tf_op jit(solution)/shard_map/ppermute | solution.py:59
  24.4 8.9 %collective-permute-start.11 = (bf16[264,640]{1,0:T(8,128)(2,1)S(1)}, bf16[264,640]{1,0:T(8,128)(2,1)S(1)}, u32[]{:S(2)}, u32[]{:S(2)}) collective-permute-start(bf16[264,640]{1,0:T(8,128)(2,1)S(1)} %collective-permute-done.4.refs_5_), channel_id=1, source_target_pairs={{0,8},{2,10},{4,12},{6,14},{8,0},{10,2},{12,4},{14,6},{16,24},{18,... | collective-permute-start | bytes 1013768 | tf_op jit(solution)/shard_map/ppermute | solution.py:49
  26.5 9.7 %collective-permute-start.8 = (bf16[2,16,3168]{2,1,0:T(8,128)(2,1)S(1)}, bf16[2,16,3168]{2,1,0:T(8,128)(2,1)S(1)}, u32[]{:S(2)}, u32[]{:S(2)}) collective-permute-start(bf16[2,16,3168]{2,1,0:T(8,128)(2,1)S(1)} %get-tuple-element.43), channel_id=1, source_target_pairs={{0,2},{2,0},{4,6},{6,4},{8,10},{10,8},{12,14},{14,12},{16,18},{18,... | collective-permute-start | bytes 608264 | tf_op jit(solution)/shard_map/ppermute | solution.py:59
  28.0 9.8 %collective-permute-start.9 = (bf16[2,16,3168]{2,1,0:T(8,128)(2,1)S(1)}, bf16[2,16,3168]{2,1,0:T(8,128)(2,1)S(1)}, u32[]{:S(2)}, u32[]{:S(2)}) collective-permute-start(bf16[2,16,3168]{2,1,0:T(8,128)(2,1)S(1)} %get-tuple-element.45), channel_id=1, source_target_pairs={{0,4},{2,6},{4,0},{6,2},{8,12},{10,14},{12,8},{14,10},{16,20},{18,... | collective-permute-start | bytes 608264 | tf_op jit(solution)/shard_map/ppermute | solution.py:59
  29.1 10.1 %copy-start.1 = (bf16[1,1,4,48,4224]{4,3,2,1,0:T(8,128)(2,1)S(1)}, bf16[1,1,4,48,4224]{4,3,2,1,0:T(8,128)(2,1)}, u32[]{:S(2)}) copy-start(bf16[1,1,4,48,4224]{4,3,2,1,0:T(8,128)(2,1)} %param.6) | copy-start | bytes 4866052
  29.1 10.1 %copy-start.5 = (f32[1,4224]{1,0:T(1,128)S(1)}, f32[1,4224]{1,0:T(1,128)}, u32[]{:S(2)}) copy-start(f32[1,4224]{1,0:T(1,128)} %gain_ref.3) | copy-start | bytes 50692
  29.1 10.1 %collective-permute-start.10 = (bf16[2,16,3168]{2,1,0:T(8,128)(2,1)S(1)}, bf16[2,16,3168]{2,1,0:T(8,128)(2,1)S(1)}, u32[]{:S(2)}, u32[]{:S(2)}) collective-permute-start(bf16[2,16,3168]{2,1,0:T(8,128)(2,1)S(1)} %get-tuple-element.47), channel_id=1, source_target_pairs={{0,6},{2,4},{4,2},{6,0},{8,14},{10,12},{12,10},{14,8},{16,22},{18,... | collective-permute-start | bytes 608264 | tf_op jit(solution)/shard_map/ppermute | solution.py:59
  34.2 8.2 %copy-start.2 = (bf16[1,4,48,4224]{3,2,1,0:T(8,128)(2,1)S(1)}, bf16[1,4,48,4224]{3,2,1,0:T(8,128)(2,1)}, u32[]{:S(2)}) copy-start(bf16[1,4,48,4224]{3,2,1,0:T(8,128)(2,1)} %param.8) | copy-start | bytes 4866052
  34.2 6.8 %collective-permute-start.12 = (bf16[1,16,3168]{2,1,0:T(8,128)(2,1)S(1)}, bf16[1,16,3168]{2,1,0:T(8,128)(2,1)S(1)}, u32[]{:S(2)}, u32[]{:S(2)}) collective-permute-start(bf16[1,16,3168]{2,1,0:T(8,128)(2,1)S(1)} %get-tuple-element.52), channel_id=1, source_target_pairs={{0,2},{2,0},{4,6},{6,4},{8,10},{10,8},{12,14},{14,12},{16,18},{18,... | collective-permute-start | bytes 304136 | tf_op jit(solution)/shard_map/ppermute | solution.py:59
  35.8 6.6 %collective-permute-start.13 = (bf16[1,16,3168]{2,1,0:T(8,128)(2,1)S(1)}, bf16[1,16,3168]{2,1,0:T(8,128)(2,1)S(1)}, u32[]{:S(2)}, u32[]{:S(2)}) collective-permute-start(bf16[1,16,3168]{2,1,0:T(8,128)(2,1)S(1)} %get-tuple-element.53), channel_id=1, source_target_pairs={{0,4},{2,6},{4,0},{6,2},{8,12},{10,14},{12,8},{14,10},{16,20},{18,... | collective-permute-start | bytes 304136 | tf_op jit(solution)/shard_map/ppermute | solution.py:59
  36.2 6.2 %collective-permute-start.14 = (bf16[1,16,3168]{2,1,0:T(8,128)(2,1)S(1)}, bf16[1,16,3168]{2,1,0:T(8,128)(2,1)S(1)}, u32[]{:S(2)}, u32[]{:S(2)}) collective-permute-start(bf16[1,16,3168]{2,1,0:T(8,128)(2,1)S(1)} %get-tuple-element.54), channel_id=1, source_target_pairs={{0,6},{2,4},{4,2},{6,0},{8,14},{10,12},{12,10},{14,8},{16,22},{18,... | collective-permute-start | bytes 304136 | tf_op jit(solution)/shard_map/ppermute | solution.py:59
  44.4 3.9 %collective-permute-start.15 = (bf16[192,4224]{1,0:T(8,128)(2,1)}, bf16[192,4224]{1,0:T(8,128)(2,1)}, u32[]{:S(2)}, u32[]{:S(2)}) collective-permute-start(bf16[192,4224]{1,0:T(8,128)(2,1)} %get-tuple-element.56.result_ref), channel_id=1, source_target_pairs={{1,0},{0,1},{3,2},{2,3},{5,4},{4,5},{7,6},{6,7},{9,8},{8,9},{11,10... | collective-permute-start | bytes 4866056 | tf_op jit(solution)/shard_map/ppermute | solution.py:509
  44.4 11.2 %all-to-all-start = ((f32[16,1,264]{2,1,0:T(1,128)}), f32[16,1,264]{2,1,0:T(1,128)S(1)}, u32[]{:S(2)}, u32[]{:S(2)}) async-start(f32[16,1,264]{2,1,0:T(1,128)} %get-tuple-element.55), calls=%async_computation | async-start | bytes 49152 | tf_op jit(solution)/shard_map/all_to_all | solution.py:512
